TPU v7x, 256 devices: a whole 4x4x8 slice. The times are simulated.
256 devices in a mesh: seq: 128 (over y, x, z), head: 2 (over core).
Axes of the slice: x: 4, y: 4, z: 8, core: 2. Of those that a mesh axis runs over, the one named last changes fastest.
Arguments:
- queries: bfloat16 [16384, 1024], P('seq', 'head'), as said below
- keys: bfloat16 [16384, 1024], P('seq', 'head'), as said below
- values: bfloat16 [16384, 1024], P('seq', 'head'), may hold values from -6 to 6
- grad_y: bfloat16 [16384, 2048], P('seq', 'head'), may hold values from -6 to 6
- out_weight: bfloat16 [1024, 2048], P('head'), may hold values from -0.125 to 0.125
- bar_start: int32 [1024], P('seq'), may hold values from 0 to 16382, as said below
- related: int32 [1024, 8], P('seq'), may hold values from -1 to 1022, as said below
- bar_summary_token: int32 [1024], P('seq'), may hold values from 0 to 16383, as said below
Outputs:
- grad_queries: bfloat16 [16384, 1024], P('seq', 'head')
- grad_keys: bfloat16 [16384, 1024], P('seq', 'head')
- values_gradient: bfloat16 [16384, 1024], P('seq', 'head')
Inputs may be any that keep to these rules, and one draw needn't show every extreme that they name: `bar_start`: bar 8 * i starts at token i * 128, so each shard of 128 tokens holds 8 whole bars; starts rise and are even, every bar has 2 tokens or more, and the last bar of each shard has exactly 2. `related`: entry j of bar b's list is b - o_j or -1, with o = 1, 2, 4, 8, 12, 16, 24, 32; it is -1 wherever b - o_j < 0, and entry 0 is b - 1 for every b >= 1. `bar_summary_token`: a token of bar c; bar 0 is summarized by token 0 and the last bar by token 16383. `queries`: real-valued, of order one. `keys`: real-valued, of order one.
All inputs are finite; a program needn't handle non-finite values.
Results may differ from a plain program's by a relative error of at most 0.0083.
Values may be sent and summed in bfloat16 or wider, within the bound.
No kernel may reach another device: no remote copies, remote signals or barrier semaphores. Data moves between devices by JAX's collectives and lax.ppermute only.
A program may use at most 64 MiB of HBM per device.

v0:
```python
import jax
import jax.numpy as jnp
from jax import lax
from jax.sharding import PartitionSpec as P

HD = 128
REACH = 4


def from_behind(block, axis, distance):
    devices = range(lax.axis_size(axis))
    route = [(i - distance, i) for i in devices if i - distance in devices]
    return lax.ppermute(block, axis, route)


def shards(queries, keys, values, grad_y, out_weight, bar_start, related, bar_summary_token):
    tok_rows = queries.shape[0]
    feat_here = queries.shape[1]
    heads_here = feat_here // HD
    bars_here = bar_start.shape[0]
    rank_here = lax.axis_index("seq")
    score_scale = HD ** (-0.5)
    grad_out = lax.dot_general(
        lax.all_gather(grad_y, "head", axis=1, tiled=True),
        out_weight,
        (((1,), (1,)), ((), ())),
        preferred_element_type=jnp.float32,
    ).astype(jnp.bfloat16)
    earlier_starts = [bar_start]
    for offset in range(1, REACH + 1):
        earlier_starts.append(from_behind(bar_start, "seq", offset))
    total_bars = bars_here * lax.axis_size("seq")
    base_row = rank_here * tok_rows
    query_pos = base_row + jnp.arange(tok_rows, dtype=jnp.int32)
    query_local = jnp.sum((bar_start[None, :] <= query_pos[:, None]).astype(jnp.int32), axis=1) - 1
    query_bar = rank_here * bars_here + query_local
    onehot_query = (query_local[:, None] == jnp.arange(bars_here, dtype=jnp.int32)[None, :]).astype(
        jnp.float32
    )
    win_starts = jnp.stack([earlier_starts[REACH - place] for place in range(REACH + 1)], axis=0)
    owners = rank_here - REACH + jnp.arange(REACH + 1, dtype=jnp.int32)
    key_pos = owners[:, None] * tok_rows + jnp.arange(tok_rows, dtype=jnp.int32)[None, :]
    key_local = (
        jnp.sum((win_starts[:, None, :] <= key_pos[:, :, None]).astype(jnp.int32), axis=-1) - 1
    )
    key_bar = jnp.where(owners[:, None] >= 0, owners[:, None] * bars_here + key_local, -2).reshape(
        -1
    )
    key_pos = key_pos.reshape(-1)
    bar_rows = rank_here * bars_here + jnp.arange(bars_here, dtype=jnp.int32)
    rel_window = jnp.any(related[:, :, None] == key_bar[None, None, :], axis=1).astype(jnp.float32)
    fine = (jnp.dot(onehot_query, rel_window) > 0.5) | (query_bar[:, None] == key_bar[None, :]) & (
        key_pos[None, :] <= query_pos[:, None]
    )
    all_bars = jnp.arange(total_bars, dtype=jnp.int32)
    rel_all = jnp.any(related[:, :, None] == all_bars[None, None, :], axis=1)
    coarse_bar = ((all_bars[None, :] < bar_rows[:, None]) & jnp.logical_not(rel_all)).astype(
        jnp.float32
    )
    coarse = jnp.dot(onehot_query, coarse_bar) > 0.5
    allowed = jnp.concatenate([fine, coarse], axis=1)
    own_pair = (keys, values)
    earlier = [own_pair] + [
        from_behind((own_pair[0], own_pair[1]), "seq", offset) for offset in range(1, REACH + 1)
    ]
    slot_rows = bar_summary_token - base_row
    sum_keys, sum_values = (
        lax.all_gather(keys[slot_rows], "seq", axis=0, tiled=True),
        lax.all_gather(values[slot_rows], "seq", axis=0, tiled=True),
    )
    all_keys = jnp.concatenate(
        [earlier[REACH - place][0] for place in range(REACH + 1)] + [sum_keys], axis=0
    )
    all_values = jnp.concatenate(
        [earlier[REACH - place][1] for place in range(REACH + 1)] + [sum_values], axis=0
    )
    query_parts = []
    key_parts = []
    value_parts = []
    for head_index in range(heads_here):
        low_col = head_index * HD
        query_head = queries[:, low_col : low_col + HD]
        key_head = all_keys[:, low_col : low_col + HD]
        value_head = all_values[:, low_col : low_col + HD]
        grad_head = grad_out[:, low_col : low_col + HD]
        scores = score_scale * lax.dot_general(
            query_head, key_head, (((1,), (1,)), ((), ())), preferred_element_type=jnp.float32
        )
        top = jnp.max(jnp.where(allowed, scores, -jnp.inf), axis=1, keepdims=True)
        weights = jnp.where(allowed, jnp.exp(scores - top), 0.0)
        probs = weights / jnp.sum(weights, axis=1, keepdims=True)
        probs_low = probs.astype(jnp.bfloat16)
        attended = jnp.dot(probs_low, value_head, preferred_element_type=jnp.float32)
        delta = jnp.sum(grad_head.astype(jnp.float32) * attended, axis=1, keepdims=True)
        dprobs = lax.dot_general(
            grad_head, value_head, (((1,), (1,)), ((), ())), preferred_element_type=jnp.float32
        )
        dscores = (probs * (dprobs - delta)).astype(jnp.bfloat16)
        query_parts.append(
            score_scale * jnp.dot(dscores, key_head, preferred_element_type=jnp.float32)
        )
        key_parts.append(
            score_scale
            * lax.dot_general(
                dscores, query_head, (((0,), (0,)), ((), ())), preferred_element_type=jnp.float32
            )
        )
        value_parts.append(
            lax.dot_general(
                probs_low, grad_head, (((0,), (0,)), ((), ())), preferred_element_type=jnp.float32
            )
        )
    grad_queries = jnp.concatenate(query_parts, axis=1).astype(jnp.bfloat16)
    key_grads = jnp.concatenate(key_parts, axis=1)
    value_grads = jnp.concatenate(value_parts, axis=1)
    local_window = (REACH + 1) * tok_rows
    key_blocks = key_grads[:local_window].reshape(REACH + 1, tok_rows, feat_here)
    value_blocks = value_grads[:local_window].reshape(REACH + 1, tok_rows, feat_here)
    key_total = key_blocks[REACH]
    value_total = value_blocks[REACH]
    for offset in range(1, REACH + 1):
        arrived = (
            from_behind(key_blocks[REACH - offset].astype(jnp.bfloat16), "seq", -offset).astype(
                jnp.float32
            ),
            from_behind(value_blocks[REACH - offset].astype(jnp.bfloat16), "seq", -offset).astype(
                jnp.float32
            ),
        )
        key_total = key_total + arrived[0]
        value_total = value_total + arrived[1]
    sum_kgrad, sum_vgrad = (
        lax.psum_scatter(key_grads[local_window:], "seq", scatter_dimension=0, tiled=True),
        lax.psum_scatter(value_grads[local_window:], "seq", scatter_dimension=0, tiled=True),
    )
    key_total = key_total.at[slot_rows].add(sum_kgrad)
    value_total = value_total.at[slot_rows].add(sum_vgrad)
    return (grad_queries, key_total.astype(jnp.bfloat16), value_total.astype(jnp.bfloat16))


def solution(mesh):
    in_specs = (
        P("seq", "head"),
        P("seq", "head"),
        P("seq", "head"),
        P("seq", "head"),
        P("head", None),
        P("seq"),
        P("seq", None),
        P("seq"),
    )
    out_specs = (P("seq", "head"), P("seq", "head"), P("seq", "head"))
    return jax.shard_map(shards, mesh=mesh, in_specs=in_specs, out_specs=out_specs, check_vma=False)
```

profile of v0, /device:TPU:2, one launch (start us, length us, event | category | flops | bytes accessed | tf_op | source)
XLA Modules:
  0.0 1640.7 jit_solution(16309192100662354332)
XLA Ops:
  8.0 2.1 gather_fusion
  10.2 5.2 collective-permute-start.2
  15.4 6.8 collective-permute-start.1
  22.2 2.8 collective-permute-start
  25.1 3.5 collective-permute-start.3
  28.6 3.8 collective-permute-start.7
  32.4 2.1 gather_fusion.1
  35.4 0.8 fusion.51
  36.3 2.4 all_gather.10
  39.9 5.5 collective-permute-start.6
  45.4 2.8 collective-permute-start.5
  48.2 4.5 collective-permute-start.9
  52.8 6.4 collective-permute-start.8
  59.8 14.7 collective-permute-done.8
  74.5 8.3 collective-permute-start.10
  83.5 1.9 collective-permute-start.11
  86.6 5.9 collective-permute-start.4
  95.3 3.7 collective-permute-done.4
  102.4 30.2 %all-gather.5.cloned.1.call-done = bf16[1024,512]{1,0:T(8,128)(2,1)} async-done(((bf16[8,512]{1,0:T(8,128)(2,1)}), bf16[1024,512]{1,0:T(8,128)(2,1)}) %all-gather.5.cloned.1.call-update) | async-done | bytes 1048592 | tf_op jit(solution)/shard_map/all_gather | solution.py:68
  132.6 2.3 constant_dynamic-update-slice_fusion
  134.8 1.3 fusion.7
  136.1 1.3 fusion.6
  137.4 1.4 select_reduce_fusion.3
  138.8 1.7 fusion.22
  140.5 0.9 fusion.24
  141.4 2.1 fusion.23
  143.5 94.5 %all-gather.7.cloned.1.call-done = bf16[1024,512]{1,0:T(8,128)(2,1)} async-done(((bf16[8,512]{1,0:T(8,128)(2,1)}), bf16[1024,512]{1,0:T(8,128)(2,1)}) %all-gather.7.cloned.1.call-update) | async-done | bytes 1048592 | tf_op jit(solution)/shard_map/all_gather | solution.py:69
  238.0 2.4 constant_dynamic-update-slice_fusion.6
  240.4 1.4 fusion.18
  241.9 1.4 fusion.19
  243.3 1.4 fusion.20
  244.6 1.4 fusion.17
  246.0 1.3 fusion.11
  247.3 1.4 fusion.8
  248.8 1.5 fusion.9
  250.3 1.3 fusion.10
  253.9 1.7 copy-done.8
  255.6 1.7 slice.163
  257.2 3.0 copy.69
  262.3 0.9 copy-done.2
  264.4 1.8 copy-done.7
  266.2 1.7 slice.169
  267.9 2.9 copy.71
  270.8 1.5 fusion.13
  272.4 1.5 fusion.16
  273.9 1.4 fusion.14
  275.2 1.4 fusion.15
  277.4 2.3 fusion.91
  279.8 4.5 collective-permute-start.12
  284.3 4.8 collective-permute-start.15
  289.1 3.0 collective-permute-start.14
  292.1 1.9 collective-permute-start.13
  294.3 2.5 collective-permute-start.16
  296.8 2.0 collective-permute-start.19
  298.8 12.9 collective-permute-start.18
  311.8 1.9 collective-permute-start.17
  313.7 1.0 fusion.50
  315.0 12.8 collective-permute-done.18
  327.8 4.1 collective-permute-done.17
  331.9 1.1 fusion.47
  333.1 606.1 %reduce-scatter.7.cloned.1.call-done = f32[8,512]{1,0:T(8,128)} async-done(((f32[1024,512]{1,0:T(8,128)}), f32[8,512]{1,0:T(8,128)}) %reduce-scatter.7.cloned.1.call-update) | async-done | bytes 16400 | tf_op jit(solution)/shard_map/reduce_scatter | solution.py:133
  939.1 0.9 scatter_fusion
  940.7 691.8 %reduce-scatter.9.cloned.1.call-done = f32[8,512]{1,0:T(8,128)} async-done(((f32[1024,512]{1,0:T(8,128)}), f32[8,512]{1,0:T(8,128)}) %reduce-scatter.9.cloned.1.call-update) | async-done | bytes 16400 | tf_op jit(solution)/shard_map/reduce_scatter | solution.py:134
  1632.5 0.9 scatter_fusion.1
  (124 shorter events, 19.9 us)
Async XLA Ops:
  7.2 31.5 %copy-start = (bf16[512,2048]{1,0:T(8,128)(2,1)S(1)}, bf16[512,2048]{1,0:T(8,128)(2,1)}, u32[]{:S(2)}) copy-start(bf16[512,2048]{1,0:T(8,128)(2,1)} %param.12) | copy-start | bytes 6291460
  7.2 125.4 %all-gather.5.cloned.1.call-start = ((), (), s32[]{:S(2)}) async-start(), calls=%async_computation.2 | async-start | bytes 1056768 | tf_op jit(solution)/shard_map/all_gather | solution.py:68
  10.2 227.9 %all-gather.7.cloned.1.call-start = ((), (), s32[]{:S(2)}) async-start(), calls=%async_computation.3 | async-start | bytes 1056768 | tf_op jit(solution)/shard_map/all_gather | solution.py:69
  10.2 29.6 %collective-permute-start.2 = (s32[8]{0:T(128)}, s32[8]{0:T(128)S(1)}, u32[]{:S(2)}, u32[]{:S(2)}) collective-permute-start(s32[8]{0:T(128)} %param.13), channel_id=1, source_target_pairs={{0,4},{2,6},{4,8},{6,10},{8,12},{10,14},{12,16},{14,18},{16,20},{1... | collective-permute-start | bytes 104 | tf_op jit(solution)/shard_map/ppermute | solution.py:13
  15.4 30.0 %collective-permute-start.1 = (s32[8]{0:T(128)}, s32[8]{0:T(128)S(1)}, u32[]{:S(2)}, u32[]{:S(2)}) collective-permute-start(s32[8]{0:T(128)} %param.13), channel_id=1, source_target_pairs={{0,6},{2,8},{4,10},{6,12},{8,14},{10,16},{12,18},{14,20},{16,22},{... | collective-permute-start | bytes 104 | tf_op jit(solution)/shard_map/ppermute | solution.py:13
  22.2 26.0 %collective-permute-start = (s32[8]{0:T(128)}, s32[8]{0:T(128)S(1)}, u32[]{:S(2)}, u32[]{:S(2)}) collective-permute-start(s32[8]{0:T(128)} %param.13), channel_id=1, source_target_pairs={{0,8},{2,10},{4,12},{6,14},{8,16},{10,18},{12,20},{14,22},{16,24},... | collective-permute-start | bytes 104 | tf_op jit(solution)/shard_map/ppermute | solution.py:13
  25.1 27.7 %collective-permute-start.3 = (s32[8]{0:T(128)}, s32[8]{0:T(128)S(1)}, u32[]{:S(2)}, u32[]{:S(2)}) collective-permute-start(s32[8]{0:T(128)} %param.13), channel_id=1, source_target_pairs={{0,2},{2,4},{4,6},{6,8},{8,10},{10,12},{12,14},{14,16},{16,18},{18... | collective-permute-start | bytes 104 | tf_op jit(solution)/shard_map/ppermute | solution.py:13
  28.6 72.5 %collective-permute-start.7 = (bf16[128,512]{1,0:T(8,128)(2,1)}, bf16[128,512]{1,0:T(8,128)(2,1)S(1)}, u32[]{:S(2)}, u32[]{:S(2)}) collective-permute-start(bf16[128,512]{1,0:T(8,128)(2,1)} %param.9), channel_id=1, source_target_pairs={{0,2},{2,4},{4,6},{6,8},{8,10},{10,12},{12,14},{14,16},{16,18},{18... | collective-permute-start | bytes 393224 | tf_op jit(solution)/shard_map/ppermute | solution.py:13
  34.5 904.6 %reduce-scatter.7.cloned.1.call-start = ((), (), s32[]{:S(2)}) async-start(), calls=%async_computation.4 | async-start | bytes 2113536 | tf_op jit(solution)/shard_map/reduce_scatter | solution.py:133
  38.7 1.2 copy-start.26
  38.7 9.5 copy-start.25
  38.7 20.5 %copy-start.28 = (s32[8]{0:T(128)S(1)}, s32[8]{0:T(128)}, u32[]{:S(2)}) copy-start(s32[8]{0:T(128)} %param.13) | copy-start | bytes 100
  38.7 20.7 %copy-start.27 = (s32[8,8]{1,0:T(8,128)S(1)}, s32[8,8]{1,0:T(8,128)}, u32[]{:S(2)}) copy-start(s32[8,8]{1,0:T(8,128)} %param.14) | copy-start | bytes 772
  39.9 60.5 %collective-permute-start.6 = (bf16[128,512]{1,0:T(8,128)(2,1)S(1)}, bf16[128,512]{1,0:T(8,128)(2,1)S(1)}, u32[]{:S(2)}, u32[]{:S(2)}) collective-permute-start(bf16[128,512]{1,0:T(8,128)(2,1)S(1)} %copy-done.26), channel_id=1, source_target_pairs={{0,4},{2,6},{4,8},{6,10},{8,12},{10,14},{12,16},{14,18},{16,20},{1... | collective-permute-start | bytes 393224 | tf_op jit(solution)/shard_map/ppermute | solution.py:13
  45.4 54.3 %collective-permute-start.5 = (bf16[128,512]{1,0:T(8,128)(2,1)S(1)}, bf16[128,512]{1,0:T(8,128)(2,1)S(1)}, u32[]{:S(2)}, u32[]{:S(2)}) collective-permute-start(bf16[128,512]{1,0:T(8,128)(2,1)S(1)} %copy-done.26), channel_id=1, source_target_pairs={{0,6},{2,8},{4,10},{6,12},{8,14},{10,16},{12,18},{14,20},{16,22},{... | collective-permute-start | bytes 393224 | tf_op jit(solution)/shard_map/ppermute | solution.py:13
  48.2 35.3 %collective-permute-start.9 = (bf16[128,512]{1,0:T(8,128)(2,1)S(1)}, bf16[128,512]{1,0:T(8,128)(2,1)S(1)}, u32[]{:S(2)}, u32[]{:S(2)}) collective-permute-start(bf16[128,512]{1,0:T(8,128)(2,1)S(1)} %copy-done.25), channel_id=1, source_target_pairs={{0,6},{2,8},{4,10},{6,12},{8,14},{10,16},{12,18},{14,20},{16,22},{... | collective-permute-start | bytes 393224 | tf_op jit(solution)/shard_map/ppermute | solution.py:13
  52.8 21.7 %collective-permute-start.8 = (bf16[128,512]{1,0:T(8,128)(2,1)S(1)}, bf16[128,512]{1,0:T(8,128)(2,1)S(1)}, u32[]{:S(2)}, u32[]{:S(2)}) collective-permute-start(bf16[128,512]{1,0:T(8,128)(2,1)S(1)} %copy-done.25), channel_id=1, source_target_pairs={{0,8},{2,10},{4,12},{6,14},{8,16},{10,18},{12,20},{14,22},{16,24},... | collective-permute-start | bytes 393224 | tf_op jit(solution)/shard_map/ppermute | solution.py:13
  74.5 12.1 collective-permute-start.10
  83.5 10.5 collective-permute-start.11
  86.6 12.4 collective-permute-start.4
  95.3 39.5 %copy-start.23 = (bf16[128,512]{1,0:T(8,128)(2,1)S(1)}, bf16[128,512]{1,0:T(8,128)(2,1)}, u32[]{:S(2)}) copy-start(bf16[128,512]{1,0:T(8,128)(2,1)} %param.8) | copy-start | bytes 393220
  238.0 2.4 copy-start.3
  238.0 3.9 copy-start.1
  240.4 2.8 copy-start.5
  247.3 5.3 copy-start.19
  248.8 3.5 copy-start.20
  248.8 2.8 copy-start.24
  251.6 1.0 copy-start.21
  251.9 1.0 copy-start.15
  252.3 0.9 copy-start.16
  252.6 0.9 copy-start.17
  253.0 0.9 copy-start.18
  253.9 1.7 copy-start.8
  260.3 1372.3 %reduce-scatter.9.cloned.1.call-start = ((), (), s32[]{:S(2)}) async-start(), calls=%async_computation.5 | async-start | bytes 2113536 | tf_op jit(solution)/shard_map/reduce_scatter | solution.py:134
  260.5 1.2 copy-start.6
  260.5 1.5 copy-start.4
  261.6 1.9 copy-start.9
  261.6 1.5 copy-start.2
  263.2 0.9 copy-start.11
  263.5 0.9 copy-start.13
  264.4 1.8 copy-start.7
  270.8 3.1 copy-start.22
  277.4 16.6 %copy-start.10 = (f32[1664,128]{0,1:T(8,128)S(1)}, f32[1664,128]{0,1:T(8,128)}, u32[]{:S(2)}) copy-start(f32[1664,128]{0,1:T(8,128)} %copy-done.9) | copy-start | bytes 2555908
  277.4 16.6 %copy-start.12 = (f32[1664,128]{0,1:T(8,128)S(1)}, f32[1664,128]{0,1:T(8,128)}, u32[]{:S(2)}) copy-start(f32[1664,128]{0,1:T(8,128)} %copy-done.11) | copy-start | bytes 2555908
  277.4 16.6 %copy-start.14 = (f32[1664,128]{0,1:T(8,128)S(1)}, f32[1664,128]{0,1:T(8,128)}, u32[]{:S(2)}) copy-start(f32[1664,128]{0,1:T(8,128)} %copy-done.13) | copy-start | bytes 2555908
  279.8 17.1 %collective-permute-start.12 = (bf16[128,512]{0,1:T(8,128)(2,1)S(1)}, bf16[128,512]{0,1:T(8,128)(2,1)S(1)}, u32[]{:S(2)}, u32[]{:S(2)}) collective-permute-start(bf16[128,512]{0,1:T(8,128)(2,1)S(1)} %get-tuple-element.26), channel_id=1, source_target_pairs={{2,0},{4,2},{6,4},{8,6},{10,8},{12,10},{14,12},{16,14},{18,16},{20... | collective-permute-start | bytes 393224 | tf_op jit(solution)/shard_map/ppermute | solution.py:13
  284.3 14.5 collective-permute-start.15
  289.1 22.6 %collective-permute-start.14 = (bf16[128,512]{0,1:T(8,128)(2,1)S(1)}, bf16[128,512]{0,1:T(8,128)(2,1)S(1)}, u32[]{:S(2)}, u32[]{:S(2)}) collective-permute-start(bf16[128,512]{0,1:T(8,128)(2,1)S(1)} %get-tuple-element.28), channel_id=1, source_target_pairs={{6,0},{8,2},{10,4},{12,6},{14,8},{16,10},{18,12},{20,14},{22,16},{... | collective-permute-start | bytes 393224 | tf_op jit(solution)/shard_map/ppermute | solution.py:13
  292.1 21.6 %collective-permute-start.13 = (bf16[128,512]{0,1:T(8,128)(2,1)S(1)}, bf16[128,512]{0,1:T(8,128)(2,1)S(1)}, u32[]{:S(2)}, u32[]{:S(2)}) collective-permute-start(bf16[128,512]{0,1:T(8,128)(2,1)S(1)} %get-tuple-element.29), channel_id=1, source_target_pairs={{4,0},{6,2},{8,4},{10,6},{12,8},{14,10},{16,12},{18,14},{20,16},{2... | collective-permute-start | bytes 393224 | tf_op jit(solution)/shard_map/ppermute | solution.py:13
  294.3 20.7 %collective-permute-start.16 = (bf16[128,512]{0,1:T(8,128)(2,1)S(1)}, bf16[128,512]{0,1:T(8,128)(2,1)S(1)}, u32[]{:S(2)}, u32[]{:S(2)}) collective-permute-start(bf16[128,512]{0,1:T(8,128)(2,1)S(1)} %get-tuple-element.22), channel_id=1, source_target_pairs={{2,0},{4,2},{6,4},{8,6},{10,8},{12,10},{14,12},{16,14},{18,16},{20... | collective-permute-start | bytes 393224 | tf_op jit(solution)/shard_map/ppermute | solution.py:13
  296.8 18.2 %collective-permute-start.19 = (bf16[128,512]{0,1:T(8,128)(2,1)S(1)}, bf16[128,512]{0,1:T(8,128)(2,1)S(1)}, u32[]{:S(2)}, u32[]{:S(2)}) collective-permute-start(bf16[128,512]{0,1:T(8,128)(2,1)S(1)} %get-tuple-element.23), channel_id=1, source_target_pairs={{8,0},{10,2},{12,4},{14,6},{16,8},{18,10},{20,12},{22,14},{24,16},... | collective-permute-start | bytes 393224 | tf_op jit(solution)/shard_map/ppermute | solution.py:13
  298.8 29.0 %collective-permute-start.18 = (bf16[128,512]{0,1:T(8,128)(2,1)S(1)}, bf16[128,512]{0,1:T(8,128)(2,1)S(1)}, u32[]{:S(2)}, u32[]{:S(2)}) collective-permute-start(bf16[128,512]{0,1:T(8,128)(2,1)S(1)} %get-tuple-element.24), channel_id=1, source_target_pairs={{6,0},{8,2},{10,4},{12,6},{14,8},{16,10},{18,12},{20,14},{22,16},{... | collective-permute-start | bytes 393224 | tf_op jit(solution)/shard_map/ppermute | solution.py:13
  311.8 20.1 %collective-permute-start.17 = (bf16[128,512]{0,1:T(8,128)(2,1)S(1)}, bf16[128,512]{0,1:T(8,128)(2,1)}, u32[]{:S(2)}, u32[]{:S(2)}) collective-permute-start(bf16[128,512]{0,1:T(8,128)(2,1)S(1)} %get-tuple-element.25), channel_id=1, source_target_pairs={{4,0},{6,2},{8,4},{10,6},{12,8},{14,10},{16,12},{18,14},{20,16},{2... | collective-permute-start | bytes 393224 | tf_op jit(solution)/shard_map/ppermute | solution.py:13
Sparse Core Ops, SparseCore 0:
  12.0 120.5 all-gather.4
  136.6 101.4 all-gather.6
  260.4 678.6 reduce-scatter.6
  941.6 690.8 reduce-scatter.8
where the time goes:
time: 1660 us; the launch traced here: 1640 us
  waiting for transfers between devices  1460 us (88%)
  starting transfers between devices  91.4 us (6%)
  local copies, waits for them, and re-layouts  32.6 us (2%)
  matrix products  26.4 us (2%)
    reduce_scatter x1, waiting for transfers between devices, shards(): lax.psum_scatter(value_grads[local_window:], 'seq', scatter_dimension=0,...  692 us
    reduce_scatter x1, waiting for transfers between devices, shards(): lax.psum_scatter(key_grads[local_window:], 'seq', scatter_dimension=0, ti...  606 us
    all_gather x1, waiting for transfers between devices, shards(): lax.all_gather(values[slot_rows], 'seq', axis=0, tiled=True)  94.5 us
    ppermute x20, starting transfers between devices, from_behind(): return lax.ppermute(block, axis, route)  91.1 us
    ppermute x20, waiting for transfers between devices, from_behind(): return lax.ppermute(block, axis, route)  36.8 us
  transfers between devices with their start and end apart: 24, of which 11 were waited for; matrix products, arithmetic and copies ran while one was open for 3% of the time, Pallas kernels for 0%

commit v1 on v0

v1 whole, which is shorter than its diff:
```python
import math

import jax
import jax.numpy as jnp
from jax import lax
from jax.experimental import pallas as pl
from jax.experimental.pallas import tpu as pltpu
from jax.sharding import PartitionSpec as P

HD = 128
REACH = 4
TOK = 128
BARS_HERE = 8
HEADS_HERE = 4
FEAT = HD * HEADS_HERE
META = 16
NZ = 8
NXY = 16
N_SEQ = NZ * NXY
WINDOW = (REACH + 1) * TOK
BARS = N_SEQ * BARS_HERE
KEYS_ALL = WINDOW + BARS
SCALE = HD ** (-0.5)
EXP_SCALE = SCALE * math.log2(math.e)

Z_GROUPS = [[j * NZ + z for z in range(NZ)] for j in range(NXY)]
XY_GROUPS = [[j * NZ + z for j in range(NXY)] for z in range(NZ)]

VMEM_LIMIT = 50 * 2**20
SMEM = pltpu.SMEM
VMEM = pltpu.VMEM


def shift(block, distance):
    route = [(i, i + distance) for i in range(N_SEQ) if 0 <= i + distance < N_SEQ]
    return lax.ppermute(block, "seq", route)


def local_bar(starts, positions):
    count = jnp.zeros_like(positions)
    for b in range(1, BARS_HERE):
        count = count + (positions >= starts[b]).astype(jnp.int32)
    return count


def pack_kernel(starts, slots, keys, values, payload, sums):
    base = starts[0]
    payload[0:TOK, :] = keys[...]
    payload[TOK : 2 * TOK, :] = values[...]
    lane = lax.broadcasted_iota(jnp.int32, (META, TOK), 1)
    row = lax.broadcasted_iota(jnp.int32, (META, TOK), 0)
    payload[2 * TOK :, :] = jnp.zeros((META, FEAT), jnp.bfloat16)
    payload[2 * TOK :, 0:TOK] = (
        local_bar(starts, lane + base).astype(jnp.float32).astype(jnp.bfloat16)
    )
    slot = jnp.full((META, TOK), -1, jnp.int32)
    for b in range(BARS_HERE):
        slot = jnp.where(row == b, slots[b] - base, slot)
    pick = (lane == slot).astype(jnp.float32).astype(jnp.bfloat16)
    key_rows = jnp.dot(pick, keys[...], preferred_element_type=jnp.float32)
    value_rows = jnp.dot(pick, values[...], preferred_element_type=jnp.float32)
    for h in range(HEADS_HERE):
        cols = slice(h * HD, (h + 1) * HD)
        sums[:, 2 * h * HD : (2 * h + 1) * HD] = key_rows[0:BARS_HERE, cols].astype(jnp.bfloat16)
        sums[:, (2 * h + 1) * HD : (2 * h + 2) * HD] = value_rows[0:BARS_HERE, cols].astype(
            jnp.bfloat16
        )


def attend_kernel(
    starts, related, queries, grad_out, own, back1, back2, back3, back4, sums,
    grad_queries, own_grad, halo_grad, sum_grad, bias,
):
    blocks = [back4, back3, back2, back1, own]
    nt = (((1,), (1,)), ((), ()))

    @pl.when(pl.program_id(0) == 0)
    def _():
        base = starts[0]
        rank = lax.shift_right_logical(base, 7)
        lane = lax.broadcasted_iota(jnp.int32, (8, TOK), 1)
        token_local = local_bar(starts, lane + base)
        token_bar = rank * BARS_HERE + token_local
        rel = []
        for j in range(8):
            entry = jnp.full((8, TOK), -1, jnp.int32)
            for b in range(BARS_HERE):
                entry = jnp.where(token_local == b, related[b, j], entry)
            rel.append(entry[0:1])
        token_bar = token_bar[0:1]
        for place in range(REACH + 1):
            offset = REACH - place
            meta = blocks[place][2 * TOK : 2 * TOK + META, :].astype(jnp.float32)
            key_local = jnp.transpose(jnp.broadcast_to(meta[0:1], (TOK, TOK))).astype(jnp.int32)
            owner = rank - offset
            key_bar = jnp.where(owner >= 0, owner * BARS_HERE + key_local, -2)
            seen = key_bar == rel[0]
            for j in range(1, 8):
                seen = seen | (key_bar == rel[j])
            if offset == 0:
                key_row = lax.broadcasted_iota(jnp.int32, (TOK, TOK), 0)
                token_col = lax.broadcasted_iota(jnp.int32, (TOK, TOK), 1)
                seen = seen | ((key_bar == token_bar) & (key_row <= token_col))
            bias[place * TOK : (place + 1) * TOK, :] = jnp.where(seen, 0.0, -jnp.inf)
        for part in range(BARS // TOK):
            bar = lax.broadcasted_iota(jnp.int32, (TOK, TOK), 0) + part * TOK
            hidden = bar >= token_bar
            for j in range(8):
                hidden = hidden | (bar == rel[j])
            low = WINDOW + part * TOK
            bias[low : low + TOK, :] = jnp.where(hidden, -jnp.inf, 0.0)

    query = queries[...]
    grad = grad_out[...]
    key_blocks = [block[0:TOK, :] for block in blocks] + [sums[:, 0:HD]]
    value_blocks = [block[TOK : 2 * TOK, :] for block in blocks] + [sums[:, HD : 2 * HD]]
    keys = jnp.concatenate(key_blocks, axis=0)
    values = jnp.concatenate(value_blocks, axis=0)
    scores = lax.dot_general(keys, query, nt, preferred_element_type=jnp.float32) + bias[...]
    top = jnp.max(scores, axis=0, keepdims=True)
    weights = jnp.exp2((scores - top) * EXP_SCALE)
    probs = weights * (1.0 / jnp.sum(weights, axis=0, keepdims=True))
    probs_low = probs.astype(jnp.bfloat16)
    dprobs = lax.dot_general(values, grad, nt, preferred_element_type=jnp.float32)
    delta = jnp.sum(probs_low.astype(jnp.float32) * dprobs, axis=0, keepdims=True)
    dscores = (probs * (dprobs - delta)).astype(jnp.bfloat16)
    grad_queries[...] = (
        SCALE
        * lax.dot_general(
            dscores, keys, (((0,), (0,)), ((), ())), preferred_element_type=jnp.float32
        )
    ).astype(jnp.bfloat16)
    dkeys = SCALE * jnp.dot(dscores, query, preferred_element_type=jnp.float32)
    dvalues = jnp.dot(probs_low, grad, preferred_element_type=jnp.float32)
    for place in range(REACH):
        rows = slice(place * TOK, (place + 1) * TOK)
        halo_grad[place, 0:TOK, :] = dkeys[rows].astype(jnp.bfloat16)
        halo_grad[place, TOK : 2 * TOK, :] = dvalues[rows].astype(jnp.bfloat16)
    own_grad[0:TOK, :] = dkeys[REACH * TOK : WINDOW]
    own_grad[TOK : 2 * TOK, :] = dvalues[REACH * TOK : WINDOW]
    sum_grad[:, 0:HD] = dkeys[WINDOW:].astype(jnp.bfloat16)
    sum_grad[:, HD : 2 * HD] = dvalues[WINDOW:].astype(jnp.bfloat16)


def finish_kernel(starts, slots, own_grad, arrived, parts, grad_keys, grad_values):
    base = starts[0]
    total = parts[0].astype(jnp.float32)
    for i in range(1, NZ):
        total = total + parts[i].astype(jnp.float32)
    row = lax.broadcasted_iota(jnp.int32, (TOK, HD), 0)
    for h in range(HEADS_HERE):
        cols = slice(h * HD, (h + 1) * HD)
        for kind, out in ((0, grad_keys), (1, grad_values)):
            rows = slice(kind * TOK, (kind + 1) * TOK)
            low = (2 * h + kind) * HD
            grad = own_grad[rows, cols] + arrived[rows, cols].astype(jnp.float32)
            for b in range(BARS_HERE):
                grad = grad + jnp.where(
                    row == slots[b] - base, total[b : b + 1, low : low + HD], 0.0
                )
            out[:, cols] = grad.astype(jnp.bfloat16)


def whole(space):
    return pl.BlockSpec(memory_space=space)


def shards(queries, keys, values, grad_y, out_weight, bar_start, related, bar_summary_token):
    bf16 = jnp.bfloat16
    payload, sums = pl.pallas_call(
        pack_kernel,
        out_shape=(
            jax.ShapeDtypeStruct((2 * TOK + META, FEAT), bf16),
            jax.ShapeDtypeStruct((BARS_HERE, 2 * FEAT), bf16),
        ),
        in_specs=[whole(SMEM), whole(SMEM), whole(VMEM), whole(VMEM)],
        out_specs=(whole(VMEM), whole(VMEM)),
    )(bar_start, bar_summary_token, keys, values)

    grad_out = lax.dot_general(
        lax.all_gather(grad_y, "head", axis=1, tiled=True),
        out_weight,
        (((1,), (1,)), ((), ())),
        preferred_element_type=jnp.float32,
    ).astype(bf16)

    back = [payload]
    for _ in range(REACH):
        back.append(shift(back[-1], 1))

    row_sums = lax.all_to_all(
        jnp.broadcast_to(sums[None], (NZ,) + sums.shape), "seq", 0, 0, axis_index_groups=Z_GROUPS
    )
    row_sums = row_sums.reshape(NZ * BARS_HERE, 2 * FEAT)
    all_sums = lax.all_to_all(
        jnp.broadcast_to(row_sums[None], (NXY,) + row_sums.shape),
        "seq",
        0,
        0,
        axis_index_groups=XY_GROUPS,
    ).reshape(BARS, 2 * FEAT)

    window = pl.BlockSpec((2 * TOK + META, HD), lambda h: (0, h))
    heads = pl.BlockSpec((TOK, HD), lambda h: (0, h))
    pairs = pl.BlockSpec((BARS, 2 * HD), lambda h: (0, h))
    grad_queries, own_grad, halo_grad, sum_grad = pl.pallas_call(
        attend_kernel,
        grid=(HEADS_HERE,),
        out_shape=(
            jax.ShapeDtypeStruct((TOK, FEAT), bf16),
            jax.ShapeDtypeStruct((2 * TOK, FEAT), jnp.float32),
            jax.ShapeDtypeStruct((REACH, 2 * TOK, FEAT), bf16),
            jax.ShapeDtypeStruct((BARS, 2 * FEAT), bf16),
        ),
        in_specs=[whole(SMEM), whole(SMEM), heads, heads] + [window] * 5 + [pairs],
        out_specs=(
            heads,
            pl.BlockSpec((2 * TOK, HD), lambda h: (0, h)),
            pl.BlockSpec((REACH, 2 * TOK, HD), lambda h: (0, 0, h)),
            pairs,
        ),
        scratch_shapes=[pltpu.VMEM((KEYS_ALL, TOK), jnp.float32)],
        compiler_params=pltpu.CompilerParams(vmem_limit_bytes=VMEM_LIMIT),
    )(bar_start, related, queries, grad_out, *back, all_sums)

    moving = shift(halo_grad[0], -1)
    for place in range(1, REACH):
        moving = (moving.astype(jnp.float32) + halo_grad[place].astype(jnp.float32)).astype(bf16)
        moving = shift(moving, -1)

    parts = lax.all_to_all(
        sum_grad.reshape(NXY, NZ * BARS_HERE, 2 * FEAT),
        "seq",
        0,
        0,
        axis_index_groups=XY_GROUPS,
    )
    row_grad = jnp.sum(parts.astype(jnp.float32), axis=0).astype(bf16)
    parts = lax.all_to_all(
        row_grad.reshape(NZ, BARS_HERE, 2 * FEAT), "seq", 0, 0, axis_index_groups=Z_GROUPS
    )

    grad_keys, grad_values = pl.pallas_call(
        finish_kernel,
        out_shape=(
            jax.ShapeDtypeStruct((TOK, FEAT), bf16),
            jax.ShapeDtypeStruct((TOK, FEAT), bf16),
        ),
        in_specs=[whole(SMEM), whole(SMEM), whole(VMEM), whole(VMEM), whole(VMEM)],
        out_specs=(whole(VMEM), whole(VMEM)),
    )(bar_start, bar_summary_token, own_grad, moving, parts)
    return grad_queries, grad_keys, grad_values


def solution(mesh):
    in_specs = (
        P("seq", "head"),
        P("seq", "head"),
        P("seq", "head"),
        P("seq", "head"),
        P("head", None),
        P("seq"),
        P("seq", None),
        P("seq"),
    )
    out_specs = (P("seq", "head"), P("seq", "head"), P("seq", "head"))
    return jax.shard_map(shards, mesh=mesh, in_specs=in_specs, out_specs=out_specs, check_vma=False)
```

time: 1660 us -> 168 us (0.10)
  waiting for transfers between devices: 1460 us -> 60.4 us
  starting transfers between devices: 91.4 us -> 56.1 us
  matrix products: 26.4 us -> 0.83 us
  local copies, waits for them, and re-layouts: 32.6 us -> 10.6 us
  blocking collectives: 2.39 us -> 19.8 us
    reduce_scatter x2 -> x0, waiting for transfers between devices: 1300 us -> none  [the longest x1 692 us: shards(): lax.psum_scatter(value_grads[local_window:], 'seq', scatter_dimension=0,...]
    all_gather x2 -> x0, waiting for transfers between devices: 125 us -> none  [the longest x1 94.5 us: shards(): lax.all_gather(values[slot_rows], 'seq', axis=0, tiled=True)]
    ppermute x20 -> x8, starting transfers between devices: 91.1 us -> 29.3 us  [shift(): return lax.ppermute(block, 'seq', route)]
    all_to_all x0 -> x3, starting transfers between devices: none -> 26.8 us  [the longest x1 15.8 us: shards(): lax.all_to_all(sum_grad.reshape(NXY, NZ * BARS_HERE, 2 * FEAT), 'seq', 0,...]
    dot_general x26 -> x0, matrix products: 25.5 us -> none  [the longest x4 5.75 us: shards(): jnp.dot(dscores, key_head, preferred_element_type=jnp.float32)]
    all_to_all x0 -> x1, blocking collectives: none -> 17.4 us  [shards(): lax.all_to_all(jnp.broadcast_to(sums[None], (NZ,) + sums.shape), 'seq', 0...]
    ppermute x20 -> x8, waiting for transfers between devices: 36.8 us -> 49.3 us  [shift(): return lax.ppermute(block, 'seq', route)]
  transfers between devices with their start and end apart: 24 -> 11, of which waited for: 11 -> 9; matrix products, arithmetic and copies ran while one was open for 3% -> 2% of each run, Pallas kernels for 0% -> 0%
where the time goes in v1:
time: 168 us; the launch traced here: 165 us
  waiting for transfers between devices  60.4 us (36%)
  starting transfers between devices  56.1 us (33%)
  blocking collectives  19.8 us (12%)
  Pallas kernels  13.6 us (8%)
  local copies, waits for them, and re-layouts  10.6 us (6%)
  other arithmetic  2.87 us (2%)
    ppermute x8, waiting for transfers between devices, shift(): return lax.ppermute(block, 'seq', route)  49.3 us
    ppermute x8, starting transfers between devices, shift(): return lax.ppermute(block, 'seq', route)  29.3 us
    all_to_all x1, blocking collectives, shards(): lax.all_to_all(jnp.broadcast_to(sums[None], (NZ,) + sums.shape), 'seq', 0...  17.4 us
    all_to_all x1, starting transfers between devices, shards(): lax.all_to_all(sum_grad.reshape(NXY, NZ * BARS_HERE, 2 * FEAT), 'seq', 0,...  15.8 us
    pallas_call x1, Pallas kernels, shards(): pl.pallas_call(attend_kernel, grid=(HEADS_HERE,), out_shape=(jax.ShapeDty...  9.37 us
    all_to_all x1, waiting for transfers between devices, shards(): lax.all_to_all(row_grad.reshape(NZ, BARS_HERE, 2 * FEAT), 'seq', 0, 0, ax...  8.98 us
    unnamed x32, local copies, waits for them, and re-layouts  8.3 us
    all_to_all x1, starting transfers between devices, shards(): lax.all_to_all(jnp.broadcast_to(row_sums[None], (NXY,) + row_sums.shape),...  7.61 us
  transfers between devices with their start and end apart: 11, of which 9 were waited for; matrix products, arithmetic and copies ran while one was open for 2% of the time, Pallas kernels for 0%

profile of v1, /device:TPU:2, one launch (start us, length us, event | category | flops | bytes accessed | tf_op | source)
XLA Modules:
  0.0 165.0 jit_solution(2301046493969921067)
XLA Ops:
  0.6 0.0 copy-start
  0.6 1.9 %shard_map.103 = (bf16[272,512]{1,0:T(8,128)(2,1)}, bf16[8,1024]{1,0:T(8,128)(2,1)}) custom-call(s32[8]{0:T(128)} %starts.5, s32[8]{0:T(128)} %slots.3, bf16[128,512]{1,0:T(8,128)(2,1)} %keys.1, bf16[128,512]{1,0:T(8,128)(2,1)} %values.1), custom_call_target="tpu_custom_call" | custom-call | tf_op jit(solution)/shard_map/pallas_call | solution.py:170
  2.5 0.7 broadcast_in_dim.6
  3.3 17.4 %all_to_all.20 = bf16[8,8,1024]{2,1,0:T(8,128)(2,1)S(1)} all-to-all(bf16[8,8,1024]{2,1,0:T(8,128)(2,1)S(1)} %broadcast_in_dim.6), channel_id=1, replica_groups={{0,2,4,6,8,10,12,14},{16,18,20,22,24,26,28,30},{32,34,36,38,40,42,44,46..., dimensions={0} | all-to-all | bytes 262144 | tf_op jit(solution)/shard_map/all_to_all | solution.py:191
  20.6 1.6 broadcast_in_dim.15
  22.2 0.0 copy-start.2
  22.2 7.6 %all-to-all-start.1 = ((bf16[16,64,1024]{2,1,0:T(8,128)(2,1)}), bf16[16,64,1024]{2,1,0:T(8,128)(2,1)}, u32[]{:S(2)}, u32[]{:S(2)}) async-start(bf16[16,64,1024]{2,1,0:T(8,128)(2,1)} %broadcast_in_dim.15), calls=%async_computation.1 | async-start | bytes 4194304 | tf_op jit(solution)/shard_map/all_to_all | solution.py:195
  29.8 0.0 copy-done.2
  29.8 2.3 %collective-permute-start = (bf16[272,512]{1,0:T(8,128)(2,1)S(1)}, bf16[272,512]{1,0:T(8,128)(2,1)S(1)}, u32[]{:S(2)}, u32[]{:S(2)}) collective-permute-start(bf16[272,512]{1,0:T(8,128)(2,1)S(1)} %copy-done.2), channel_id=1, source_target_pairs={{0,2},{2,4},{4,6},{6,8},{8,10},{10,12},{12,14},{14,16},{16,18},{18... | collective-permute-start | bytes 835592 | tf_op jit(solution)/shard_map/ppermute | solution.py:36
  32.1 8.3 %collective-permute-done.back1 = bf16[272,512]{1,0:T(8,128)(2,1)S(1)} collective-permute-done((bf16[272,512]{1,0:T(8,128)(2,1)S(1)}, bf16[272,512]{1,0:T(8,128)(2,1)S(1)}, u32[]{:S(2)}, u32[]{:S(2)}) %collective-permute-start) | collective-permute-done | bytes 278560 | tf_op jit(solution)/shard_map/ppermute | solution.py:36
  40.3 0.0 copy-start.3
  40.3 1.9 %collective-permute-start.1 = (bf16[272,512]{1,0:T(8,128)(2,1)S(1)}, bf16[272,512]{1,0:T(8,128)(2,1)S(1)}, u32[]{:S(2)}, u32[]{:S(2)}) collective-permute-start(bf16[272,512]{1,0:T(8,128)(2,1)S(1)} %collective-permute-done.back1), channel_id=1, source_target_pairs={{0,2},{2,4},{4,6},{6,8},{8,10},{10,12},{12,14},{14,16},{16,18},{18... | collective-permute-start | bytes 835592 | tf_op jit(solution)/shard_map/ppermute | solution.py:36
  42.3 8.7 %collective-permute-done.1.back2 = bf16[272,512]{1,0:T(8,128)(2,1)S(1)} collective-permute-done((bf16[272,512]{1,0:T(8,128)(2,1)S(1)}, bf16[272,512]{1,0:T(8,128)(2,1)S(1)}, u32[]{:S(2)}, u32[]{:S(2)}) %collective-permute-start.1) | collective-permute-done | bytes 278560 | tf_op jit(solution)/shard_map/ppermute | solution.py:36
  51.0 0.0 copy-start.5
  51.0 1.9 %collective-permute-start.2 = (bf16[272,512]{1,0:T(8,128)(2,1)S(1)}, bf16[272,512]{1,0:T(8,128)(2,1)S(1)}, u32[]{:S(2)}, u32[]{:S(2)}) collective-permute-start(bf16[272,512]{1,0:T(8,128)(2,1)S(1)} %collective-permute-done.1.back2), channel_id=1, source_target_pairs={{0,2},{2,4},{4,6},{6,8},{8,10},{10,12},{12,14},{14,16},{16,18},{18... | collective-permute-start | bytes 835592 | tf_op jit(solution)/shard_map/ppermute | solution.py:36
  52.9 2.4 %all_gather.3 = bf16[128,2048]{1,0:T(8,128)(2,1)S(1)} all-gather(bf16[128,1024]{1,0:T(8,128)(2,1)} %param.11), channel_id=1, replica_groups=mesh['seq'=128,'head'=2] {'head'}, dimensions={1}, use_global_device_ids=true | all-gather | bytes 786432 | tf_op jit(solution)/shard_map/all_gather | solution.py:181
  55.3 6.3 %collective-permute-done.2.back3 = bf16[272,512]{1,0:T(8,128)(2,1)S(1)} collective-permute-done((bf16[272,512]{1,0:T(8,128)(2,1)S(1)}, bf16[272,512]{1,0:T(8,128)(2,1)S(1)}, u32[]{:S(2)}, u32[]{:S(2)}) %collective-permute-start.2) | collective-permute-done | bytes 278560 | tf_op jit(solution)/shard_map/ppermute | solution.py:36
  61.6 0.0 copy-start.7
  61.6 1.9 %collective-permute-start.3 = (bf16[272,512]{1,0:T(8,128)(2,1)S(1)}, bf16[272,512]{1,0:T(8,128)(2,1)S(1)}, u32[]{:S(2)}, u32[]{:S(2)}) collective-permute-start(bf16[272,512]{1,0:T(8,128)(2,1)S(1)} %collective-permute-done.2.back3), channel_id=1, source_target_pairs={{0,2},{2,4},{4,6},{6,8},{8,10},{10,12},{12,14},{14,16},{16,18},{18... | collective-permute-start | bytes 835592 | tf_op jit(solution)/shard_map/ppermute | solution.py:36
  63.6 0.0 copy-done
  63.6 0.8 convolution_convert_fusion.grad_out
  64.4 7.9 %collective-permute-done.3.back4 = bf16[272,512]{1,0:T(8,128)(2,1)S(1)} collective-permute-done((bf16[272,512]{1,0:T(8,128)(2,1)S(1)}, bf16[272,512]{1,0:T(8,128)(2,1)S(1)}, u32[]{:S(2)}, u32[]{:S(2)}) %collective-permute-start.3) | collective-permute-done | bytes 278560 | tf_op jit(solution)/shard_map/ppermute | solution.py:36
  72.3 0.0 copy-start.9
  72.3 0.7 copy-done.9
  73.0 2.1 %all-to-all-done.1 = bf16[16,64,1024]{2,1,0:T(8,128)(2,1)} async-done(((bf16[16,64,1024]{2,1,0:T(8,128)(2,1)}), bf16[16,64,1024]{2,1,0:T(8,128)(2,1)}, u32[]{:S(2)}, u32[]{:S(2)}) %all-to-all-start.1) | async-done | bytes 2097184 | tf_op jit(solution)/shard_map/all_to_all | solution.py:195
  75.2 0.0 copy-done.3
  75.2 0.0 copy-done.5
  75.2 0.0 copy-done.7
  75.2 0.0 copy-start.4
  75.2 0.9 copy-done.4
  76.1 0.0 copy-start.6
  76.1 1.0 copy-done.6
  77.1 0.0 copy-start.8
  77.1 1.0 copy-done.8
  78.0 0.0 copy-start.10
  78.0 1.0 copy-done.10
  79.0 0.0 copy-start.11
  79.0 0.9 copy-done.11
  79.9 0.0 copy-start.12
  79.9 0.7 copy-done.12
  80.6 0.0 copy-start.13
  80.6 0.7 copy-done.13
  81.3 9.4 %shard_map.104 = (bf16[128,512]{1,0:T(8,128)(2,1)}, f32[256,512]{1,0:T(8,128)S(1)}, bf16[4,256,512]{2,1,0:T(8,128)(2,1)S(1)}, bf16[1024,1024]{1,0:T(8,128)(2,1)}) custom-call(s32[8]{0:T(128)S(1)} %copy-done.12, s32[8,8]{1,0:T(8,128)S(1)} %copy-done.13, bf16[128,512]{1,0:T(8,128)(2,1)S(1)} %copy-done.11, ...), custom_call_target="tpu_custom_call" | custom-call | tf_op jit(solution)/shard_map/pallas_call | solution.py:206
  90.6 0.8 copy-done.1
  91.4 15.8 %all-to-all-start.2 = ((bf16[16,64,1024]{2,1,0:T(8,128)(2,1)}), bf16[16,64,1024]{2,1,0:T(8,128)(2,1)}, u32[]{:S(2)}, u32[]{:S(2)}) async-start(bf16[16,64,1024]{2,1,0:T(8,128)(2,1)} %bitcast.17), calls=%async_computation.2 | async-start | bytes 4194304 | tf_op jit(solution)/shard_map/all_to_all | solution.py:231
  107.3 1.9 %collective-permute-start.4 = (bf16[256,512]{1,0:T(8,128)(2,1)S(1)}, bf16[256,512]{1,0:T(8,128)(2,1)S(1)}, u32[]{:S(2)}, u32[]{:S(2)}) collective-permute-start(bf16[256,512]{1,0:T(8,128)(2,1)S(1)} %slice_bitcast_fusion), channel_id=1, source_target_pairs={{2,0},{4,2},{6,4},{8,6},{10,8},{12,10},{14,12},{16,14},{18,16},{20... | collective-permute-start | bytes 786440 | tf_op jit(solution)/shard_map/ppermute | solution.py:36
  109.2 6.8 %collective-permute-done.4 = bf16[256,512]{1,0:T(8,128)(2,1)S(1)} collective-permute-done((bf16[256,512]{1,0:T(8,128)(2,1)S(1)}, bf16[256,512]{1,0:T(8,128)(2,1)S(1)}, u32[]{:S(2)}, u32[]{:S(2)}) %collective-permute-start.4) | collective-permute-done | bytes 262176 | tf_op jit(solution)/shard_map/ppermute | solution.py:36
  116.0 0.1 fusion.2
  116.1 6.3 %collective-permute-start.5 = (bf16[256,512]{1,0:T(8,128)(2,1)S(1)}, bf16[256,512]{1,0:T(8,128)(2,1)S(1)}, u32[]{:S(2)}, u32[]{:S(2)}) collective-permute-start(bf16[256,512]{1,0:T(8,128)(2,1)S(1)} %fusion.2), channel_id=1, source_target_pairs={{2,0},{4,2},{6,4},{8,6},{10,8},{12,10},{14,12},{16,14},{18,16},{20... | collective-permute-start | bytes 786440 | tf_op jit(solution)/shard_map/ppermute | solution.py:36
  122.4 6.1 %collective-permute-done.5 = bf16[256,512]{1,0:T(8,128)(2,1)S(1)} collective-permute-done((bf16[256,512]{1,0:T(8,128)(2,1)S(1)}, bf16[256,512]{1,0:T(8,128)(2,1)S(1)}, u32[]{:S(2)}, u32[]{:S(2)}) %collective-permute-start.5) | collective-permute-done | bytes 262176 | tf_op jit(solution)/shard_map/ppermute | solution.py:36
  128.5 0.1 fusion.1
  128.6 6.6 %collective-permute-start.6 = (bf16[256,512]{1,0:T(8,128)(2,1)S(1)}, bf16[256,512]{1,0:T(8,128)(2,1)S(1)}, u32[]{:S(2)}, u32[]{:S(2)}) collective-permute-start(bf16[256,512]{1,0:T(8,128)(2,1)S(1)} %fusion.1), channel_id=1, source_target_pairs={{2,0},{4,2},{6,4},{8,6},{10,8},{12,10},{14,12},{16,14},{18,16},{20... | collective-permute-start | bytes 786440 | tf_op jit(solution)/shard_map/ppermute | solution.py:36
  135.1 5.3 %collective-permute-done.6 = bf16[256,512]{1,0:T(8,128)(2,1)S(1)} collective-permute-done((bf16[256,512]{1,0:T(8,128)(2,1)S(1)}, bf16[256,512]{1,0:T(8,128)(2,1)S(1)}, u32[]{:S(2)}, u32[]{:S(2)}) %collective-permute-start.6) | collective-permute-done | bytes 262176 | tf_op jit(solution)/shard_map/ppermute | solution.py:36
  140.4 0.1 fusion
  140.4 6.5 %collective-permute-start.7 = (bf16[256,512]{1,0:T(8,128)(2,1)S(1)}, bf16[256,512]{1,0:T(8,128)(2,1)S(1)}, u32[]{:S(2)}, u32[]{:S(2)}) collective-permute-start(bf16[256,512]{1,0:T(8,128)(2,1)S(1)} %fusion), channel_id=1, source_target_pairs={{2,0},{4,2},{6,4},{8,6},{10,8},{12,10},{14,12},{16,14},{18,16},{20... | collective-permute-start | bytes 786440 | tf_op jit(solution)/shard_map/ppermute | solution.py:36
  146.9 0.0 all-to-all-done.2
  147.0 2.7 %reduce_sum.12 = bf16[64,1024]{1,0:T(8,128)(2,1)} reduce(bf16[16,64,1024]{2,1,0:T(8,128)(2,1)} %all-to-all-done.2, bf16[]{:T(256)} %constant.2.clone.1), dimensions={0}, to_apply=%region_0.0 | reduce | flops 983040 | bytes 2228226 | tf_op jit(solution)/shard_map/reduce_sum | solution.py:238
  149.6 3.4 %all-to-all-start.3 = ((bf16[8,8,1024]{2,1,0:T(8,128)(2,1)}), bf16[8,8,1024]{2,1,0:T(8,128)(2,1)S(1)}, u32[]{:S(2)}, u32[]{:S(2)}) async-start(bf16[8,8,1024]{2,1,0:T(8,128)(2,1)} %bitcast.7), calls=%async_computation.3 | async-start | bytes 262144 | tf_op jit(solution)/shard_map/all_to_all | solution.py:239
  153.0 0.0 collective-permute-done.7.arrived
  153.0 0.0 copy-start.15
  153.0 9.0 %all-to-all-done.3.parts = bf16[8,8,1024]{2,1,0:T(8,128)(2,1)S(1)} async-done(((bf16[8,8,1024]{2,1,0:T(8,128)(2,1)}), bf16[8,8,1024]{2,1,0:T(8,128)(2,1)S(1)}, u32[]{:S(2)}, u32[]{:S(2)}) %all-to-all-start.3) | async-done | bytes 131104 | tf_op jit(solution)/shard_map/all_to_all | solution.py:239
  162.0 0.0 copy-done.15
  162.0 0.6 copy-done.14
  162.7 2.3 %shard_map.105 = (bf16[128,512]{1,0:T(8,128)(2,1)}, bf16[128,512]{1,0:T(8,128)(2,1)}) custom-call(s32[8]{0:T(128)} %starts.5, s32[8]{0:T(128)} %slots.3, f32[256,512]{1,0:T(8,128)} %copy-done.1, bf16[256,512]{1,0:T(8,128)(2,1)} %copy-done.15, bf16[8,8,1024]{2,1,0:T(8,128)(2,1)} %copy-done.14), custom_call_target="tpu_custom_call" | custom-call | tf_op jit(solution)/shard_map/pallas_call | solution.py:243
  (3 shorter events, 0.0 us)
Async XLA Ops:
  0.6 62.9 %copy-start = (bf16[512,2048]{1,0:T(8,128)(2,1)S(1)}, bf16[512,2048]{1,0:T(8,128)(2,1)}, u32[]{:S(2)}) copy-start(bf16[512,2048]{1,0:T(8,128)(2,1)} %param.12) | copy-start | bytes 6291460
  22.2 7.6 %copy-start.2 = (bf16[272,512]{1,0:T(8,128)(2,1)S(1)}, bf16[272,512]{1,0:T(8,128)(2,1)}, u32[]{:S(2)}) copy-start(bf16[272,512]{1,0:T(8,128)(2,1)} %get-tuple-element.11.own) | copy-start | bytes 835588
  22.2 53.0 %all-to-all-start.1 = ((bf16[16,64,1024]{2,1,0:T(8,128)(2,1)}), bf16[16,64,1024]{2,1,0:T(8,128)(2,1)}, u32[]{:S(2)}, u32[]{:S(2)}) async-start(bf16[16,64,1024]{2,1,0:T(8,128)(2,1)} %broadcast_in_dim.15), calls=%async_computation.1 | async-start | bytes 4194304 | tf_op jit(solution)/shard_map/all_to_all | solution.py:195
  29.8 10.6 %collective-permute-start = (bf16[272,512]{1,0:T(8,128)(2,1)S(1)}, bf16[272,512]{1,0:T(8,128)(2,1)S(1)}, u32[]{:S(2)}, u32[]{:S(2)}) collective-permute-start(bf16[272,512]{1,0:T(8,128)(2,1)S(1)} %copy-done.2), channel_id=1, source_target_pairs={{0,2},{2,4},{4,6},{6,8},{8,10},{10,12},{12,14},{14,16},{16,18},{18... | collective-permute-start | bytes 835592 | tf_op jit(solution)/shard_map/ppermute | solution.py:36
  40.3 34.8 %copy-start.3 = (bf16[272,512]{1,0:T(8,128)(2,1)}, bf16[272,512]{1,0:T(8,128)(2,1)S(1)}, u32[]{:S(2)}) copy-start(bf16[272,512]{1,0:T(8,128)(2,1)S(1)} %collective-permute-done.back1) | copy-start | bytes 835588
  40.3 10.6 %collective-permute-start.1 = (bf16[272,512]{1,0:T(8,128)(2,1)S(1)}, bf16[272,512]{1,0:T(8,128)(2,1)S(1)}, u32[]{:S(2)}, u32[]{:S(2)}) collective-permute-start(bf16[272,512]{1,0:T(8,128)(2,1)S(1)} %collective-permute-done.back1), channel_id=1, source_target_pairs={{0,2},{2,4},{4,6},{6,8},{8,10},{10,12},{12,14},{14,16},{16,18},{18... | collective-permute-start | bytes 835592 | tf_op jit(solution)/shard_map/ppermute | solution.py:36
  51.0 24.2 %copy-start.5 = (bf16[272,512]{1,0:T(8,128)(2,1)}, bf16[272,512]{1,0:T(8,128)(2,1)S(1)}, u32[]{:S(2)}) copy-start(bf16[272,512]{1,0:T(8,128)(2,1)S(1)} %collective-permute-done.1.back2) | copy-start | bytes 835588
  51.0 10.6 %collective-permute-start.2 = (bf16[272,512]{1,0:T(8,128)(2,1)S(1)}, bf16[272,512]{1,0:T(8,128)(2,1)S(1)}, u32[]{:S(2)}, u32[]{:S(2)}) collective-permute-start(bf16[272,512]{1,0:T(8,128)(2,1)S(1)} %collective-permute-done.1.back2), channel_id=1, source_target_pairs={{0,2},{2,4},{4,6},{6,8},{8,10},{10,12},{12,14},{14,16},{16,18},{18... | collective-permute-start | bytes 835592 | tf_op jit(solution)/shard_map/ppermute | solution.py:36
  61.6 13.5 %copy-start.7 = (bf16[272,512]{1,0:T(8,128)(2,1)}, bf16[272,512]{1,0:T(8,128)(2,1)S(1)}, u32[]{:S(2)}) copy-start(bf16[272,512]{1,0:T(8,128)(2,1)S(1)} %collective-permute-done.2.back3) | copy-start | bytes 835588
  61.6 10.6 %collective-permute-start.3 = (bf16[272,512]{1,0:T(8,128)(2,1)S(1)}, bf16[272,512]{1,0:T(8,128)(2,1)S(1)}, u32[]{:S(2)}, u32[]{:S(2)}) collective-permute-start(bf16[272,512]{1,0:T(8,128)(2,1)S(1)} %collective-permute-done.2.back3), channel_id=1, source_target_pairs={{0,2},{2,4},{4,6},{6,8},{8,10},{10,12},{12,14},{14,16},{16,18},{18... | collective-permute-start | bytes 835592 | tf_op jit(solution)/shard_map/ppermute | solution.py:36
  72.3 0.7 copy-start.9
  75.2 1.0 copy-start.4
  76.1 1.0 copy-start.6
  77.1 1.0 copy-start.8
  78.0 1.0 copy-start.10
  79.0 0.9 copy-start.11
  79.9 0.7 copy-start.12
  80.6 0.7 copy-start.13
  90.6 0.8 copy-start.1
  91.4 55.5 %all-to-all-start.2 = ((bf16[16,64,1024]{2,1,0:T(8,128)(2,1)}), bf16[16,64,1024]{2,1,0:T(8,128)(2,1)}, u32[]{:S(2)}, u32[]{:S(2)}) async-start(bf16[16,64,1024]{2,1,0:T(8,128)(2,1)} %bitcast.17), calls=%async_computation.2 | async-start | bytes 4194304 | tf_op jit(solution)/shard_map/all_to_all | solution.py:231
  107.3 8.7 %collective-permute-start.4 = (bf16[256,512]{1,0:T(8,128)(2,1)S(1)}, bf16[256,512]{1,0:T(8,128)(2,1)S(1)}, u32[]{:S(2)}, u32[]{:S(2)}) collective-permute-start(bf16[256,512]{1,0:T(8,128)(2,1)S(1)} %slice_bitcast_fusion), channel_id=1, source_target_pairs={{2,0},{4,2},{6,4},{8,6},{10,8},{12,10},{14,12},{16,14},{18,16},{20... | collective-permute-start | bytes 786440 | tf_op jit(solution)/shard_map/ppermute | solution.py:36
  116.1 12.4 %collective-permute-start.5 = (bf16[256,512]{1,0:T(8,128)(2,1)S(1)}, bf16[256,512]{1,0:T(8,128)(2,1)S(1)}, u32[]{:S(2)}, u32[]{:S(2)}) collective-permute-start(bf16[256,512]{1,0:T(8,128)(2,1)S(1)} %fusion.2), channel_id=1, source_target_pairs={{2,0},{4,2},{6,4},{8,6},{10,8},{12,10},{14,12},{16,14},{18,16},{20... | collective-permute-start | bytes 786440 | tf_op jit(solution)/shard_map/ppermute | solution.py:36
  128.6 11.8 %collective-permute-start.6 = (bf16[256,512]{1,0:T(8,128)(2,1)S(1)}, bf16[256,512]{1,0:T(8,128)(2,1)S(1)}, u32[]{:S(2)}, u32[]{:S(2)}) collective-permute-start(bf16[256,512]{1,0:T(8,128)(2,1)S(1)} %fusion.1), channel_id=1, source_target_pairs={{2,0},{4,2},{6,4},{8,6},{10,8},{12,10},{14,12},{16,14},{18,16},{20... | collective-permute-start | bytes 786440 | tf_op jit(solution)/shard_map/ppermute | solution.py:36
  140.4 12.6 %collective-permute-start.7 = (bf16[256,512]{1,0:T(8,128)(2,1)S(1)}, bf16[256,512]{1,0:T(8,128)(2,1)S(1)}, u32[]{:S(2)}, u32[]{:S(2)}) collective-permute-start(bf16[256,512]{1,0:T(8,128)(2,1)S(1)} %fusion), channel_id=1, source_target_pairs={{2,0},{4,2},{6,4},{8,6},{10,8},{12,10},{14,12},{16,14},{18,16},{20... | collective-permute-start | bytes 786440 | tf_op jit(solution)/shard_map/ppermute | solution.py:36
  149.6 12.4 %all-to-all-start.3 = ((bf16[8,8,1024]{2,1,0:T(8,128)(2,1)}), bf16[8,8,1024]{2,1,0:T(8,128)(2,1)S(1)}, u32[]{:S(2)}, u32[]{:S(2)}) async-start(bf16[8,8,1024]{2,1,0:T(8,128)(2,1)} %bitcast.7), calls=%async_computation.3 | async-start | bytes 262144 | tf_op jit(solution)/shard_map/all_to_all | solution.py:239
  153.0 9.0 %copy-start.15 = (bf16[256,512]{1,0:T(8,128)(2,1)}, bf16[256,512]{1,0:T(8,128)(2,1)S(1)}, u32[]{:S(2)}) copy-start(bf16[256,512]{1,0:T(8,128)(2,1)S(1)} %collective-permute-done.7.arrived) | copy-start | bytes 786436
  162.0 0.6 copy-start.14

commit v2 on v0

v2 whole, which is shorter than its diff:
```python
import math

import jax
import jax.numpy as jnp
from jax import lax
from jax.experimental import pallas as pl
from jax.experimental.pallas import tpu as pltpu
from jax.sharding import PartitionSpec as P

HD = 128
REACH = 4
TOK = 128
BARS_HERE = 8
HEADS_HERE = 4
FEAT = HD * HEADS_HERE
META = 16
ROWS = 2 * TOK + META
NZ = 8
NXY = 16
N_SEQ = NZ * NXY
OFFSETS = (1, 2, 4, 8, 12, 16, 24, 32)
SCALE = HD ** (-0.5)
LOG2E = math.log2(math.e)
EXP_SCALE = SCALE * LOG2E
LOWEST = -1e30

Z_GROUPS = [[j * NZ + z for z in range(NZ)] for j in range(NXY)]
XY_GROUPS = [[j * NZ + z for j in range(NXY)] for z in range(NZ)]
TO_NEXT = [(j * NZ + z, j * NZ + (z + 1) % NZ) for j in range(NXY) for z in range(NZ)]
TO_PREVIOUS = [(dst, src) for src, dst in TO_NEXT]
ROW_UP = [(i, i + NZ) for i in range(N_SEQ - NZ) if i % NZ >= NZ - REACH]
ROW_DOWN = [(dst, src) for src, dst in ROW_UP]

VMEM_LIMIT = 50 * 2**20
SMEM = pltpu.SMEM
VMEM = pltpu.VMEM
HBM = pltpu.HBM
NT = (((1,), (1,)), ((), ()))
TN = (((0,), (0,)), ((), ()))
BF16 = jnp.bfloat16
F32 = jnp.float32


def whole(space):
    return pl.BlockSpec(memory_space=space)


def shape(dims, dtype=BF16):
    return jax.ShapeDtypeStruct(dims, dtype)


def local_bar(starts, positions):
    count = jnp.zeros_like(positions)
    for b in range(1, BARS_HERE):
        count = count + (positions >= starts[b]).astype(jnp.int32)
    return count


def low(flags):
    return flags.astype(F32).astype(BF16)


def query_pack_kernel(starts, related, queries, grad_y, out_weight, packed):
    packed[0:TOK, :] = queries[...]
    grad_out = lax.dot_general(grad_y[...], out_weight[...], NT, preferred_element_type=F32)
    packed[TOK : 2 * TOK, :] = grad_out.astype(BF16)
    lane = lax.broadcasted_iota(jnp.int32, (META, TOK), 1)
    row = lax.broadcasted_iota(jnp.int32, (META, TOK), 0)
    bar = local_bar(starts, lane + starts[0])
    info = jnp.where(row == 0, bar, 0)
    for j in range(len(OFFSETS)):
        entry = jnp.zeros((META, TOK), jnp.int32)
        for b in range(BARS_HERE):
            has = (related[b, j] >= 0).astype(jnp.int32)
            entry = jnp.where(bar == b, has, entry)
        info = jnp.where(row == j + 1, entry, info)
    packed[2 * TOK :, :] = jnp.zeros((META, FEAT), BF16)
    packed[2 * TOK :, 0:TOK] = low(info)


def key_pack_kernel(starts, slots, keys, values, packed, sums):
    base = starts[0]
    packed[0:TOK, :] = keys[...]
    packed[TOK : 2 * TOK, :] = values[...]
    lane = lax.broadcasted_iota(jnp.int32, (META, TOK), 1)
    row = lax.broadcasted_iota(jnp.int32, (META, TOK), 0)
    packed[2 * TOK :, :] = jnp.zeros((META, FEAT), BF16)
    packed[2 * TOK :, 0:TOK] = low(local_bar(starts, lane + base))
    slot = jnp.full((META, TOK), -1, jnp.int32)
    for b in range(BARS_HERE):
        slot = jnp.where(row == b, slots[b] - base, slot)
    pick = low(lane == slot)
    for kind, source in ((0, keys), (1, values)):
        rows = jnp.dot(pick, source[...], preferred_element_type=F32)[0:BARS_HERE].astype(BF16)
        for h in range(HEADS_HERE):
            at = (2 * h + kind) * HD
            for j in range(NXY):
                sums[j, :, at : at + HD] = rows[:, h * HD : (h + 1) * HD]


def place_of(starts):
    rank = lax.shift_right_logical(starts[0], 7)
    return rank, jnp.bitwise_and(rank, NZ - 1)


def load_all(chunks, blocks, sums, packed, pairs, keys, sems):
    copies = [pltpu.make_async_copy(blocks[i], pairs.at[i], sems.at[i]) for i in range(2)]
    copies.append(pltpu.make_async_copy(sums, keys, sems.at[2]))
    copies += [
        pltpu.make_async_copy(chunks[o], packed.at[o], sems.at[3 + o]) for o in range(NZ)
    ]
    for copy in copies:
        copy.start()
    return copies


def build_bias(starts, packed, pairs, bias):
    rank, z = place_of(starts)
    own_local, previous_local = (
        jnp.transpose(
            jnp.broadcast_to(pairs[i, 2 * TOK :, 0:TOK].astype(F32)[0:1], (TOK, TOK))
        ).astype(jnp.int32)
        for i in range(2)
    )
    key_row = lax.broadcasted_iota(jnp.int32, (TOK, TOK), 0)
    token_col = lax.broadcasted_iota(jnp.int32, (TOK, TOK), 1)
    summary_bar = (
        lax.shift_right_logical(key_row, 3) * (NZ * BARS_HERE)
        + jnp.bitwise_and(key_row, BARS_HERE - 1)
        + z * BARS_HERE
    )
    for o in range(NZ):
        owner = rank - z + jnp.bitwise_and(z + o, NZ - 1)
        info = packed[o, 2 * TOK :, 0:TOK].astype(F32).astype(jnp.int32)
        token_bar = info[0:1] + owner * BARS_HERE
        rel = [
            jnp.where(info[j + 1 : j + 2] > 0, token_bar - OFFSETS[j], -1)
            for j in range(len(OFFSETS))
        ]
        if o <= REACH:
            key_owner = owner - o
            key_local = jnp.where(z + o >= NZ, previous_local, own_local)
            key_bar = jnp.where(key_owner >= 0, key_local + key_owner * BARS_HERE, -2)
            seen = key_bar == rel[0]
            for entry in rel[1:]:
                seen = seen | (key_bar == entry)
            if o == 0:
                seen = seen | ((key_bar == token_bar) & (key_row <= token_col))
            bias[o] = jnp.where(seen, 0.0, -jnp.inf)
        hidden = summary_bar >= token_bar
        for entry in rel:
            hidden = hidden | (summary_bar == entry)
        bias[REACH + 1 + o] = jnp.where(hidden, -jnp.inf, 0.0)


def products(starts, packed, pairs, keys, bias, h, o):
    _, z = place_of(starts)
    cols = slice(h * HD, (h + 1) * HD)
    at = 2 * h * HD
    query = packed[o, 0:TOK, cols]
    grad = packed[o, TOK : 2 * TOK, cols]
    key, value = keys[:, at : at + HD], keys[:, at + HD : at + 2 * HD]
    mask = bias[REACH + 1 + o]
    if o <= REACH:
        side = lax.shift_right_logical(z + o, 3)
        key = jnp.concatenate([pairs[side, 0:TOK, cols], key], axis=0)
        value = jnp.concatenate([pairs[side, TOK : 2 * TOK, cols], value], axis=0)
        mask = jnp.concatenate([bias[o], mask], axis=0)
    scores = lax.dot_general(key, query, NT, preferred_element_type=F32)
    dprobs = lax.dot_general(value, grad, NT, preferred_element_type=F32)
    return key, query, grad, scores, dprobs, mask


def stats_kernel(*refs):
    starts, *refs = refs
    chunks, (own, previous, sums, stats, bias_out), refs = refs[:NZ], refs[NZ : NZ + 5], refs[NZ + 5 :]
    packed, pairs, keys, bias, sems, bias_sem = refs
    copies = load_all(chunks, (own, previous), sums, packed, pairs, keys, sems)
    for copy in copies:
        copy.wait()
    build_bias(starts, packed, pairs, bias)
    bias_copy = pltpu.make_async_copy(bias, bias_out, bias_sem)
    bias_copy.start()
    _, z = place_of(starts)
    for o in range(NZ):
        chunk = jnp.bitwise_and(z + o, NZ - 1)
        log_sums, means = [], []
        for h in range(HEADS_HERE):
            _, _, _, scores, dprobs, mask = products(starts, packed, pairs, keys, bias, h, o)
            scores = scores + mask
            top = jnp.maximum(jnp.max(scores, axis=0, keepdims=True), LOWEST)
            weights = jnp.exp2((scores - top) * EXP_SCALE)
            total = jnp.sum(weights, axis=0, keepdims=True)
            weighted = jnp.sum(weights * dprobs, axis=0, keepdims=True)
            log_sums.append(top * EXP_SCALE + jnp.log(total) * LOG2E)
            means.append(jnp.where(total > 0.0, weighted / total, 0.0))
        merged = jnp.concatenate(log_sums + means, axis=0)
        for peer in range(NZ):
            stats[peer, chunk] = merged
    bias_copy.wait()


def grads_kernel(*refs):
    starts, *refs = refs
    chunks, (own, previous, sums, bias_in, stats), refs = refs[:NZ], refs[NZ : NZ + 5], refs[NZ + 5 :]
    query_grad, previous_grad, own_grad, sum_grad = refs[:4]
    packed, pairs, keys, bias, merged, sems, bias_sem = refs[4:]
    copies = load_all(chunks, (own, previous), sums, packed, pairs, keys, sems)
    copies.append(pltpu.make_async_copy(bias_in, bias, bias_sem))
    copies[-1].start()
    top = stats[0, :, 0:HEADS_HERE, :]
    for i in range(1, NZ):
        top = jnp.maximum(top, stats[i, :, 0:HEADS_HERE, :])
    total = jnp.zeros_like(top)
    mean = jnp.zeros_like(top)
    for i in range(NZ):
        weight = jnp.exp2(stats[i, :, 0:HEADS_HERE, :] - top)
        total = total + weight
        mean = mean + weight * stats[i, :, HEADS_HERE:, :]
    merged[:, 0:HEADS_HERE, :] = top + jnp.log(total) * LOG2E
    merged[:, HEADS_HERE:, :] = mean / total
    for copy in copies:
        copy.wait()
    _, z = place_of(starts)
    for h in range(HEADS_HERE):
        cols = slice(h * HD, (h + 1) * HD)
        at = 2 * h * HD
        own_key = jnp.zeros((TOK, HD), F32)
        own_value, previous_key, previous_value = own_key, own_key, own_key
        probs_parts, dscores_parts, queries, grads = [], [], [], []
        for o in range(NZ):
            chunk = jnp.bitwise_and(z + o, NZ - 1)
            key, query, grad, scores, dprobs, mask = products(
                starts, packed, pairs, keys, bias, h, o
            )
            log_sum = merged[chunk, h : h + 1, :]
            delta = merged[chunk, HEADS_HERE + h : HEADS_HERE + h + 1, :]
            probs = jnp.exp2(scores * EXP_SCALE - log_sum + mask)
            probs_low = probs.astype(BF16)
            dscores = (probs * (dprobs - delta)).astype(BF16)
            dquery = lax.dot_general(dscores, key, TN, preferred_element_type=F32)
            query_grad[chunk, :, cols] = (SCALE * dquery).astype(BF16)
            if o <= REACH:
                dkey = jnp.dot(dscores[0:TOK], query, preferred_element_type=F32)
                dvalue = jnp.dot(probs_low[0:TOK], grad, preferred_element_type=F32)
                wraps = (z + o >= NZ).astype(F32)
                own_key = own_key + dkey * (1.0 - wraps)
                own_value = own_value + dvalue * (1.0 - wraps)
                previous_key = previous_key + dkey * wraps
                previous_value = previous_value + dvalue * wraps
                dscores, probs_low = dscores[TOK:], probs_low[TOK:]
            probs_parts.append(probs_low)
            dscores_parts.append(dscores)
            queries.append(query)
            grads.append(grad)
        own_grad[0:TOK, cols] = own_key * SCALE
        own_grad[TOK : 2 * TOK, cols] = own_value
        previous_grad[0:TOK, cols] = (previous_key * SCALE).astype(BF16)
        previous_grad[TOK : 2 * TOK, cols] = previous_value.astype(BF16)
        dkey = jnp.dot(
            jnp.concatenate(dscores_parts, axis=1),
            jnp.concatenate(queries, axis=0),
            preferred_element_type=F32,
        )
        dvalue = jnp.dot(
            jnp.concatenate(probs_parts, axis=1),
            jnp.concatenate(grads, axis=0),
            preferred_element_type=F32,
        )
        sum_grad[:, at : at + HD] = (dkey * SCALE).astype(BF16)
        sum_grad[:, at + HD : at + 2 * HD] = dvalue.astype(BF16)


def finish_kernel(starts, slots, own_grad, arrived, parts, grad_keys, grad_values):
    base = starts[0]
    total = parts[0].astype(F32)
    for i in range(1, NXY):
        total = total + parts[i].astype(F32)
    row = lax.broadcasted_iota(jnp.int32, (TOK, HD), 0)
    for h in range(HEADS_HERE):
        cols = slice(h * HD, (h + 1) * HD)
        for kind, out in ((0, grad_keys), (1, grad_values)):
            rows = slice(kind * TOK, (kind + 1) * TOK)
            at = (2 * h + kind) * HD
            grad = own_grad[rows, cols] + arrived[rows, cols].astype(F32)
            for b in range(BARS_HERE):
                grad = grad + jnp.where(row == slots[b] - base, total[b : b + 1, at : at + HD], 0.0)
            out[:, cols] = grad.astype(BF16)


def query_sum_kernel(parts, grad_queries):
    total = parts[0].astype(F32)
    for i in range(1, NZ):
        total = total + parts[i].astype(F32)
    grad_queries[...] = total.astype(BF16)


def shards(queries, keys, values, grad_y, out_weight, bar_start, related, bar_summary_token):
    params = pltpu.CompilerParams(vmem_limit_bytes=VMEM_LIMIT)
    packed = pl.pallas_call(
        query_pack_kernel,
        out_shape=shape((ROWS, FEAT)),
        in_specs=[whole(SMEM)] * 2 + [whole(VMEM)] * 3,
        out_specs=whole(VMEM),
        compiler_params=params,
    )(bar_start, related, queries, lax.all_gather(grad_y, "head", axis=1, tiled=True), out_weight)

    after, before = [packed], [packed]
    after.append(lax.ppermute(after[-1], "seq", TO_PREVIOUS))
    before.append(lax.ppermute(before[-1], "seq", TO_NEXT))

    own, sums = pl.pallas_call(
        key_pack_kernel,
        out_shape=(shape((ROWS, FEAT)), shape((NXY, BARS_HERE, 2 * FEAT))),
        in_specs=[whole(SMEM)] * 2 + [whole(VMEM)] * 2,
        out_specs=(whole(VMEM),) * 2,
    )(bar_start, bar_summary_token, keys, values)
    previous = lax.ppermute(own, "seq", ROW_UP)
    all_sums = lax.all_to_all(sums, "seq", 0, 0, axis_index_groups=XY_GROUPS).reshape(
        NXY * BARS_HERE, 2 * FEAT
    )

    for _ in range(2):
        after.append(lax.ppermute(after[-1], "seq", TO_PREVIOUS))
        before.append(lax.ppermute(before[-1], "seq", TO_NEXT))
    after.append(lax.ppermute(after[-1], "seq", TO_PREVIOUS))
    chunks = after + before[:0:-1]

    held = [
        VMEM((NZ, ROWS, FEAT), BF16),
        VMEM((2, ROWS, FEAT), BF16),
        VMEM((NXY * BARS_HERE, 2 * FEAT), BF16),
        VMEM((REACH + 1 + NZ, TOK, TOK), F32),
    ]
    sems = [pltpu.SemaphoreType.DMA((NZ + 3,)), pltpu.SemaphoreType.DMA]
    stats, bias = pl.pallas_call(
        stats_kernel,
        out_shape=(
            shape((NZ, NZ, 2 * HEADS_HERE, TOK), F32),
            shape((REACH + 1 + NZ, TOK, TOK), F32),
        ),
        in_specs=[whole(SMEM)] + [whole(HBM)] * (NZ + 3),
        out_specs=(whole(VMEM), whole(HBM)),
        scratch_shapes=held + sems,
        compiler_params=params,
    )(bar_start, *chunks, own, previous, all_sums)

    stats = lax.all_to_all(stats, "seq", 0, 0, axis_index_groups=Z_GROUPS)

    query_grad, previous_grad, own_grad, sum_grad = pl.pallas_call(
        grads_kernel,
        out_shape=(
            shape((NZ, TOK, FEAT)),
            shape((2 * TOK, FEAT)),
            shape((2 * TOK, FEAT), F32),
            shape((NXY * BARS_HERE, 2 * FEAT)),
        ),
        in_specs=[whole(SMEM)] + [whole(HBM)] * (NZ + 4) + [whole(VMEM)],
        out_specs=(whole(VMEM),) * 4,
        scratch_shapes=held + [VMEM((NZ, 2 * HEADS_HERE, TOK), F32)] + sems,
        compiler_params=params,
    )(bar_start, *chunks, own, previous, all_sums, bias, stats)

    query_parts = lax.all_to_all(query_grad, "seq", 0, 0, axis_index_groups=Z_GROUPS)
    parts = lax.all_to_all(
        sum_grad.reshape(NXY, BARS_HERE, 2 * FEAT), "seq", 0, 0, axis_index_groups=XY_GROUPS
    )
    arrived = lax.ppermute(previous_grad, "seq", ROW_DOWN)

    grad_keys, grad_values = pl.pallas_call(
        finish_kernel,
        out_shape=(shape((TOK, FEAT)), shape((TOK, FEAT))),
        in_specs=[whole(SMEM)] * 2 + [whole(VMEM)] * 3,
        out_specs=(whole(VMEM),) * 2,
    )(bar_start, bar_summary_token, own_grad, arrived, parts)
    grad_queries = pl.pallas_call(
        query_sum_kernel,
        out_shape=shape((TOK, FEAT)),
        in_specs=[whole(VMEM)],
        out_specs=whole(VMEM),
    )(query_parts)
    return grad_queries, grad_keys, grad_values


def solution(mesh):
    in_specs = (
        P("seq", "head"),
        P("seq", "head"),
        P("seq", "head"),
        P("seq", "head"),
        P("head", None),
        P("seq"),
        P("seq", None),
        P("seq"),
    )
    out_specs = (P("seq", "head"), P("seq", "head"), P("seq", "head"))
    return jax.shard_map(shards, mesh=mesh, in_specs=in_specs, out_specs=out_specs, check_vma=False)
```

time: 1660 us -> 128 us (0.08); the launches traced: 1640 us -> 127 us
  waiting for transfers between devices: 1460 us -> 32.1 us
  starting transfers between devices: 91.4 us -> 22 us
  blocking collectives: 2.39 us -> 42.7 us
  matrix products: 26.4 us -> 0 us
  local copies, waits for them, and re-layouts: 32.6 us -> 6.48 us
  Pallas kernels: 0 us -> 23.3 us
    reduce_scatter x2 -> x0, waiting for transfers between devices: 1300 us -> none  [the longest x1 692 us: shards(): lax.psum_scatter(value_grads[local_window:], 'seq', scatter_dimension=0,...]
    all_gather x2 -> x0, waiting for transfers between devices: 125 us -> none  [the longest x1 94.5 us: shards(): lax.all_gather(values[slot_rows], 'seq', axis=0, tiled=True)]
    ppermute x20 -> x9, starting transfers between devices: 91.1 us -> 18.4 us  [the longest x4 17 us: shards(): after.append(lax.ppermute(after[-1], 'seq', TO_PREVIOUS))]
    all_to_all x0 -> x3, blocking collectives: none -> 40.3 us  [the longest x1 14.8 us: shards(): lax.all_to_all(sums, 'seq', 0, 0, axis_index_groups=XY_GROUPS)]
    dot_general x27 -> x0, matrix products: 26.4 us -> none  [the longest x4 5.75 us: shards(): jnp.dot(dscores, key_head, preferred_element_type=jnp.float32)]
    ppermute x20 -> x9, waiting for transfers between devices: 36.8 us -> 13.4 us  [the longest x4 13.4 us: shards(): after.append(lax.ppermute(after[-1], 'seq', TO_PREVIOUS))]
    pallas_call x0 -> x6, Pallas kernels: none -> 23.3 us  [the longest x1 11.4 us: shards(): pl.pallas_call(grads_kernel, out_shape=(shape((NZ, TOK, FEAT)), shape((2...]
    all_to_all x0 -> x1, waiting for transfers between devices: none -> 18.7 us  [shards(): lax.all_to_all(query_grad, 'seq', 0, 0, axis_index_groups=Z_GROUPS)]
  transfers between devices with their start and end apart: 24 -> 10, of which waited for: 11 -> 4; matrix products, arithmetic and copies ran while one was open for 3% -> 0% of each run, Pallas kernels for 0% -> 3%
where the time goes in v2:
time: 128 us; the launch traced here: 127 us
  blocking collectives  42.7 us (33%)
  waiting for transfers between devices  32.1 us (25%)
  Pallas kernels  23.3 us (18%)
  starting transfers between devices  22 us (17%)
  local copies, waits for them, and re-layouts  6.48 us (5%)
    all_to_all x1, waiting for transfers between devices, shards(): lax.all_to_all(query_grad, 'seq', 0, 0, axis_index_groups=Z_GROUPS)  18.7 us
    ppermute x4, starting transfers between devices, shards(): after.append(lax.ppermute(after[-1], 'seq', TO_PREVIOUS))  17 us
    all_to_all x1, blocking collectives, shards(): lax.all_to_all(sums, 'seq', 0, 0, axis_index_groups=XY_GROUPS)  14.8 us
    all_to_all x1, blocking collectives, shards(): stats = lax.all_to_all(stats, 'seq', 0, 0, axis_index_groups=Z_GROUPS)  13.6 us
    ppermute x4, waiting for transfers between devices, shards(): after.append(lax.ppermute(after[-1], 'seq', TO_PREVIOUS))  13.4 us
    all_to_all x1, blocking collectives, shards(): lax.all_to_all(sum_grad.reshape(NXY, BARS_HERE, 2 * FEAT), 'seq', 0, 0, a...  12 us
    pallas_call x1, Pallas kernels, shards(): pl.pallas_call(grads_kernel, out_shape=(shape((NZ, TOK, FEAT)), shape((2...  11.4 us
    unnamed x16, local copies, waits for them, and re-layouts  6.48 us
  transfers between devices with their start and end apart: 10, of which 4 were waited for; matrix products, arithmetic and copies ran while one was open for 0% of the time, Pallas kernels for 3%

profile of v2, /device:TPU:2, one launch (start us, length us, event | category | flops | bytes accessed | tf_op | source)
XLA Modules:
  0.0 127.4 jit_solution(11164493969413173483)
XLA Ops:
  0.6 2.4 %all_gather.3.grad_y = bf16[128,2048]{1,0:T(8,128)(2,1)S(1)} all-gather(bf16[128,1024]{1,0:T(8,128)(2,1)} %param.11), channel_id=1, replica_groups=mesh['seq'=128,'head'=2] {'head'}, dimensions={1}, use_global_device_ids=true | all-gather | bytes 786432 | tf_op jit(solution)/shard_map/all_gather | solution.py:306
  3.0 0.0 copy-start
  3.0 1.6 %copy-done = bf16[512,2048]{1,0:T(8,128)(2,1)S(1)} copy-done((bf16[512,2048]{1,0:T(8,128)(2,1)S(1)}, bf16[512,2048]{1,0:T(8,128)(2,1)}, u32[]{:S(2)}) %copy-start) | copy-done | bytes 2097176
  4.6 0.0 copy-start.2
  4.6 0.9 copy-done.2
  5.5 0.0 copy-start.3
  5.5 0.7 copy-done.3
  6.2 0.0 copy-start.5
  6.2 0.7 copy-done.5
  6.9 0.0 copy-start.4
  6.9 1.4 %shard_map.103.refs_1_ = bf16[272,512]{1,0:T(8,128)(2,1)S(1)} custom-call(s32[8]{0:T(128)S(1)} %copy-done.3, s32[8,8]{1,0:T(8,128)S(1)} %copy-done.5, bf16[128,512]{1,0:T(8,128)(2,1)S(1)} %copy-done.2, bf16[128,2048]{1,0:T(8,128)(2,1)S(1)} %all_gather.3.grad_y, bf16[512,2048]{1,0:T(8,128)(2,1)S(1)} %copy-done), custom_call_target="tpu_custom_call" | custom-call | tf_op jit(solution)/shard_map/pallas_call | solution.py:300
  8.3 5.9 %collective-permute-start = (bf16[272,512]{1,0:T(8,128)(2,1)S(1)}, bf16[272,512]{1,0:T(8,128)(2,1)S(1)}, u32[]{:S(2)}, u32[]{:S(2)}) collective-permute-start(bf16[272,512]{1,0:T(8,128)(2,1)S(1)} %shard_map.103.refs_1_), channel_id=1, source_target_pairs={{2,0},{4,2},{6,4},{8,6},{10,8},{12,10},{14,12},{0,14},{18,16},{20,... | collective-permute-start | bytes 835592 | tf_op jit(solution)/shard_map/ppermute | solution.py:309
  14.2 0.0 collective-permute-start.4
  14.2 6.2 %collective-permute-done.refs_2_ = bf16[272,512]{1,0:T(8,128)(2,1)S(1)} collective-permute-done((bf16[272,512]{1,0:T(8,128)(2,1)S(1)}, bf16[272,512]{1,0:T(8,128)(2,1)S(1)}, u32[]{:S(2)}, u32[]{:S(2)}) %collective-permute-start) | collective-permute-done | bytes 278560 | tf_op jit(solution)/shard_map/ppermute | solution.py:309
  20.5 3.7 %collective-permute-start.1 = (bf16[272,512]{1,0:T(8,128)(2,1)S(1)}, bf16[272,512]{1,0:T(8,128)(2,1)S(1)}, u32[]{:S(2)}, u32[]{:S(2)}) collective-permute-start(bf16[272,512]{1,0:T(8,128)(2,1)S(1)} %collective-permute-done.refs_2_), channel_id=1, source_target_pairs={{2,0},{4,2},{6,4},{8,6},{10,8},{12,10},{14,12},{0,14},{18,16},{20,... | collective-permute-start | bytes 835592 | tf_op jit(solution)/shard_map/ppermute | solution.py:324
  24.2 0.0 collective-permute-done.4.refs_8_
  24.2 0.0 collective-permute-start.5
  24.2 5.4 %collective-permute-done.1.refs_3_ = bf16[272,512]{1,0:T(8,128)(2,1)S(1)} collective-permute-done((bf16[272,512]{1,0:T(8,128)(2,1)S(1)}, bf16[272,512]{1,0:T(8,128)(2,1)S(1)}, u32[]{:S(2)}, u32[]{:S(2)}) %collective-permute-start.1) | collective-permute-done | bytes 278560 | tf_op jit(solution)/shard_map/ppermute | solution.py:324
  29.5 3.7 %collective-permute-start.2 = (bf16[272,512]{1,0:T(8,128)(2,1)S(1)}, bf16[272,512]{1,0:T(8,128)(2,1)S(1)}, u32[]{:S(2)}, u32[]{:S(2)}) collective-permute-start(bf16[272,512]{1,0:T(8,128)(2,1)S(1)} %collective-permute-done.1.refs_3_), channel_id=1, source_target_pairs={{2,0},{4,2},{6,4},{8,6},{10,8},{12,10},{14,12},{0,14},{18,16},{20,... | collective-permute-start | bytes 835592 | tf_op jit(solution)/shard_map/ppermute | solution.py:324
  33.2 1.9 %shard_map.104 = (bf16[272,512]{1,0:T(8,128)(2,1)}, bf16[16,8,1024]{2,1,0:T(8,128)(2,1)}) custom-call(s32[8]{0:T(128)} %starts.5, s32[8]{0:T(128)} %slots.3, bf16[128,512]{1,0:T(8,128)(2,1)} %keys.1, bf16[128,512]{1,0:T(8,128)(2,1)} %values.1), custom_call_target="tpu_custom_call" | custom-call | tf_op jit(solution)/shard_map/pallas_call | solution.py:312
  35.1 0.7 collective-permute-start.7
  35.8 0.0 collective-permute-done.5.refs_7_
  35.8 0.1 collective-permute-start.6
  35.9 1.8 %collective-permute-done.2.refs_4_ = bf16[272,512]{1,0:T(8,128)(2,1)S(1)} collective-permute-done((bf16[272,512]{1,0:T(8,128)(2,1)S(1)}, bf16[272,512]{1,0:T(8,128)(2,1)S(1)}, u32[]{:S(2)}, u32[]{:S(2)}) %collective-permute-start.2) | collective-permute-done | bytes 278560 | tf_op jit(solution)/shard_map/ppermute | solution.py:324
  37.7 3.7 %collective-permute-start.3 = (bf16[272,512]{1,0:T(8,128)(2,1)S(1)}, bf16[272,512]{1,0:T(8,128)(2,1)S(1)}, u32[]{:S(2)}, u32[]{:S(2)}) collective-permute-start(bf16[272,512]{1,0:T(8,128)(2,1)S(1)} %collective-permute-done.2.refs_4_), channel_id=1, source_target_pairs={{2,0},{4,2},{6,4},{8,6},{10,8},{12,10},{14,12},{0,14},{18,16},{20,... | collective-permute-start | bytes 835592 | tf_op jit(solution)/shard_map/ppermute | solution.py:326
  41.4 14.8 %all_to_all.20 = bf16[16,8,1024]{2,1,0:T(8,128)(2,1)S(1)} all-to-all(bf16[16,8,1024]{2,1,0:T(8,128)(2,1)} %get-tuple-element.14), channel_id=1, replica_groups={{0,16,32,48,64,80,96,112,128,144,160,176,192,208,224,240},{2,18,34,50,6..., dimensions={0} | all-to-all | bytes 524288 | tf_op jit(solution)/shard_map/all_to_all | solution.py:319
  56.2 0.0 collective-permute-done.7.refs_10_
  56.2 0.0 collective-permute-done.6.refs_6_
  56.2 0.0 collective-permute-done.3.refs_5_
  56.2 0.0 copy-done.4
  56.2 0.0 copy-start.1
  56.2 0.9 copy-done.1
  57.2 4.1 %shard_map.105 = (f32[8,8,8,128]{3,2,1,0:T(8,128)S(1)}, f32[13,128,128]{2,1,0:T(8,128)}) custom-call(s32[8]{0:T(128)S(1)} %copy-done.4, bf16[272,512]{1,0:T(8,128)(2,1)S(1)} %shard_map.103.refs_1_, bf16[272,512]{1,0:T(8,128)(2,1)S(1)} %collective-permute-done.refs_2_, bf16[272,512]{1,0:T(8,128)(2,1)S(1)} %collective-permute-done.1.refs_3_, ...), custom_call_target="tpu_custom_call" | custom-call | tf_op jit(solution)/shard_map/pallas_call | solution.py:336
  61.3 13.6 %all_to_all.21.refs_13_ = f32[8,8,8,128]{3,2,1,0:T(8,128)S(1)} all-to-all(f32[8,8,8,128]{3,2,1,0:T(8,128)S(1)} %get-tuple-element.16), channel_id=1, replica_groups={{0,2,4,6,8,10,12,14},{16,18,20,22,24,26,28,30},{32,34,36,38,40,42,44,46..., dimensions={0} | all-to-all | bytes 524288 | tf_op jit(solution)/shard_map/all_to_all | solution.py:348
  74.9 11.4 %shard_map.106 = (bf16[8,128,512]{2,1,0:T(8,128)(2,1)}, bf16[256,512]{1,0:T(8,128)(2,1)S(1)}, f32[256,512]{1,0:T(8,128)}, bf16[128,1024]{1,0:T(8,128)(2,1)S(1)}) custom-call(s32[8]{0:T(128)S(1)} %copy-done.4, bf16[272,512]{1,0:T(8,128)(2,1)S(1)} %shard_map.103.refs_1_, bf16[272,512]{1,0:T(8,128)(2,1)S(1)} %collective-permute-done.refs_2_, ...), custom_call_target="tpu_custom_call" | custom-call | tf_op jit(solution)/shard_map/pallas_call | solution.py:350
  86.2 12.0 %all_to_all.22.parts = bf16[16,8,1024]{2,1,0:T(8,128)(2,1)} all-to-all(bf16[16,8,1024]{2,1,0:T(8,128)(2,1)S(1)} %bitcast.4), channel_id=1, replica_groups={{0,16,32,48,64,80,96,112,128,144,160,176,192,208,224,240},{2,18,34,50,6..., dimensions={0} | all-to-all | bytes 524288 | tf_op jit(solution)/shard_map/all_to_all | solution.py:365
  98.2 3.6 %all-to-all-start.2 = ((bf16[8,128,512]{2,1,0:T(8,128)(2,1)}), bf16[8,128,512]{2,1,0:T(8,128)(2,1)S(1)}, u32[]{:S(2)}, u32[]{:S(2)}) async-start(bf16[8,128,512]{2,1,0:T(8,128)(2,1)} %get-tuple-element.17), calls=%async_computation.2 | async-start | bytes 2097152 | tf_op jit(solution)/shard_map/all_to_all | solution.py:364
  101.8 0.7 collective-permute-start.8
  102.5 0.0 collective-permute-done.8.arrived
  102.5 0.0 copy-start.7
  102.5 0.7 copy-done.7
  103.2 2.5 %shard_map.108 = (bf16[128,512]{1,0:T(8,128)(2,1)}, bf16[128,512]{1,0:T(8,128)(2,1)}) custom-call(s32[8]{0:T(128)} %starts.5, s32[8]{0:T(128)} %slots.3, f32[256,512]{1,0:T(8,128)} %get-tuple-element.18.own_grad, bf16[256,512]{1,0:T(8,128)(2,1)} %copy-done.7, bf16[16,8,1024]{2,1,0:T(8,128)(2,1)} %all_to_all.22.parts), custom_call_target="tpu_custom_call" | custom-call | tf_op jit(solution)/shard_map/pallas_call | solution.py:370
  105.7 18.7 %all-to-all-done.2.parts = bf16[8,128,512]{2,1,0:T(8,128)(2,1)S(1)} async-done(((bf16[8,128,512]{2,1,0:T(8,128)(2,1)}), bf16[8,128,512]{2,1,0:T(8,128)(2,1)S(1)}, u32[]{:S(2)}, u32[]{:S(2)}) %all-to-all-start.2) | async-done | bytes 1048608 | tf_op jit(solution)/shard_map/all_to_all | solution.py:364
  124.4 0.0 copy-start.6
  124.4 1.0 copy-done.6
  125.4 2.0 %shard_map.107 = bf16[128,512]{1,0:T(8,128)(2,1)} custom-call(bf16[8,128,512]{2,1,0:T(8,128)(2,1)} %copy-done.6), custom_call_target="tpu_custom_call" | custom-call | tf_op jit(solution)/shard_map/pallas_call | solution.py:376
Async XLA Ops:
  3.0 1.6 %copy-start = (bf16[512,2048]{1,0:T(8,128)(2,1)S(1)}, bf16[512,2048]{1,0:T(8,128)(2,1)}, u32[]{:S(2)}) copy-start(bf16[512,2048]{1,0:T(8,128)(2,1)} %out_weight.1) | copy-start | bytes 6291460
  4.6 0.9 copy-start.2
  5.5 0.7 copy-start.3
  6.2 0.7 copy-start.5
  6.9 49.3 %copy-start.4 = (s32[8]{0:T(128)S(1)}, s32[8]{0:T(128)}, u32[]{:S(2)}) copy-start(s32[8]{0:T(128)} %starts.5) | copy-start | bytes 100
  8.3 12.2 %collective-permute-start = (bf16[272,512]{1,0:T(8,128)(2,1)S(1)}, bf16[272,512]{1,0:T(8,128)(2,1)S(1)}, u32[]{:S(2)}, u32[]{:S(2)}) collective-permute-start(bf16[272,512]{1,0:T(8,128)(2,1)S(1)} %shard_map.103.refs_1_), channel_id=1, source_target_pairs={{2,0},{4,2},{6,4},{8,6},{10,8},{12,10},{14,12},{0,14},{18,16},{20,... | collective-permute-start | bytes 835592 | tf_op jit(solution)/shard_map/ppermute | solution.py:309
  14.2 9.9 %collective-permute-start.4 = (bf16[272,512]{1,0:T(8,128)(2,1)S(1)}, bf16[272,512]{1,0:T(8,128)(2,1)S(1)}, u32[]{:S(2)}, u32[]{:S(2)}) collective-permute-start(bf16[272,512]{1,0:T(8,128)(2,1)S(1)} %shard_map.103.refs_1_), channel_id=1, source_target_pairs={{0,2},{2,4},{4,6},{6,8},{8,10},{10,12},{12,14},{14,0},{16,18},{18,... | collective-permute-start | bytes 835592 | tf_op jit(solution)/shard_map/ppermute | solution.py:310
  20.5 9.1 %collective-permute-start.1 = (bf16[272,512]{1,0:T(8,128)(2,1)S(1)}, bf16[272,512]{1,0:T(8,128)(2,1)S(1)}, u32[]{:S(2)}, u32[]{:S(2)}) collective-permute-start(bf16[272,512]{1,0:T(8,128)(2,1)S(1)} %collective-permute-done.refs_2_), channel_id=1, source_target_pairs={{2,0},{4,2},{6,4},{8,6},{10,8},{12,10},{14,12},{0,14},{18,16},{20,... | collective-permute-start | bytes 835592 | tf_op jit(solution)/shard_map/ppermute | solution.py:324
  24.2 11.6 %collective-permute-start.5 = (bf16[272,512]{1,0:T(8,128)(2,1)S(1)}, bf16[272,512]{1,0:T(8,128)(2,1)S(1)}, u32[]{:S(2)}, u32[]{:S(2)}) collective-permute-start(bf16[272,512]{1,0:T(8,128)(2,1)S(1)} %collective-permute-done.4.refs_8_), channel_id=1, source_target_pairs={{0,2},{2,4},{4,6},{6,8},{8,10},{10,12},{12,14},{14,0},{16,18},{18,... | collective-permute-start | bytes 835592 | tf_op jit(solution)/shard_map/ppermute | solution.py:325
  29.5 8.2 %collective-permute-start.2 = (bf16[272,512]{1,0:T(8,128)(2,1)S(1)}, bf16[272,512]{1,0:T(8,128)(2,1)S(1)}, u32[]{:S(2)}, u32[]{:S(2)}) collective-permute-start(bf16[272,512]{1,0:T(8,128)(2,1)S(1)} %collective-permute-done.1.refs_3_), channel_id=1, source_target_pairs={{2,0},{4,2},{6,4},{8,6},{10,8},{12,10},{14,12},{0,14},{18,16},{20,... | collective-permute-start | bytes 835592 | tf_op jit(solution)/shard_map/ppermute | solution.py:324
  35.1 21.1 %collective-permute-start.7 = (bf16[272,512]{1,0:T(8,128)(2,1)}, bf16[272,512]{1,0:T(8,128)(2,1)S(1)}, u32[]{:S(2)}, u32[]{:S(2)}) collective-permute-start(bf16[272,512]{1,0:T(8,128)(2,1)} %get-tuple-element.13.refs_9_), channel_id=1, source_target_pairs={{8,24},{10,26},{12,28},{14,30},{24,40},{26,42},{28,44},{30,46},{40... | collective-permute-start | bytes 835592 | tf_op jit(solution)/shard_map/ppermute | solution.py:318
  35.8 20.4 %collective-permute-start.6 = (bf16[272,512]{1,0:T(8,128)(2,1)S(1)}, bf16[272,512]{1,0:T(8,128)(2,1)S(1)}, u32[]{:S(2)}, u32[]{:S(2)}) collective-permute-start(bf16[272,512]{1,0:T(8,128)(2,1)S(1)} %collective-permute-done.5.refs_7_), channel_id=1, source_target_pairs={{0,2},{2,4},{4,6},{6,8},{8,10},{10,12},{12,14},{14,0},{16,18},{18,... | collective-permute-start | bytes 835592 | tf_op jit(solution)/shard_map/ppermute | solution.py:325
  37.7 18.5 %collective-permute-start.3 = (bf16[272,512]{1,0:T(8,128)(2,1)S(1)}, bf16[272,512]{1,0:T(8,128)(2,1)S(1)}, u32[]{:S(2)}, u32[]{:S(2)}) collective-permute-start(bf16[272,512]{1,0:T(8,128)(2,1)S(1)} %collective-permute-done.2.refs_4_), channel_id=1, source_target_pairs={{2,0},{4,2},{6,4},{8,6},{10,8},{12,10},{14,12},{0,14},{18,16},{20,... | collective-permute-start | bytes 835592 | tf_op jit(solution)/shard_map/ppermute | solution.py:326
  56.2 1.0 copy-start.1
  98.2 26.2 %all-to-all-start.2 = ((bf16[8,128,512]{2,1,0:T(8,128)(2,1)}), bf16[8,128,512]{2,1,0:T(8,128)(2,1)S(1)}, u32[]{:S(2)}, u32[]{:S(2)}) async-start(bf16[8,128,512]{2,1,0:T(8,128)(2,1)} %get-tuple-element.17), calls=%async_computation.2 | async-start | bytes 2097152 | tf_op jit(solution)/shard_map/all_to_all | solution.py:364
  101.8 0.7 collective-permute-start.8
  102.5 0.7 copy-start.7
  124.4 1.0 copy-start.6

commit v3 on v2

v3 whole, which is shorter than its diff:
```python
import math

import jax
import jax.numpy as jnp
from jax import lax
from jax.experimental import pallas as pl
from jax.experimental.pallas import tpu as pltpu
from jax.sharding import PartitionSpec as P

HD = 128
REACH = 4
TOK = 128
BARS_HERE = 8
HEADS_HERE = 4
FEAT = HD * HEADS_HERE
META = 16
ROWS = 2 * TOK + META
NZ = 8
NY = 4
NX = 4
NXY = NY * NX
N_SEQ = NZ * NXY
OFFSETS = (1, 2, 4, 8, 12, 16, 24, 32)
SCALE = HD ** (-0.5)
LOG2E = math.log2(math.e)
EXP_SCALE = SCALE * LOG2E
LOWEST = -1e30

Z_GROUPS = [[j * NZ + z for z in range(NZ)] for j in range(NXY)]
XY_GROUPS = [[j * NZ + z for j in range(NXY)] for z in range(NZ)]


def route(dy, dx, dz):
    return [
        ((y * NX + x) * NZ + z, ((y + dy) % NY * NX + (x + dx) % NX) * NZ + (z + dz) % NZ)
        for y in range(NY)
        for x in range(NX)
        for z in range(NZ)
    ]


TO_NEXT = route(0, 0, 1)
TO_PREVIOUS = route(0, 0, -1)
ROW_UP = [(i, i + NZ) for i in range(N_SEQ - NZ) if i % NZ >= NZ - REACH]
ROW_DOWN = [(dst, src) for src, dst in ROW_UP]
EARLY = (0, 1, 7, 2, 6, 3, 5)
LATE = (4,)
ORDER = EARLY + LATE

VMEM_LIMIT = 50 * 2**20
SMEM = pltpu.SMEM
VMEM = pltpu.VMEM
HBM = pltpu.HBM
NT = (((1,), (1,)), ((), ()))
TN = (((0,), (0,)), ((), ()))
BF16 = jnp.bfloat16
F32 = jnp.float32


def whole(space):
    return pl.BlockSpec(memory_space=space)


def shape(dims, dtype=BF16):
    return jax.ShapeDtypeStruct(dims, dtype)


def pinned(*arrays):
    return [pltpu.with_memory_space_constraint(array, HBM) for array in arrays]


def local_bar(starts, positions):
    count = jnp.zeros_like(positions)
    for b in range(1, BARS_HERE):
        count = count + (positions >= starts[b]).astype(jnp.int32)
    return count


def low(flags):
    return flags.astype(F32).astype(BF16)


def pack_kernel(
    core, starts, related, slots, queries, keys, values, grad_own, out_weight,
    partial, query_pack, key_pack, sums, weight, grad, sems,
):
    half = grad_own.shape[1]
    copies = [pltpu.make_async_copy(grad_own, grad, sems.at[0])]
    cols = pl.ds(pl.multiple_of(core[0] * half, half), half)
    copies.append(pltpu.make_async_copy(out_weight.at[:, cols], weight, sems.at[1]))
    copies.append(pltpu.make_async_copy(queries, query_pack.at[pl.ds(0, TOK)], sems.at[3]))
    copies.append(pltpu.make_async_copy(keys, key_pack.at[pl.ds(0, TOK)], sems.at[4]))
    copies.append(pltpu.make_async_copy(values, key_pack.at[pl.ds(TOK, TOK)], sems.at[5]))
    for copy in copies:
        copy.start()
    base = starts[0]
    lane = lax.broadcasted_iota(jnp.int32, (META, TOK), 1)
    row = lax.broadcasted_iota(jnp.int32, (META, TOK), 0)
    bar = local_bar(starts, lane + base)
    info = jnp.where(row == 0, bar, 0)
    for j in range(len(OFFSETS)):
        entry = jnp.zeros((META, TOK), jnp.int32)
        for b in range(BARS_HERE):
            has = (related[b, j] >= 0).astype(jnp.int32)
            entry = jnp.where(bar == b, has, entry)
        info = jnp.where(row == j + 1, entry, info)
    query_pack[TOK:, :] = jnp.zeros((TOK + META, FEAT), BF16)
    query_pack[2 * TOK :, 0:TOK] = low(info)
    key_pack[2 * TOK :, :] = jnp.zeros((META, FEAT), BF16)
    key_pack[2 * TOK :, 0:TOK] = low(bar)
    slot = jnp.full((META, TOK), -1, jnp.int32)
    for b in range(BARS_HERE):
        slot = jnp.where(row == b, slots[b] - base, slot)
    pick = low(lane == slot)
    for copy in copies[2:]:
        copy.wait()
    for kind in range(2):
        source = key_pack[kind * TOK : (kind + 1) * TOK, :]
        rows = jnp.dot(pick, source, preferred_element_type=F32)[0:BARS_HERE].astype(BF16)
        for h in range(HEADS_HERE):
            at = (2 * h + kind) * HD
            for j in range(NXY):
                sums[j, :, at : at + HD] = rows[:, h * HD : (h + 1) * HD]
    for copy in copies[:2]:
        copy.wait()
    partial[...] = lax.dot_general(weight[...], grad[...], NT, preferred_element_type=F32)


def grad_pack_kernel(core, pack, partial, grad_other, out_weight, packed, weight, sem):
    half = grad_other.shape[1]
    cols = pl.ds(pl.multiple_of((1 - core[0]) * half, half), half)
    copy = pltpu.make_async_copy(out_weight.at[:, cols], weight, sem)
    copy.start()
    packed[0:TOK, :] = pack[0:TOK, :]
    packed[2 * TOK :, :] = pack[2 * TOK :, :]
    copy.wait()
    turned = partial[...] + lax.dot_general(
        weight[...], grad_other[...], NT, preferred_element_type=F32
    )
    for h in range(HEADS_HERE):
        cols = slice(h * HD, (h + 1) * HD)
        packed[TOK : 2 * TOK, cols] = jnp.transpose(turned[cols]).astype(BF16)


def place():
    rank = lax.axis_index("seq")
    return rank, jnp.bitwise_and(rank, NZ - 1)


def load_keys(own, previous, sums, pairs, keys, sems):
    copies = [
        pltpu.make_async_copy(own, pairs.at[0], sems.at[0]),
        pltpu.make_async_copy(previous, pairs.at[1], sems.at[1]),
        pltpu.make_async_copy(sums, keys, sems.at[2]),
    ]
    for copy in copies:
        copy.start()
    return copies


class Bias:
    def __init__(self, packed, pairs):
        rank, self.z = place()
        self.row_start = rank - self.z
        self.packed = packed
        self.local = [
            jnp.transpose(
                jnp.broadcast_to(pairs[i, 2 * TOK :, 0:TOK].astype(F32)[0:1], (TOK, TOK))
            ).astype(jnp.int32)
            for i in range(2)
        ]
        self.key_row = lax.broadcasted_iota(jnp.int32, (TOK, TOK), 0)
        self.token_col = lax.broadcasted_iota(jnp.int32, (TOK, TOK), 1)
        owner = lax.shift_right_logical(self.key_row, 3) * NZ + self.z
        self.summary_bar = owner * BARS_HERE + jnp.bitwise_and(self.key_row, BARS_HERE - 1)

    def build(self, o, bias):
        owner = self.row_start + jnp.bitwise_and(self.z + o, NZ - 1)
        info = self.packed[o, 2 * TOK :, 0:TOK].astype(F32).astype(jnp.int32)
        token_bar = info[0:1] + owner * BARS_HERE
        rel = [
            jnp.where(info[j + 1 : j + 2] > 0, token_bar - OFFSETS[j], -1)
            for j in range(len(OFFSETS))
        ]
        if o <= REACH:
            key_owner = owner - o
            key_local = jnp.where(self.z + o >= NZ, self.local[1], self.local[0])
            key_bar = jnp.where(key_owner >= 0, key_local + key_owner * BARS_HERE, -2)
            seen = key_bar == rel[0]
            for entry in rel[1:]:
                seen = seen | (key_bar == entry)
            if o == 0:
                seen = seen | ((key_bar == token_bar) & (self.key_row <= self.token_col))
            bias[o] = jnp.where(seen, 0.0, -jnp.inf)
        hidden = self.summary_bar >= token_bar
        for entry in rel:
            hidden = hidden | (self.summary_bar == entry)
        bias[REACH + 1 + o] = jnp.where(hidden, -jnp.inf, 0.0)


def bias_blocks(order):
    return [o for o in order if o <= REACH] + [REACH + 1 + o for o in order]


def products(packed, pairs, keys, bias, h, o):
    _, z = place()
    cols = slice(h * HD, (h + 1) * HD)
    at = 2 * h * HD
    query = packed[o, 0:TOK, cols]
    grad = packed[o, TOK : 2 * TOK, cols]
    key, value = keys[:, at : at + HD], keys[:, at + HD : at + 2 * HD]
    mask = bias[REACH + 1 + o]
    if o <= REACH:
        side = lax.shift_right_logical(z + o, 3)
        key = jnp.concatenate([pairs[side, 0:TOK, cols], key], axis=0)
        value = jnp.concatenate([pairs[side, TOK : 2 * TOK, cols], value], axis=0)
        mask = jnp.concatenate([bias[o], mask], axis=0)
    scores = lax.dot_general(key, query, NT, preferred_element_type=F32)
    dprobs = lax.dot_general(value, grad, NT, preferred_element_type=F32)
    return key, scores, dprobs, mask


def stats_kernel(order, *refs):
    chunks, (own, previous, sums), refs = refs[: len(order)], refs[len(order) : len(order) + 3], refs[len(order) + 3 :]
    earlier, refs = (refs[0], refs[1:]) if len(order) < REACH else (None, refs)
    stats, bias_out, packed, pairs, keys, bias, key_sems, chunk_sems, bias_sems = refs
    key_copies = load_keys(own, previous, sums, pairs, keys, key_sems)
    copies = [
        pltpu.make_async_copy(chunk, packed.at[o], chunk_sems.at[o])
        for o, chunk in zip(order, chunks)
    ]
    for copy in copies:
        copy.start()
    for copy in key_copies:
        copy.wait()
    masks = Bias(packed, pairs)
    writes = []
    for i, o in enumerate(order):
        copies[i].wait()
        masks.build(o, bias)
        for block in bias_blocks((o,)):
            place_out = bias_out.at[bias_blocks(order).index(block)]
            writes.append(pltpu.make_async_copy(bias.at[block], place_out, bias_sems.at[block]))
            writes[-1].start()
        chunk = jnp.bitwise_and(masks.z + o, NZ - 1)
        log_sums, means = [], []
        made = [products(packed, pairs, keys, bias, h, o) for h in range(HEADS_HERE)]
        for _, scores, dprobs, mask in made:
            scores = scores + mask
            top = jnp.maximum(jnp.max(scores, axis=0, keepdims=True), LOWEST)
            weights = jnp.exp2((scores - top) * EXP_SCALE)
            total = jnp.sum(weights, axis=0, keepdims=True)
            weighted = jnp.sum(weights * dprobs, axis=0, keepdims=True)
            log_sums.append(top * EXP_SCALE + jnp.log(total) * LOG2E)
            means.append(jnp.where(total > 0.0, weighted / total, 0.0))
        merged = jnp.concatenate(log_sums + means, axis=0)
        if earlier is None:
            stats[chunk] = merged
            continue
        for peer in range(NZ):
            stats[peer] = earlier[...]
            stats[peer, chunk] = merged
    for copy in writes:
        copy.wait()


def merge_stats(stats, merged):
    top = stats[0, :, 0:HEADS_HERE, :]
    for i in range(1, NZ):
        top = jnp.maximum(top, stats[i, :, 0:HEADS_HERE, :])
    total = jnp.zeros_like(top)
    mean = jnp.zeros_like(top)
    for i in range(NZ):
        weight = jnp.exp2(stats[i, :, 0:HEADS_HERE, :] - top)
        total = total + weight
        mean = mean + weight * stats[i, :, HEADS_HERE:, :]
    merged[:, 0:HEADS_HERE, :] = top + jnp.log(total) * LOG2E
    merged[:, HEADS_HERE:, :] = mean / total


def query_grad_kernel(*refs):
    order = ORDER
    near = [o for o in order if o <= REACH]
    chunks, refs = refs[:NZ], refs[NZ:]
    own, previous, sums, bias_most, bias_last, stats_in, *refs = refs
    query_grads, (coarse_out, window_out, previous_grad), refs = refs[:NZ], refs[NZ : NZ + 3], refs[NZ + 3 :]
    packed, pairs, keys, bias, stats, merged, coarse, window, *refs = refs
    key_sems, chunk_sems, bias_sems, stats_sem, out_sems = refs
    stats_copy = pltpu.make_async_copy(stats_in, stats, stats_sem)
    stats_copy.start()
    key_copies = load_keys(own, previous, sums, pairs, keys, key_sems)
    copies = []
    for i, o in enumerate(order):
        mine = [pltpu.make_async_copy(chunks[o], packed.at[o], chunk_sems.at[o])]
        for block in bias_blocks((o,)):
            source, among = (bias_most, EARLY) if o in EARLY else (bias_last, LATE)
            source = source.at[bias_blocks(among).index(block)]
            mine.append(pltpu.make_async_copy(source, bias.at[block], bias_sems.at[block]))
        for copy in mine:
            copy.start()
        copies.append(mine)
    stats_copy.wait()
    merge_stats(stats, merged)
    for copy in key_copies:
        copy.wait()
    _, z = place()
    keys_turned = [
        jnp.transpose(keys[:, 2 * h * HD : (2 * h + 1) * HD]) for h in range(HEADS_HERE)
    ]
    pairs_turned = [
        [jnp.transpose(pairs[i, 0:TOK, h * HD : (h + 1) * HD]) for i in range(2)]
        for h in range(HEADS_HERE)
    ]
    writes = []
    others = [[None, None] for _ in range(HEADS_HERE)]
    for i, o in enumerate(order):
        for copy in copies[i]:
            copy.wait()
        chunk = jnp.bitwise_and(z + o, NZ - 1)
        made = [products(packed, pairs, keys, bias, h, o) for h in range(HEADS_HERE)]
        low_parts = []
        for h, (_, scores, dprobs, mask) in enumerate(made):
            log_sum = merged[chunk, h : h + 1, :]
            delta = merged[chunk, HEADS_HERE + h : HEADS_HERE + h + 1, :]
            probs = jnp.exp2(scores * EXP_SCALE - log_sum + mask)
            low_parts.append(((probs * (dprobs - delta)).astype(BF16), probs.astype(BF16)))
        for h, (dscores, probs_low) in enumerate(low_parts):
            turned = keys_turned[h]
            if o <= REACH:
                side = pairs_turned[h][0]
                if o > 0:
                    side = jnp.where(z + o >= NZ, pairs_turned[h][1], side)
                turned = jnp.concatenate([side, turned], axis=1)
            dquery = jnp.dot(turned, dscores, preferred_element_type=F32)
            query_grads[o][h * HD : (h + 1) * HD, :] = (SCALE * dquery).astype(BF16)
        for h, (dscores, probs_low) in enumerate(low_parts):
            if o <= REACH:
                window[near.index(o), 0, h] = dscores[0:TOK]
                window[near.index(o), 1, h] = probs_low[0:TOK]
            if 0 < o <= REACH:
                wraps = (z + o >= NZ).astype(F32)
                cols = slice(h * HD, (h + 1) * HD)
                for kind, left in enumerate((dscores, probs_low)):
                    right = packed[o, kind * TOK : (kind + 1) * TOK, cols]
                    part = wraps * jnp.dot(left[0:TOK], right, preferred_element_type=F32)
                    old = others[h][kind]
                    others[h][kind] = part if old is None else old + part
            coarse[i, 0, h] = dscores[-TOK:]
            coarse[i, 1, h] = probs_low[-TOK:]
        writes.append(pltpu.make_async_copy(coarse.at[i], coarse_out.at[i], out_sems.at[0, o]))
        writes[-1].start()
        if o <= REACH:
            at = near.index(o)
            writes.append(
                pltpu.make_async_copy(window.at[at], window_out.at[at], out_sems.at[1, o])
            )
            writes[-1].start()
    for h in range(HEADS_HERE):
        cols = slice(h * HD, (h + 1) * HD)
        previous_grad[0:TOK, cols] = (others[h][0] * SCALE).astype(BF16)
        previous_grad[TOK : 2 * TOK, cols] = others[h][1].astype(BF16)
    for copy in writes:
        copy.wait()


def key_grad_kernel(*refs):
    order = ORDER
    near = [o for o in order if o <= REACH]
    chunks, (coarse_in, window_in), refs = refs[:NZ], refs[NZ : NZ + 2], refs[NZ + 2 :]
    own_grad, *sum_grads = refs[: 1 + NY]
    packed, coarse, window, sum_grad, sems = refs[1 + NY :]
    copies = [pltpu.make_async_copy(chunks[i], packed.at[i], sems.at[i]) for i in range(NZ)]
    copies.append(pltpu.make_async_copy(coarse_in, coarse, sems.at[NZ]))
    copies.append(pltpu.make_async_copy(window_in, window, sems.at[NZ + 1]))
    for copy in copies:
        copy.start()
    for copy in copies:
        copy.wait()
    _, z = place()
    for h in range(HEADS_HERE):
        cols = slice(h * HD, (h + 1) * HD)
        for kind in range(2):
            tokens = [packed[i, kind * TOK : (kind + 1) * TOK, cols] for i in range(NZ)]
            scale = SCALE if kind == 0 else 1.0
            at = (2 * h + kind) * HD
            rows = slice(kind * TOK, (kind + 1) * TOK)
            total = jnp.dot(
                jnp.concatenate([coarse[i, kind, h] for i in range(NZ)], axis=1),
                jnp.concatenate(tokens, axis=0),
                preferred_element_type=F32,
            )
            total = total * scale
            for j in range(NXY):
                part = total[j * BARS_HERE : (j + 1) * BARS_HERE]
                sum_grad[j, :, at : at + HD] = part
            mine = jnp.zeros((TOK, HD), F32)
            for i, o in enumerate(near):
                part = jnp.dot(
                    window[i, kind, h], tokens[order.index(o)], preferred_element_type=F32
                )
                mine = mine + part * (z + o < NZ).astype(F32)
            own_grad[rows, cols] = mine * scale
    rank, _ = place()
    y = lax.shift_right_logical(rank, 5)
    x = lax.shift_right_logical(rank, 3)
    for i in range(NY):
        for k in range(NX):
            j = jnp.bitwise_and(y - i, NY - 1) * NX + jnp.bitwise_and(x - k, NX - 1)
            rows = slice(k * BARS_HERE, (k + 1) * BARS_HERE)
            sum_grads[i][rows, :] = sum_grad[j].astype(BF16)


def finish_kernel(
    starts, slots, own_grad, arrived, part0, part1, part2, part3, here, from_before, from_after,
    grad_queries, grad_keys, grad_values
):
    base = starts[0]
    total = part0[0:BARS_HERE, :].astype(F32)
    for part in (part1, part2, part3):
        total = total + part[...].astype(F32)
    row = lax.broadcasted_iota(jnp.int32, (TOK, HD), 0)
    for h in range(HEADS_HERE):
        cols = slice(h * HD, (h + 1) * HD)
        for kind, out in ((0, grad_keys), (1, grad_values)):
            rows = slice(kind * TOK, (kind + 1) * TOK)
            at = (2 * h + kind) * HD
            grad = own_grad[rows, cols] + arrived[rows, cols].astype(F32)
            for b in range(BARS_HERE):
                grad = grad + jnp.where(row == slots[b] - base, total[b : b + 1, at : at + HD], 0.0)
            out[:, cols] = grad.astype(BF16)
    for h in range(HEADS_HERE):
        rows = slice(h * HD, (h + 1) * HD)
        total = here[rows, :].astype(F32) + from_before[rows, :].astype(F32)
        total = total + from_after[rows, :].astype(F32)
        grad_queries[:, rows] = jnp.transpose(total).astype(BF16)


def add_low(*parts):
    total = parts[0].astype(F32)
    for part in parts[1:]:
        total = total + part.astype(F32)
    return total.astype(BF16)


def shards(queries, keys, values, grad_y, out_weight, bar_start, related, bar_summary_token):
    params = pltpu.CompilerParams(vmem_limit_bytes=VMEM_LIMIT)
    dma = pltpu.SemaphoreType.DMA
    grad_other = lax.ppermute(grad_y, "head", [(0, 1), (1, 0)])
    half = grad_y.shape[1]
    core = jnp.reshape(lax.axis_index("head"), (1,))
    partial, query_pack, own, sums = pl.pallas_call(
        pack_kernel,
        out_shape=(
            shape((FEAT, TOK), F32),
            shape((ROWS, FEAT)),
            shape((ROWS, FEAT)),
            shape((NXY, BARS_HERE, 2 * FEAT)),
        ),
        in_specs=[whole(SMEM)] * 4 + [whole(HBM)] * 5,
        out_specs=(whole(VMEM),) * 4,
        scratch_shapes=[VMEM((FEAT, half), BF16), VMEM(grad_y.shape, BF16), dma((6,))],
        compiler_params=params,
    )(
        core,
        *pinned(bar_start, related, bar_summary_token),
        *pinned(queries, keys, values, grad_y, out_weight),
    )
    packed = pl.pallas_call(
        grad_pack_kernel,
        out_shape=shape((ROWS, FEAT)),
        in_specs=[whole(SMEM)] + [whole(VMEM)] * 3 + [whole(HBM)],
        out_specs=whole(VMEM),
        scratch_shapes=[VMEM((FEAT, half), BF16), dma],
        compiler_params=params,
    )(
        core,
        *[pltpu.with_memory_space_constraint(x, VMEM) for x in (query_pack, partial)],
        grad_other,
        *pinned(out_weight),
    )

    after, before = [packed], [packed]

    def ring_step():
        after.append(lax.ppermute(after[-1], "seq", TO_PREVIOUS))
        before.append(lax.ppermute(before[-1], "seq", TO_NEXT))

    ring_step()
    all_sums = lax.all_to_all(sums, "seq", 0, 0, axis_index_groups=XY_GROUPS)
    after[1], before[1], all_sums = lax.optimization_barrier((after[1], before[1], all_sums))
    all_sums = all_sums.reshape(NXY * BARS_HERE, 2 * FEAT)
    ring_step()
    previous = lax.ppermute(own, "seq", ROW_UP)
    after[2], before[2], previous = lax.optimization_barrier((after[2], before[2], previous))
    ring_step()
    after.append(lax.ppermute(after[-1], "seq", TO_PREVIOUS))
    chunks = after + before[:0:-1]

    bars = NXY * BARS_HERE
    bias_shape = (REACH + 1 + NZ, TOK, TOK)
    stats_shape = (NZ, NZ, 2 * HEADS_HERE, TOK)
    held = [
        VMEM((NZ, ROWS, FEAT), BF16),
        VMEM((2, ROWS, FEAT), BF16),
        VMEM((bars, 2 * FEAT), BF16),
        VMEM(bias_shape, F32),
    ]
    def stats_of(order, *earlier):
        out = (shape(stats_shape, F32),) if earlier else (shape(stats_shape[1:], F32),)
        blocks = (len(bias_blocks(order)),) + bias_shape[1:]
        return pl.pallas_call(
            lambda *refs: stats_kernel(order, *refs),
            out_shape=out + (shape(blocks, F32),),
            in_specs=[whole(HBM)] * (len(order) + 3) + [whole(VMEM)] * len(earlier),
            out_specs=(whole(VMEM), whole(HBM)),
            scratch_shapes=held + [dma((3,)), dma((NZ,)), dma(bias_shape[:1])],
            compiler_params=params,
        )(*[chunks[o] for o in order], own, previous, all_sums, *earlier)

    partial_stats, bias_most = stats_of(EARLY)
    stats, bias_last = stats_of(LATE, partial_stats)

    stats = lax.all_to_all(stats, "seq", 0, 0, axis_index_groups=Z_GROUPS)

    coarse_shape = (NZ, 2, HEADS_HERE, bars, TOK)
    window_shape = (REACH + 1, 2, HEADS_HERE, TOK, TOK)
    *grads, coarse, window, previous_grad = pl.pallas_call(
        query_grad_kernel,
        out_shape=(shape((FEAT, TOK)),) * NZ
        + (shape(coarse_shape), shape(window_shape), shape((2 * TOK, FEAT))),
        in_specs=[whole(HBM)] * (NZ + 6),
        out_specs=(whole(VMEM),) * NZ + (whole(HBM),) * 2 + (whole(VMEM),),
        scratch_shapes=held
        + [
            VMEM(stats_shape, F32),
            VMEM(stats_shape[1:], F32),
            VMEM(coarse_shape, BF16),
            VMEM(window_shape, BF16),
            dma((3,)),
            dma((NZ,)),
            dma(bias_shape[:1]),
            dma,
            dma((2, NZ)),
        ],
        compiler_params=params,
    )(*chunks, own, previous, all_sums, bias_most, bias_last, stats)

    def forward_step(array):
        return lax.ppermute(array, "seq", TO_NEXT)

    def backward_step(array):
        return lax.ppermute(array, "seq", TO_PREVIOUS)

    forward, backward = forward_step(grads[4]), backward_step(grads[5])
    arrived = lax.ppermute(previous_grad, "seq", ROW_DOWN)
    own_grad, *sum_grads = pl.pallas_call(
        key_grad_kernel,
        out_shape=(shape((2 * TOK, FEAT), F32),) + (shape((NX * BARS_HERE, 2 * FEAT)),) * NY,
        in_specs=[whole(HBM)] * (NZ + 2),
        out_specs=(whole(VMEM),) * (1 + NY),
        scratch_shapes=[
            VMEM((NZ, ROWS, FEAT), BF16),
            VMEM(coarse_shape, BF16),
            VMEM(window_shape, BF16),
            VMEM((NXY, BARS_HERE, 2 * FEAT), F32),
            dma((NZ + 2,)),
        ],
        compiler_params=params,
    )(*[chunks[o] for o in ORDER], coarse, window)

    move = lambda array, *by: lax.ppermute(array, "seq", route(*by))
    forward, backward = forward_step(add_low(forward, grads[3])), backward_step(add_low(backward, grads[6]))
    moved = [move(sum_grads[i], -i, 0, 0) for i in range(1, NY)]
    forward, backward, *moved = lax.optimization_barrier((forward, backward, *moved))
    forward, backward = forward_step(add_low(forward, grads[2])), backward_step(add_low(backward, grads[7]))
    row_grad = add_low(sum_grads[0], *moved)
    parts = [
        move(row_grad[k * BARS_HERE : (k + 1) * BARS_HERE], 0, -k, 0) for k in range(1, NX)
    ]
    forward, backward, *parts = lax.optimization_barrier((forward, backward, *parts))
    forward = forward_step(add_low(forward, grads[1]))

    grad_queries, grad_keys, grad_values = pl.pallas_call(
        finish_kernel,
        out_shape=(shape((TOK, FEAT)),) * 3,
        in_specs=[whole(SMEM)] * 2 + [whole(VMEM)] * 9,
        out_specs=(whole(VMEM),) * 3,
    )(
        *pinned(bar_start, bar_summary_token),
        own_grad,
        arrived,
        row_grad,
        *parts,
        grads[0],
        forward,
        backward,
    )
    return grad_queries, grad_keys, grad_values


def solution(mesh):
    in_specs = (
        P("seq", "head"),
        P("seq", "head"),
        P("seq", "head"),
        P("seq", "head"),
        P("head", None),
        P("seq"),
        P("seq", None),
        P("seq"),
    )
    out_specs = (P("seq", "head"), P("seq", "head"), P("seq", "head"))
    return jax.shard_map(shards, mesh=mesh, in_specs=in_specs, out_specs=out_specs, check_vma=False)
```

time: 128 us -> 116 us (0.906)
  blocking collectives: 42.7 us -> 14.4 us
  starting transfers between devices: 22 us -> 35.8 us
  waiting for transfers between devices: 32.1 us -> 39.3 us
  local copies, waits for them, and re-layouts: 6.48 us -> 0.65 us
    ppermute x3 -> x20, waiting for transfers between devices: 0.01 us -> 31.7 us  [the longest x3 11 us: ring_step(): after.append(lax.ppermute(after[-1], 'seq', TO_PREVIOUS))]
    all_to_all x2 -> x0, blocking collectives: 26.8 us -> none  [the longest x1 14.8 us: shards(): lax.all_to_all(sums, 'seq', 0, 0, axis_index_groups=XY_GROUPS)]
    ppermute x3 -> x20, starting transfers between devices: 0.09 us -> 26.4 us  [the longest x3 9.66 us: backward_step(): return lax.ppermute(array, 'seq', TO_PREVIOUS)]
    ppermute x4 -> x1, starting transfers between devices: 17 us -> 0.56 us  [shards(): after.append(lax.ppermute(after[-1], 'seq', TO_PREVIOUS))]
    ppermute x4 -> x1, waiting for transfers between devices: 13.4 us -> 0.61 us  [shards(): after.append(lax.ppermute(after[-1], 'seq', TO_PREVIOUS))]
    all_to_all x1, waiting for transfers between devices: 18.7 us -> 7.01 us  [shards(): all_sums = lax.all_to_all(sums, 'seq', 0, 0, axis_index_groups=XY_GROUPS)]
    unnamed x16 -> x28, local copies, waits for them, and re-layouts: 6.48 us -> 0.64 us
    all_to_all x1, starting transfers between devices: 3.56 us -> 7.48 us  [shards(): all_sums = lax.all_to_all(sums, 'seq', 0, 0, axis_index_groups=XY_GROUPS)]
  transfers between devices with their start and end apart: 10 -> 24, of which waited for: 4 -> 13; matrix products, arithmetic and copies ran while one was open for 0% -> 0% of each run, Pallas kernels for 3% -> 10%
where the time goes in v3:
time: 116 us; the launch traced here: 115 us
  waiting for transfers between devices  39.3 us (34%)
  starting transfers between devices  35.8 us (31%)
  Pallas kernels  23.8 us (21%)
  blocking collectives  14.4 us (12%)
    all_to_all x1, blocking collectives, shards(): stats = lax.all_to_all(stats, 'seq', 0, 0, axis_index_groups=Z_GROUPS)  14.4 us
    ppermute x3, waiting for transfers between devices, ring_step(): after.append(lax.ppermute(after[-1], 'seq', TO_PREVIOUS))  11 us
    ppermute x4, waiting for transfers between devices, forward_step(): return lax.ppermute(array, 'seq', TO_NEXT)  9.86 us
    ppermute x3, starting transfers between devices, backward_step(): return lax.ppermute(array, 'seq', TO_PREVIOUS)  9.66 us
    ppermute x6, waiting for transfers between devices, shards(): move = lambda array, *by: lax.ppermute(array, 'seq', route(*by))  8.48 us
    all_to_all x1, starting transfers between devices, shards(): all_sums = lax.all_to_all(sums, 'seq', 0, 0, axis_index_groups=XY_GROUPS)  7.48 us
    all_to_all x1, waiting for transfers between devices, shards(): all_sums = lax.all_to_all(sums, 'seq', 0, 0, axis_index_groups=XY_GROUPS)  7.01 us
    pallas_call x2, Pallas kernels, stats_of(): pl.pallas_call(lambda *refs: stats_kernel(order, *refs), out_shape=out +...  6.59 us
  transfers between devices with their start and end apart: 24, of which 13 were waited for; matrix products, arithmetic and copies ran while one was open for 0% of the time, Pallas kernels for 10%

profile of v3, /device:TPU:2, one launch (start us, length us, event | category | flops | bytes accessed | tf_op | source)
XLA Modules:
  0.0 115.1 jit_solution(3315005881747944800)
XLA Ops:
  0.6 0.1 collective-permute-start
  0.7 3.0 %shard_map.103 = (f32[512,128]{1,0:T(8,128)S(1)}, bf16[272,512]{1,0:T(8,128)(2,1)S(1)}, bf16[272,512]{1,0:T(8,128)(2,1)S(1)}, bf16[16,8,1024]{2,1,0:T(8,128)(2,1)}) custom-call(s32[1]{0:T(128)} %bitcast.core, s32[8]{0:T(128)} %starts.3, s32[8,8]{1,0:T(8,128)} %related.1, s32[8]{0:T(128)} %slots.3, bf16[128,512]{1,0:T(8,128)(2,1)} %queries.1, ...), custom_call_target="tpu_custom_call" | custom-call | tf_op jit(solution)/shard_map/pallas_call | solution.py:451
  3.8 0.0 copy-start.2
  3.8 0.0 collective-permute-done.grad_other
  3.8 1.8 %shard_map.104.refs_0_ = bf16[272,512]{1,0:T(8,128)(2,1)S(1)} custom-call(s32[1]{0:T(128)} %bitcast.core, bf16[272,512]{1,0:T(8,128)(2,1)S(1)} %get-tuple-element.43.pack, f32[512,128]{1,0:T(8,128)S(1)} %get-tuple-element.44.partial, bf16[128,1024]{1,0:T(8,128)(2,1)S(1)} %collective-permute-done.grad_other, bf16[512,2048]{1,0:T(8,128)(2,1)} %out_weight.3), custom_call_target="tpu_custom_call" | custom-call | tf_op jit(solution)/shard_map/pallas_call | solution.py:468
  5.7 2.0 %collective-permute-start.2 = (bf16[272,512]{1,0:T(8,128)(2,1)S(1)}, bf16[272,512]{1,0:T(8,128)(2,1)S(1)}, u32[]{:S(2)}, u32[]{:S(2)}) collective-permute-start(bf16[272,512]{1,0:T(8,128)(2,1)S(1)} %shard_map.104.refs_0_), channel_id=1, source_target_pairs={{0,2},{2,4},{4,6},{6,8},{8,10},{10,12},{12,14},{14,0},{16,18},{18,... | collective-permute-start | bytes 835592 | tf_op jit(solution)/shard_map/ppermute | solution.py:486
  7.7 4.0 %collective-permute-start.1 = (bf16[272,512]{1,0:T(8,128)(2,1)S(1)}, bf16[272,512]{1,0:T(8,128)(2,1)S(1)}, u32[]{:S(2)}, u32[]{:S(2)}) collective-permute-start(bf16[272,512]{1,0:T(8,128)(2,1)S(1)} %shard_map.104.refs_0_), channel_id=1, source_target_pairs={{0,14},{2,0},{4,2},{6,4},{8,6},{10,8},{12,10},{14,12},{16,30},{18,... | collective-permute-start | bytes 835592 | tf_op jit(solution)/shard_map/ppermute | solution.py:485
  11.7 7.5 %all-to-all-start = ((bf16[16,8,1024]{2,1,0:T(8,128)(2,1)}), bf16[16,8,1024]{2,1,0:T(8,128)(2,1)S(1)}, u32[]{:S(2)}, u32[]{:S(2)}) async-start(bf16[16,8,1024]{2,1,0:T(8,128)(2,1)} %get-tuple-element.45), calls=%async_computation | async-start | bytes 524288 | tf_op jit(solution)/shard_map/all_to_all | solution.py:489
  19.2 0.7 collective-permute-start.5
  19.8 7.0 %all-to-all-done = bf16[16,8,1024]{2,1,0:T(8,128)(2,1)S(1)} async-done(((bf16[16,8,1024]{2,1,0:T(8,128)(2,1)}), bf16[16,8,1024]{2,1,0:T(8,128)(2,1)S(1)}, u32[]{:S(2)}, u32[]{:S(2)}) %all-to-all-start) | async-done | bytes 262176 | tf_op jit(solution)/shard_map/all_to_all | solution.py:489
  26.9 0.0 collective-permute-done.2.refs_2_.refs_7_
  26.9 0.0 collective-permute-done.1.refs_1_
  26.9 1.7 %collective-permute-start.3 = (bf16[272,512]{1,0:T(8,128)(2,1)S(1)}, bf16[272,512]{1,0:T(8,128)(2,1)S(1)}, u32[]{:S(2)}, u32[]{:S(2)}) collective-permute-start(bf16[272,512]{1,0:T(8,128)(2,1)S(1)} %collective-permute-done.1.refs_1_), channel_id=1, source_target_pairs={{0,14},{2,0},{4,2},{6,4},{8,6},{10,8},{12,10},{14,12},{16,30},{18,... | collective-permute-start | bytes 835592 | tf_op jit(solution)/shard_map/ppermute | solution.py:485
  28.6 0.4 collective-permute-start.4
  29.0 0.0 collective-permute-done.5.refs_8_.refs_2_.refs_9_
  29.0 5.5 %collective-permute-done.3.refs_3_.refs_2_ = bf16[272,512]{1,0:T(8,128)(2,1)S(1)} collective-permute-done((bf16[272,512]{1,0:T(8,128)(2,1)S(1)}, bf16[272,512]{1,0:T(8,128)(2,1)S(1)}, u32[]{:S(2)}, u32[]{:S(2)}) %collective-permute-start.3) | collective-permute-done | bytes 278560 | tf_op jit(solution)/shard_map/ppermute | solution.py:485
  34.5 2.3 %collective-permute-done.4.refs_4_.refs_6_ = bf16[272,512]{1,0:T(8,128)(2,1)S(1)} collective-permute-done((bf16[272,512]{1,0:T(8,128)(2,1)S(1)}, bf16[272,512]{1,0:T(8,128)(2,1)S(1)}, u32[]{:S(2)}, u32[]{:S(2)}) %collective-permute-start.4) | collective-permute-done | bytes 278560 | tf_op jit(solution)/shard_map/ppermute | solution.py:486
  36.8 0.3 collective-permute-start.6
  37.1 1.7 %collective-permute-start.7 = (bf16[272,512]{1,0:T(8,128)(2,1)S(1)}, bf16[272,512]{1,0:T(8,128)(2,1)S(1)}, u32[]{:S(2)}, u32[]{:S(2)}) collective-permute-start(bf16[272,512]{1,0:T(8,128)(2,1)S(1)} %collective-permute-done.4.refs_4_.refs_6_), channel_id=1, source_target_pairs={{0,2},{2,4},{4,6},{6,8},{8,10},{10,12},{12,14},{14,0},{16,18},{18,... | collective-permute-start | bytes 835592 | tf_op jit(solution)/shard_map/ppermute | solution.py:486
  38.9 5.5 %collective-permute-done.6.refs_5_.refs_3_ = bf16[272,512]{1,0:T(8,128)(2,1)S(1)} collective-permute-done((bf16[272,512]{1,0:T(8,128)(2,1)S(1)}, bf16[272,512]{1,0:T(8,128)(2,1)S(1)}, u32[]{:S(2)}, u32[]{:S(2)}) %collective-permute-start.6) | collective-permute-done | bytes 278560 | tf_op jit(solution)/shard_map/ppermute | solution.py:485
  44.3 0.6 collective-permute-start.8
  44.9 0.0 collective-permute-done.7.refs_6_.refs_5_
  44.9 5.4 %shard_map.105 = (f32[8,8,128]{2,1,0:T(8,128)S(1)}, f32[11,128,128]{2,1,0:T(8,128)S(1)}) custom-call(bf16[272,512]{1,0:T(8,128)(2,1)S(1)} %shard_map.104.refs_0_, bf16[272,512]{1,0:T(8,128)(2,1)S(1)} %collective-permute-done.1.refs_1_, bf16[272,512]{1,0:T(8,128)(2,1)S(1)} %collective-permute-done.2.refs_2_.refs_7_, ...), custom_call_target="tpu_custom_call" | custom-call | tf_op jit(solution)/shard_map/pallas_call | solution.py:511
  50.3 0.0 copy-start.4
  50.3 0.6 collective-permute-done.8.refs_0_.refs_4_.refs_7_
  50.9 0.0 copy-done.2
  50.9 1.2 %shard_map.106 = (f32[8,8,8,128]{3,2,1,0:T(8,128)S(1)}, f32[2,128,128]{2,1,0:T(8,128)S(1)}) custom-call(bf16[272,512]{1,0:T(8,128)(2,1)S(1)} %collective-permute-done.8.refs_0_.refs_4_.refs_7_, bf16[272,512]{1,0:T(8,128)(2,1)S(1)} %get-tuple-element.48.refs_7_.refs_1_.refs_8_, bf16[272,512]{1,0:T(8,128)(2,1)S(1)} %collective-permute-done.5.refs_8_.refs_2_.refs_9_, ...), custom_call_target="tpu_custom_call" | custom-call | tf_op jit(solution)/shard_map/pallas_call | solution.py:511
  52.1 14.4 %all_to_all.10.refs_13_ = f32[8,8,8,128]{3,2,1,0:T(8,128)S(1)} all-to-all(f32[8,8,8,128]{3,2,1,0:T(8,128)S(1)} %get-tuple-element.56), channel_id=1, replica_groups={{0,2,4,6,8,10,12,14},{16,18,20,22,24,26,28,30},{32,34,36,38,40,42,44,46..., dimensions={0} | all-to-all | bytes 524288 | tf_op jit(solution)/shard_map/all_to_all | solution.py:523
  66.5 0.0 copy-start.1
  66.5 6.3 %shard_map.107 = (bf16[512,128]{1,0:T(8,128)(2,1)S(1)}, bf16[512,128]{1,0:T(8,128)(2,1)S(1)}, bf16[512,128]{1,0:T(8,128)(2,1)S(1)}, bf16[512,128]{1,0:T(8,128)(2...) custom-call(bf16[272,512]{1,0:T(8,128)(2,1)S(1)} %shard_map.104.refs, ...), custom_call_target="tpu_custom_call" | custom-call | tf_op jit(solution)/shard_map/pallas_call | solution.py:527
  72.8 0.2 collective-permute-start.10
  73.0 3.1 %collective-permute-start.12 = (bf16[512,128]{1,0:T(8,128)(2,1)S(1)}, bf16[512,128]{1,0:T(8,128)(2,1)S(1)}, u32[]{:S(2)}, u32[]{:S(2)}) collective-permute-start(bf16[512,128]{1,0:T(8,128)(2,1)S(1)} %get-tuple-element.64), channel_id=1, source_target_pairs={{0,14},{2,0},{4,2},{6,4},{8,6},{10,8},{12,10},{14,12},{16,30},{18,... | collective-permute-start | bytes 393224 | tf_op jit(solution)/shard_map/ppermute | solution.py:552
  76.1 3.7 %collective-permute-done.10 = bf16[512,128]{1,0:T(8,128)(2,1)S(1)} collective-permute-done((bf16[512,128]{1,0:T(8,128)(2,1)S(1)}, bf16[512,128]{1,0:T(8,128)(2,1)S(1)}, u32[]{:S(2)}, u32[]{:S(2)}) %collective-permute-start.10) | collective-permute-done | bytes 131104 | tf_op jit(solution)/shard_map/ppermute | solution.py:549
  79.9 0.1 collective-permute-start.11
  80.0 0.0 collective-permute-done.12
  80.0 3.3 %collective-permute-start.13 = (bf16[512,128]{1,0:T(8,128)(2,1)S(1)}, bf16[512,128]{1,0:T(8,128)(2,1)S(1)}, u32[]{:S(2)}, u32[]{:S(2)}) collective-permute-start(bf16[512,128]{1,0:T(8,128)(2,1)S(1)} %add_convert_fusion.3), channel_id=1, source_target_pairs={{0,14},{2,0},{4,2},{6,4},{8,6},{10,8},{12,10},{14,12},{16,30},{18,... | collective-permute-start | bytes 393224 | tf_op jit(solution)/shard_map/ppermute | solution.py:552
  83.3 3.4 %shard_map.108 = (f32[256,512]{1,0:T(8,128)S(1)}, bf16[32,1024]{1,0:T(8,128)(2,1)S(1)}, bf16[32,1024]{1,0:T(8,128)(2,1)S(1)}, bf16[32,1024]{1,0:T(8,128)(2,1)S(1)}, bf16[32,1024]{1,0:T(8,128)(2,1)S(1)}) custom-call(bf16[272,512]{1,0:T(8,128)(2,1)S(1)} %shard_map.104.refs_0_, bf16[272,512]{1,0:T(8,128)(2,1)S(1)} %collective-permute-done.1.refs_1_, ...), custom_call_target="tpu_custom_call" | custom-call | tf_op jit(solution)/shard_map/pallas_call | solution.py:556
  86.7 1.2 %collective-permute-start.14 = (bf16[32,1024]{1,0:T(8,128)(2,1)S(1)}, bf16[32,1024]{1,0:T(8,128)(2,1)S(1)}, u32[]{:S(2)}, u32[]{:S(2)}) collective-permute-start(bf16[32,1024]{1,0:T(8,128)(2,1)S(1)} %get-tuple-element.66), channel_id=1, source_target_pairs={{0,192},{2,194},{4,196},{6,198},{8,200},{10,202},{12,204},{14,206}... | collective-permute-start | bytes 196616 | tf_op jit(solution)/shard_map/ppermute | solution.py:571
  87.9 0.0 collective-permute-start.15
  87.9 1.0 collective-permute-start.16
  88.9 2.2 %collective-permute-done.14 = bf16[32,1024]{1,0:T(8,128)(2,1)S(1)} collective-permute-done((bf16[32,1024]{1,0:T(8,128)(2,1)S(1)}, bf16[32,1024]{1,0:T(8,128)(2,1)S(1)}, u32[]{:S(2)}, u32[]{:S(2)}) %collective-permute-start.14) | collective-permute-done | bytes 65568 | tf_op jit(solution)/shard_map/ppermute | solution.py:571
  91.1 2.7 %collective-permute-done.15 = bf16[32,1024]{1,0:T(8,128)(2,1)S(1)} collective-permute-done((bf16[32,1024]{1,0:T(8,128)(2,1)S(1)}, bf16[32,1024]{1,0:T(8,128)(2,1)S(1)}, u32[]{:S(2)}, u32[]{:S(2)}) %collective-permute-start.15) | collective-permute-done | bytes 65568 | tf_op jit(solution)/shard_map/ppermute | solution.py:571
  93.7 0.6 collective-permute-done.16
  94.4 0.0 collective-permute-done.11
  94.4 0.0 collective-permute-done.13
  94.4 0.1 collective-permute-start.17
  94.6 3.3 %collective-permute-start.18 = (bf16[512,128]{1,0:T(8,128)(2,1)S(1)}, bf16[512,128]{1,0:T(8,128)(2,1)S(1)}, u32[]{:S(2)}, u32[]{:S(2)}) collective-permute-start(bf16[512,128]{1,0:T(8,128)(2,1)S(1)} %add_convert_fusion.1), channel_id=1, source_target_pairs={{0,14},{2,0},{4,2},{6,4},{8,6},{10,8},{12,10},{14,12},{16,30},{18,... | collective-permute-start | bytes 393224 | tf_op jit(solution)/shard_map/ppermute | solution.py:552
  97.9 0.0 copy-start.7
  97.9 0.6 collective-permute-start.21
  98.5 3.2 %collective-permute-start.20 = (bf16[8,1024]{1,0:T(8,128)(2,1)S(1)}, bf16[8,1024]{1,0:T(8,128)(2,1)S(1)}, u32[]{:S(2)}, u32[]{:S(2)}) collective-permute-start(bf16[8,1024]{1,0:T(8,128)(2,1)S(1)} %get-tuple-element.84), channel_id=1, source_target_pairs={{0,32},{2,34},{4,36},{6,38},{8,40},{10,42},{12,44},{14,46},{16,48}... | collective-permute-start | bytes 49160 | tf_op jit(solution)/shard_map/ppermute | solution.py:571
  101.7 0.1 collective-permute-start.19
  101.8 0.1 collective-permute-done.21.part3
  102.0 0.7 collective-permute-start.9
  102.6 1.1 collective-permute-done.20.part2
  103.8 1.7 %collective-permute-done.19.part1 = bf16[8,1024]{1,0:T(8,128)(2,1)S(1)} collective-permute-done((bf16[8,1024]{1,0:T(8,128)(2,1)S(1)}, bf16[8,1024]{1,0:T(8,128)(2,1)S(1)}, u32[]{:S(2)}, u32[]{:S(2)}) %collective-permute-start.19) | collective-permute-done | bytes 16416 | tf_op jit(solution)/shard_map/ppermute | solution.py:571
  105.5 0.0 collective-permute-done.17
  105.5 0.0 collective-permute-done.18.from_after
  105.5 0.1 collective-permute-start.22
  105.6 0.0 collective-permute-done.9.arrived
  105.7 6.1 %collective-permute-done.22.from_before = bf16[512,128]{1,0:T(8,128)(2,1)S(1)} collective-permute-done((bf16[512,128]{1,0:T(8,128)(2,1)S(1)}, bf16[512,128]{1,0:T(8,128)(2,1)S(1)}, u32[]{:S(2)}, u32[]{:S(2)}) %collective-permute-start.22) | collective-permute-done | bytes 131104 | tf_op jit(solution)/shard_map/ppermute | solution.py:549
  111.8 0.0 copy-done.5
  111.8 0.0 copy-done.11
  111.8 0.6 copy-done.10
  112.4 2.7 %shard_map.109 = (bf16[128,512]{1,0:T(8,128)(2,1)}, bf16[128,512]{1,0:T(8,128)(2,1)}, bf16[128,512]{1,0:T(8,128)(2,1)}) custom-call(s32[8]{0:T(128)} %starts.3, s32[8]{0:T(128)} %slots.3, f32[256,512]{1,0:T(8,128)} %copy-done.5, bf16[256,512]{1,0:T(8,128)(2,1)} %copy-done.8, bf16[32,1024]{1,0:T(8,128)(2,1)} %copy-done.7, bf16[8,1024]{1,0:T(8,128)(2,1)} %copy-done.13, ...), custom_call_target="tpu_custom_call" | custom-call | tf_op jit(solution)/shard_map/pallas_call | solution.py:583
  (27 shorter events, 0.3 us)
Async XLA Ops:
  0.6 3.2 %collective-permute-start = (bf16[128,1024]{1,0:T(8,128)(2,1)}, bf16[128,1024]{1,0:T(8,128)(2,1)S(1)}, u32[]{:S(2)}, u32[]{:S(2)}) collective-permute-start(bf16[128,1024]{1,0:T(8,128)(2,1)} %grad_own.1), channel_id=1, source_target_pairs={{0,1},{1,0},{2,3},{3,2},{4,5},{5,4},{6,7},{7,6},{8,9},{9,8},{10,11... | collective-permute-start | bytes 786440 | tf_op jit(solution)/shard_map/ppermute | solution.py:448
  3.8 47.1 %copy-start.2 = (bf16[272,512]{1,0:T(8,128)(2,1)}, bf16[272,512]{1,0:T(8,128)(2,1)S(1)}, u32[]{:S(2)}) copy-start(bf16[272,512]{1,0:T(8,128)(2,1)S(1)} %get-tuple-element.48.refs_7_.refs_1_.refs_8_) | copy-start | bytes 835588
  5.7 21.2 %collective-permute-start.2 = (bf16[272,512]{1,0:T(8,128)(2,1)S(1)}, bf16[272,512]{1,0:T(8,128)(2,1)S(1)}, u32[]{:S(2)}, u32[]{:S(2)}) collective-permute-start(bf16[272,512]{1,0:T(8,128)(2,1)S(1)} %shard_map.104.refs_0_), channel_id=1, source_target_pairs={{0,2},{2,4},{4,6},{6,8},{8,10},{10,12},{12,14},{14,0},{16,18},{18,... | collective-permute-start | bytes 835592 | tf_op jit(solution)/shard_map/ppermute | solution.py:486
  7.7 19.2 %collective-permute-start.1 = (bf16[272,512]{1,0:T(8,128)(2,1)S(1)}, bf16[272,512]{1,0:T(8,128)(2,1)S(1)}, u32[]{:S(2)}, u32[]{:S(2)}) collective-permute-start(bf16[272,512]{1,0:T(8,128)(2,1)S(1)} %shard_map.104.refs_0_), channel_id=1, source_target_pairs={{0,14},{2,0},{4,2},{6,4},{8,6},{10,8},{12,10},{14,12},{16,30},{18,... | collective-permute-start | bytes 835592 | tf_op jit(solution)/shard_map/ppermute | solution.py:485
  11.7 15.2 %all-to-all-start = ((bf16[16,8,1024]{2,1,0:T(8,128)(2,1)}), bf16[16,8,1024]{2,1,0:T(8,128)(2,1)S(1)}, u32[]{:S(2)}, u32[]{:S(2)}) async-start(bf16[16,8,1024]{2,1,0:T(8,128)(2,1)} %get-tuple-element.45), calls=%async_computation | async-start | bytes 524288 | tf_op jit(solution)/shard_map/all_to_all | solution.py:489
  19.2 9.8 %collective-permute-start.5 = (bf16[272,512]{1,0:T(8,128)(2,1)S(1)}, bf16[272,512]{1,0:T(8,128)(2,1)S(1)}, u32[]{:S(2)}, u32[]{:S(2)}) collective-permute-start(bf16[272,512]{1,0:T(8,128)(2,1)S(1)} %get-tuple-element.48.refs_7_.refs_1_.refs_8_), channel_id=1, source_target_pairs={{8,24},{10,26},{12,28},{14,30},{24,40},{26,42},{28,44},{30,46},{40... | collective-permute-start | bytes 835592 | tf_op jit(solution)/shard_map/ppermute | solution.py:493
  26.9 39.6 %copy-start = (bf16[272,512]{1,0:T(8,128)(2,1)}, bf16[272,512]{1,0:T(8,128)(2,1)S(1)}, u32[]{:S(2)}) copy-start(bf16[272,512]{1,0:T(8,128)(2,1)S(1)} %collective-permute-done.2.refs_2_.refs_7_) | copy-start | bytes 835588
  26.9 7.6 %collective-permute-start.3 = (bf16[272,512]{1,0:T(8,128)(2,1)S(1)}, bf16[272,512]{1,0:T(8,128)(2,1)S(1)}, u32[]{:S(2)}, u32[]{:S(2)}) collective-permute-start(bf16[272,512]{1,0:T(8,128)(2,1)S(1)} %collective-permute-done.1.refs_1_), channel_id=1, source_target_pairs={{0,14},{2,0},{4,2},{6,4},{8,6},{10,8},{12,10},{14,12},{16,30},{18,... | collective-permute-start | bytes 835592 | tf_op jit(solution)/shard_map/ppermute | solution.py:485
  28.6 8.2 %collective-permute-start.4 = (bf16[272,512]{1,0:T(8,128)(2,1)S(1)}, bf16[272,512]{1,0:T(8,128)(2,1)S(1)}, u32[]{:S(2)}, u32[]{:S(2)}) collective-permute-start(bf16[272,512]{1,0:T(8,128)(2,1)S(1)} %collective-permute-done.2.refs_2_.refs_7_), channel_id=1, source_target_pairs={{0,2},{2,4},{4,6},{6,8},{8,10},{10,12},{12,14},{14,0},{16,18},{18,... | collective-permute-start | bytes 835592 | tf_op jit(solution)/shard_map/ppermute | solution.py:486
  29.0 37.5 %copy-start.3 = (bf16[272,512]{1,0:T(8,128)(2,1)}, bf16[272,512]{1,0:T(8,128)(2,1)S(1)}, u32[]{:S(2)}) copy-start(bf16[272,512]{1,0:T(8,128)(2,1)S(1)} %collective-permute-done.5.refs_8_.refs_2_.refs_9_) | copy-start | bytes 835588
  36.8 7.5 %collective-permute-start.6 = (bf16[272,512]{1,0:T(8,128)(2,1)S(1)}, bf16[272,512]{1,0:T(8,128)(2,1)S(1)}, u32[]{:S(2)}, u32[]{:S(2)}) collective-permute-start(bf16[272,512]{1,0:T(8,128)(2,1)S(1)} %collective-permute-done.3.refs_3_.refs_2_), channel_id=1, source_target_pairs={{0,14},{2,0},{4,2},{6,4},{8,6},{10,8},{12,10},{14,12},{16,30},{18,... | collective-permute-start | bytes 835592 | tf_op jit(solution)/shard_map/ppermute | solution.py:485
  37.1 7.8 %collective-permute-start.7 = (bf16[272,512]{1,0:T(8,128)(2,1)S(1)}, bf16[272,512]{1,0:T(8,128)(2,1)S(1)}, u32[]{:S(2)}, u32[]{:S(2)}) collective-permute-start(bf16[272,512]{1,0:T(8,128)(2,1)S(1)} %collective-permute-done.4.refs_4_.refs_6_), channel_id=1, source_target_pairs={{0,2},{2,4},{4,6},{6,8},{8,10},{10,12},{12,14},{14,0},{16,18},{18,... | collective-permute-start | bytes 835592 | tf_op jit(solution)/shard_map/ppermute | solution.py:486
  44.3 6.5 %collective-permute-start.8 = (bf16[272,512]{1,0:T(8,128)(2,1)S(1)}, bf16[272,512]{1,0:T(8,128)(2,1)S(1)}, u32[]{:S(2)}, u32[]{:S(2)}) collective-permute-start(bf16[272,512]{1,0:T(8,128)(2,1)S(1)} %collective-permute-done.6.refs_5_.refs_3_), channel_id=1, source_target_pairs={{0,14},{2,0},{4,2},{6,4},{8,6},{10,8},{12,10},{14,12},{16,30},{18,... | collective-permute-start | bytes 835592 | tf_op jit(solution)/shard_map/ppermute | solution.py:496
  50.3 16.2 %copy-start.4 = (f32[11,128,128]{2,1,0:T(8,128)}, f32[11,128,128]{2,1,0:T(8,128)S(1)}, u32[]{:S(2)}) copy-start(f32[11,128,128]{2,1,0:T(8,128)S(1)} %get-tuple-element.53.refs_11_) | copy-start | bytes 2162692
  66.5 16.8 %copy-start.1 = (bf16[272,512]{1,0:T(8,128)(2,1)S(1)}, bf16[272,512]{1,0:T(8,128)(2,1)}, u32[]{:S(2)}) copy-start(bf16[272,512]{1,0:T(8,128)(2,1)} %copy-done) | copy-start | bytes 835588
  72.8 13.9 %copy-start.6 = (bf16[512,128]{1,0:T(8,128)(2,1)}, bf16[512,128]{1,0:T(8,128)(2,1)S(1)}, u32[]{:S(2)}) copy-start(bf16[512,128]{1,0:T(8,128)(2,1)S(1)} %get-tuple-element.79.here) | copy-start | bytes 393220
  72.8 7.0 %collective-permute-start.10 = (bf16[512,128]{1,0:T(8,128)(2,1)S(1)}, bf16[512,128]{1,0:T(8,128)(2,1)S(1)}, u32[]{:S(2)}, u32[]{:S(2)}) collective-permute-start(bf16[512,128]{1,0:T(8,128)(2,1)S(1)} %get-tuple-element.62), channel_id=1, source_target_pairs={{0,2},{2,4},{4,6},{6,8},{8,10},{10,12},{12,14},{14,0},{16,18},{18,... | collective-permute-start | bytes 393224 | tf_op jit(solution)/shard_map/ppermute | solution.py:549
  73.0 6.9 %collective-permute-start.12 = (bf16[512,128]{1,0:T(8,128)(2,1)S(1)}, bf16[512,128]{1,0:T(8,128)(2,1)S(1)}, u32[]{:S(2)}, u32[]{:S(2)}) collective-permute-start(bf16[512,128]{1,0:T(8,128)(2,1)S(1)} %get-tuple-element.64), channel_id=1, source_target_pairs={{0,14},{2,0},{4,2},{6,4},{8,6},{10,8},{12,10},{14,12},{16,30},{18,... | collective-permute-start | bytes 393224 | tf_op jit(solution)/shard_map/ppermute | solution.py:552
  79.9 14.5 %collective-permute-start.11 = (bf16[512,128]{1,0:T(8,128)(2,1)S(1)}, bf16[512,128]{1,0:T(8,128)(2,1)S(1)}, u32[]{:S(2)}, u32[]{:S(2)}) collective-permute-start(bf16[512,128]{1,0:T(8,128)(2,1)S(1)} %add_convert_fusion.4), channel_id=1, source_target_pairs={{0,2},{2,4},{4,6},{6,8},{8,10},{10,12},{12,14},{14,0},{16,18},{18,... | collective-permute-start | bytes 393224 | tf_op jit(solution)/shard_map/ppermute | solution.py:549
  80.0 14.4 %collective-permute-start.13 = (bf16[512,128]{1,0:T(8,128)(2,1)S(1)}, bf16[512,128]{1,0:T(8,128)(2,1)S(1)}, u32[]{:S(2)}, u32[]{:S(2)}) collective-permute-start(bf16[512,128]{1,0:T(8,128)(2,1)S(1)} %add_convert_fusion.3), channel_id=1, source_target_pairs={{0,14},{2,0},{4,2},{6,4},{8,6},{10,8},{12,10},{14,12},{16,30},{18,... | collective-permute-start | bytes 393224 | tf_op jit(solution)/shard_map/ppermute | solution.py:552
  86.7 25.1 %copy-start.5 = (f32[256,512]{1,0:T(8,128)}, f32[256,512]{1,0:T(8,128)S(1)}, u32[]{:S(2)}) copy-start(f32[256,512]{1,0:T(8,128)S(1)} %get-tuple-element.59.own_grad) | copy-start | bytes 1572868
  86.7 4.3 %collective-permute-start.14 = (bf16[32,1024]{1,0:T(8,128)(2,1)S(1)}, bf16[32,1024]{1,0:T(8,128)(2,1)S(1)}, u32[]{:S(2)}, u32[]{:S(2)}) collective-permute-start(bf16[32,1024]{1,0:T(8,128)(2,1)S(1)} %get-tuple-element.66), channel_id=1, source_target_pairs={{0,192},{2,194},{4,196},{6,198},{8,200},{10,202},{12,204},{14,206}... | collective-permute-start | bytes 196616 | tf_op jit(solution)/shard_map/ppermute | solution.py:571
  87.9 5.8 %collective-permute-start.15 = (bf16[32,1024]{1,0:T(8,128)(2,1)S(1)}, bf16[32,1024]{1,0:T(8,128)(2,1)S(1)}, u32[]{:S(2)}, u32[]{:S(2)}) collective-permute-start(bf16[32,1024]{1,0:T(8,128)(2,1)S(1)} %get-tuple-element.67), channel_id=1, source_target_pairs={{0,128},{2,130},{4,132},{6,134},{8,136},{10,138},{12,140},{14,142}... | collective-permute-start | bytes 196616 | tf_op jit(solution)/shard_map/ppermute | solution.py:571
  87.9 6.5 %collective-permute-start.16 = (bf16[32,1024]{1,0:T(8,128)(2,1)S(1)}, bf16[32,1024]{1,0:T(8,128)(2,1)S(1)}, u32[]{:S(2)}, u32[]{:S(2)}) collective-permute-start(bf16[32,1024]{1,0:T(8,128)(2,1)S(1)} %get-tuple-element.68), channel_id=1, source_target_pairs={{0,64},{2,66},{4,68},{6,70},{8,72},{10,74},{12,76},{14,78},{16,80}... | collective-permute-start | bytes 196616 | tf_op jit(solution)/shard_map/ppermute | solution.py:571
  94.4 11.1 %collective-permute-start.17 = (bf16[512,128]{1,0:T(8,128)(2,1)S(1)}, bf16[512,128]{1,0:T(8,128)(2,1)S(1)}, u32[]{:S(2)}, u32[]{:S(2)}) collective-permute-start(bf16[512,128]{1,0:T(8,128)(2,1)S(1)} %add_convert_fusion.2), channel_id=1, source_target_pairs={{0,2},{2,4},{4,6},{6,8},{8,10},{10,12},{12,14},{14,0},{16,18},{18,... | collective-permute-start | bytes 393224 | tf_op jit(solution)/shard_map/ppermute | solution.py:549
  94.6 10.9 %collective-permute-start.18 = (bf16[512,128]{1,0:T(8,128)(2,1)S(1)}, bf16[512,128]{1,0:T(8,128)(2,1)S(1)}, u32[]{:S(2)}, u32[]{:S(2)}) collective-permute-start(bf16[512,128]{1,0:T(8,128)(2,1)S(1)} %add_convert_fusion.1), channel_id=1, source_target_pairs={{0,14},{2,0},{4,2},{6,4},{8,6},{10,8},{12,10},{14,12},{16,30},{18,... | collective-permute-start | bytes 393224 | tf_op jit(solution)/shard_map/ppermute | solution.py:552
  97.9 13.9 %copy-start.7 = (bf16[32,1024]{1,0:T(8,128)(2,1)}, bf16[32,1024]{1,0:T(8,128)(2,1)S(1)}, u32[]{:S(2)}) copy-start(bf16[32,1024]{1,0:T(8,128)(2,1)S(1)} %add_convert_fusion.5.part0) | copy-start | bytes 196612
  97.9 4.0 %collective-permute-start.21 = (bf16[8,1024]{1,0:T(8,128)(2,1)S(1)}, bf16[8,1024]{1,0:T(8,128)(2,1)S(1)}, u32[]{:S(2)}, u32[]{:S(2)}) collective-permute-start(bf16[8,1024]{1,0:T(8,128)(2,1)S(1)} %get-tuple-element.83), channel_id=1, source_target_pairs={{0,16},{2,18},{4,20},{6,22},{8,24},{10,26},{12,28},{14,30},{16,32}... | collective-permute-start | bytes 49160 | tf_op jit(solution)/shard_map/ppermute | solution.py:571
  98.5 5.2 %collective-permute-start.20 = (bf16[8,1024]{1,0:T(8,128)(2,1)S(1)}, bf16[8,1024]{1,0:T(8,128)(2,1)S(1)}, u32[]{:S(2)}, u32[]{:S(2)}) collective-permute-start(bf16[8,1024]{1,0:T(8,128)(2,1)S(1)} %get-tuple-element.84), channel_id=1, source_target_pairs={{0,32},{2,34},{4,36},{6,38},{8,40},{10,42},{12,44},{14,46},{16,48}... | collective-permute-start | bytes 49160 | tf_op jit(solution)/shard_map/ppermute | solution.py:571
  101.7 3.7 %collective-permute-start.19 = (bf16[8,1024]{1,0:T(8,128)(2,1)S(1)}, bf16[8,1024]{1,0:T(8,128)(2,1)S(1)}, u32[]{:S(2)}, u32[]{:S(2)}) collective-permute-start(bf16[8,1024]{1,0:T(8,128)(2,1)S(1)} %get-tuple-element.85), channel_id=1, source_target_pairs={{0,48},{2,50},{4,52},{6,54},{8,56},{10,58},{12,60},{14,62},{16,0},... | collective-permute-start | bytes 49160 | tf_op jit(solution)/shard_map/ppermute | solution.py:571
  102.0 9.8 %copy-start.11 = (bf16[8,1024]{1,0:T(8,128)(2,1)}, bf16[8,1024]{1,0:T(8,128)(2,1)S(1)}, u32[]{:S(2)}) copy-start(bf16[8,1024]{1,0:T(8,128)(2,1)S(1)} %collective-permute-done.21.part3) | copy-start | bytes 49156
  102.0 3.7 %collective-permute-start.9 = (bf16[256,512]{1,0:T(8,128)(2,1)S(1)}, bf16[256,512]{1,0:T(8,128)(2,1)S(1)}, u32[]{:S(2)}, u32[]{:S(2)}) collective-permute-start(bf16[256,512]{1,0:T(8,128)(2,1)S(1)} %get-tuple-element.60), channel_id=1, source_target_pairs={{24,8},{26,10},{28,12},{30,14},{40,24},{42,26},{44,28},{46,30},{56... | collective-permute-start | bytes 786440 | tf_op jit(solution)/shard_map/ppermute | solution.py:555
  103.8 8.1 %copy-start.12 = (bf16[8,1024]{1,0:T(8,128)(2,1)}, bf16[8,1024]{1,0:T(8,128)(2,1)S(1)}, u32[]{:S(2)}) copy-start(bf16[8,1024]{1,0:T(8,128)(2,1)S(1)} %collective-permute-done.20.part2) | copy-start | bytes 49156
  105.5 6.3 %copy-start.13 = (bf16[8,1024]{1,0:T(8,128)(2,1)}, bf16[8,1024]{1,0:T(8,128)(2,1)S(1)}, u32[]{:S(2)}) copy-start(bf16[8,1024]{1,0:T(8,128)(2,1)S(1)} %collective-permute-done.19.part1) | copy-start | bytes 49156
  105.5 6.3 %copy-start.9 = (bf16[512,128]{1,0:T(8,128)(2,1)}, bf16[512,128]{1,0:T(8,128)(2,1)S(1)}, u32[]{:S(2)}) copy-start(bf16[512,128]{1,0:T(8,128)(2,1)S(1)} %collective-permute-done.18.from_after) | copy-start | bytes 393220
  105.5 6.3 %collective-permute-start.22 = (bf16[512,128]{1,0:T(8,128)(2,1)S(1)}, bf16[512,128]{1,0:T(8,128)(2,1)S(1)}, u32[]{:S(2)}, u32[]{:S(2)}) collective-permute-start(bf16[512,128]{1,0:T(8,128)(2,1)S(1)} %add_convert_fusion), channel_id=1, source_target_pairs={{0,2},{2,4},{4,6},{6,8},{8,10},{10,12},{12,14},{14,0},{16,18},{18,... | collective-permute-start | bytes 393224 | tf_op jit(solution)/shard_map/ppermute | solution.py:549
  105.6 6.2 %copy-start.8 = (bf16[256,512]{1,0:T(8,128)(2,1)}, bf16[256,512]{1,0:T(8,128)(2,1)S(1)}, u32[]{:S(2)}) copy-start(bf16[256,512]{1,0:T(8,128)(2,1)S(1)} %collective-permute-done.9.arrived) | copy-start | bytes 786436
  111.8 0.6 copy-start.10

commit v4 on v3

--- a/solution.py
+++ b/solution.py
@@ -46,6 +46,7 @@
 EARLY = (0, 1, 7, 2, 6, 3, 5)
 LATE = (4,)
 ORDER = EARLY + LATE
+TOGETHER = 2
 
 VMEM_LIMIT = 50 * 2**20
 SMEM = pltpu.SMEM
@@ -313,18 +314,21 @@
     ]
     writes = []
     others = [[None, None] for _ in range(HEADS_HERE)]
-    for i, o in enumerate(order):
-        for copy in copies[i]:
-            copy.wait()
-        chunk = jnp.bitwise_and(z + o, NZ - 1)
-        made = [products(packed, pairs, keys, bias, h, o) for h in range(HEADS_HERE)]
+    for first in range(0, NZ, TOGETHER):
+        group = range(first, first + TOGETHER)
+        for i in group:
+            for copy in copies[i]:
+                copy.wait()
+        units = [(i, order[i], h) for i in group for h in range(HEADS_HERE)]
+        made = [products(packed, pairs, keys, bias, h, o) for _, o, h in units]
         low_parts = []
-        for h, (_, scores, dprobs, mask) in enumerate(made):
+        for (i, o, h), (_, scores, dprobs, mask) in zip(units, made):
+            chunk = jnp.bitwise_and(z + o, NZ - 1)
             log_sum = merged[chunk, h : h + 1, :]
             delta = merged[chunk, HEADS_HERE + h : HEADS_HERE + h + 1, :]
             probs = jnp.exp2(scores * EXP_SCALE - log_sum + mask)
             low_parts.append(((probs * (dprobs - delta)).astype(BF16), probs.astype(BF16)))
-        for h, (dscores, probs_low) in enumerate(low_parts):
+        for (i, o, h), (dscores, probs_low) in zip(units, low_parts):
             turned = keys_turned[h]
             if o <= REACH:
                 side = pairs_turned[h][0]
@@ -332,8 +336,9 @@
                     side = jnp.where(z + o >= NZ, pairs_turned[h][1], side)
                 turned = jnp.concatenate([side, turned], axis=1)
             dquery = jnp.dot(turned, dscores, preferred_element_type=F32)
-            query_grads[o][h * HD : (h + 1) * HD, :] = (SCALE * dquery).astype(BF16)
-        for h, (dscores, probs_low) in enumerate(low_parts):
+            turned = jnp.transpose(SCALE * dquery)
+            query_grads[o][:, h * HD : (h + 1) * HD] = turned.astype(BF16)
+        for (i, o, h), (dscores, probs_low) in zip(units, low_parts):
             if o <= REACH:
                 window[near.index(o), 0, h] = dscores[0:TOK]
                 window[near.index(o), 1, h] = probs_low[0:TOK]
@@ -347,14 +352,16 @@
                     others[h][kind] = part if old is None else old + part
             coarse[i, 0, h] = dscores[-TOK:]
             coarse[i, 1, h] = probs_low[-TOK:]
-        writes.append(pltpu.make_async_copy(coarse.at[i], coarse_out.at[i], out_sems.at[0, o]))
-        writes[-1].start()
-        if o <= REACH:
-            at = near.index(o)
-            writes.append(
-                pltpu.make_async_copy(window.at[at], window_out.at[at], out_sems.at[1, o])
-            )
+        for i in group:
+            o = order[i]
+            writes.append(pltpu.make_async_copy(coarse.at[i], coarse_out.at[i], out_sems.at[0, o]))
             writes[-1].start()
+            if o <= REACH:
+                at = near.index(o)
+                writes.append(
+                    pltpu.make_async_copy(window.at[at], window_out.at[at], out_sems.at[1, o])
+                )
+                writes[-1].start()
     for h in range(HEADS_HERE):
         cols = slice(h * HD, (h + 1) * HD)
         previous_grad[0:TOK, cols] = (others[h][0] * SCALE).astype(BF16)
@@ -367,72 +374,71 @@
     order = ORDER
     near = [o for o in order if o <= REACH]
     chunks, (coarse_in, window_in), refs = refs[:NZ], refs[NZ : NZ + 2], refs[NZ + 2 :]
-    own_grad, *sum_grads = refs[: 1 + NY]
-    packed, coarse, window, sum_grad, sems = refs[1 + NY :]
-    copies = [pltpu.make_async_copy(chunks[i], packed.at[i], sems.at[i]) for i in range(NZ)]
-    copies.append(pltpu.make_async_copy(coarse_in, coarse, sems.at[NZ]))
-    copies.append(pltpu.make_async_copy(window_in, window, sems.at[NZ + 1]))
-    for copy in copies:
-        copy.start()
-    for copy in copies:
-        copy.wait()
+    own_grad, sum_grad, packed, coarse, window, sems = refs
+    copies = []
+    for i, o in enumerate(order):
+        mine = [pltpu.make_async_copy(chunks[i], packed.at[i], sems.at[0, i])]
+        mine.append(pltpu.make_async_copy(coarse_in.at[i], coarse.at[i], sems.at[1, i]))
+        if o in near:
+            at = near.index(o)
+            mine.append(pltpu.make_async_copy(window_in.at[at], window.at[at], sems.at[2, i]))
+        for copy in mine:
+            copy.start()
+        copies.append(mine)
     _, z = place()
-    for h in range(HEADS_HERE):
-        cols = slice(h * HD, (h + 1) * HD)
-        for kind in range(2):
-            tokens = [packed[i, kind * TOK : (kind + 1) * TOK, cols] for i in range(NZ)]
-            scale = SCALE if kind == 0 else 1.0
-            at = (2 * h + kind) * HD
-            rows = slice(kind * TOK, (kind + 1) * TOK)
-            total = jnp.dot(
-                jnp.concatenate([coarse[i, kind, h] for i in range(NZ)], axis=1),
+    units = [(h, kind) for h in range(HEADS_HERE) for kind in range(2)]
+    totals, mine = [None] * len(units), [None] * len(units)
+    half = NZ // 2
+    for first in range(0, NZ, half):
+        group = range(first, first + half)
+        for i in group:
+            for copy in copies[i]:
+                copy.wait()
+        for unit, (h, kind) in enumerate(units):
+            cols = slice(h * HD, (h + 1) * HD)
+            tokens = [packed[i, kind * TOK : (kind + 1) * TOK, cols] for i in group]
+            part = jnp.dot(
+                jnp.concatenate([coarse[i, kind, h] for i in group], axis=1),
                 jnp.concatenate(tokens, axis=0),
                 preferred_element_type=F32,
             )
-            total = total * scale
-            for j in range(NXY):
-                part = total[j * BARS_HERE : (j + 1) * BARS_HERE]
-                sum_grad[j, :, at : at + HD] = part
-            mine = jnp.zeros((TOK, HD), F32)
-            for i, o in enumerate(near):
-                part = jnp.dot(
-                    window[i, kind, h], tokens[order.index(o)], preferred_element_type=F32
-                )
-                mine = mine + part * (z + o < NZ).astype(F32)
-            own_grad[rows, cols] = mine * scale
-    rank, _ = place()
-    y = lax.shift_right_logical(rank, 5)
-    x = lax.shift_right_logical(rank, 3)
-    for i in range(NY):
-        for k in range(NX):
-            j = jnp.bitwise_and(y - i, NY - 1) * NX + jnp.bitwise_and(x - k, NX - 1)
-            rows = slice(k * BARS_HERE, (k + 1) * BARS_HERE)
-            sum_grads[i][rows, :] = sum_grad[j].astype(BF16)
-
-
-def finish_kernel(
-    starts, slots, own_grad, arrived, part0, part1, part2, part3, here, from_before, from_after,
-    grad_queries, grad_keys, grad_values
-):
+            totals[unit] = part if first == 0 else totals[unit] + part
+            for i in group:
+                if order[i] in near:
+                    part = jnp.dot(
+                        window[near.index(order[i]), kind, h],
+                        tokens[i - first],
+                        preferred_element_type=F32,
+                    )
+                    part = part * (z + order[i] < NZ).astype(F32)
+                    mine[unit] = part if mine[unit] is None else mine[unit] + part
+    for unit, (h, kind) in enumerate(units):
+        scale = SCALE if kind == 0 else 1.0
+        at = (2 * h + kind) * HD
+        own_grad[kind * TOK : (kind + 1) * TOK, h * HD : (h + 1) * HD] = mine[unit] * scale
+        sum_grad[:, at : at + HD] = (totals[unit] * scale).astype(BF16)
+
+
+def finish_kernel(starts, slots, own_grad, arrived, parts, grad_keys, grad_values):
     base = starts[0]
-    total = part0[0:BARS_HERE, :].astype(F32)
-    for part in (part1, part2, part3):
-        total = total + part[...].astype(F32)
-    row = lax.broadcasted_iota(jnp.int32, (TOK, HD), 0)
+    total = parts[0].astype(F32)
+    for i in range(1, NXY):
+        total = total + parts[i].astype(F32)
+    high = total.astype(BF16).astype(F32)
+    halves = jnp.concatenate([high, total - high], axis=0).astype(BF16)
+    lane = lax.broadcasted_iota(jnp.int32, (2 * BARS_HERE, TOK), 1)
+    row = lax.broadcasted_iota(jnp.int32, (2 * BARS_HERE, TOK), 0)
+    slot = jnp.full((2 * BARS_HERE, TOK), -1, jnp.int32)
+    for b in range(BARS_HERE):
+        slot = jnp.where(jnp.bitwise_and(row, BARS_HERE - 1) == b, slots[b] - base, slot)
+    placed = lax.dot_general(low(lane == slot), halves, TN, preferred_element_type=F32)
     for h in range(HEADS_HERE):
         cols = slice(h * HD, (h + 1) * HD)
         for kind, out in ((0, grad_keys), (1, grad_values)):
             rows = slice(kind * TOK, (kind + 1) * TOK)
             at = (2 * h + kind) * HD
             grad = own_grad[rows, cols] + arrived[rows, cols].astype(F32)
-            for b in range(BARS_HERE):
-                grad = grad + jnp.where(row == slots[b] - base, total[b : b + 1, at : at + HD], 0.0)
-            out[:, cols] = grad.astype(BF16)
-    for h in range(HEADS_HERE):
-        rows = slice(h * HD, (h + 1) * HD)
-        total = here[rows, :].astype(F32) + from_before[rows, :].astype(F32)
-        total = total + from_after[rows, :].astype(F32)
-        grad_queries[:, rows] = jnp.transpose(total).astype(BF16)
+            out[:, cols] = (grad + placed[:, at : at + HD]).astype(BF16)
 
 
 def add_low(*parts):
@@ -526,7 +532,7 @@
     window_shape = (REACH + 1, 2, HEADS_HERE, TOK, TOK)
     *grads, coarse, window, previous_grad = pl.pallas_call(
         query_grad_kernel,
-        out_shape=(shape((FEAT, TOK)),) * NZ
+        out_shape=(shape((TOK, FEAT)),) * NZ
         + (shape(coarse_shape), shape(window_shape), shape((2 * TOK, FEAT))),
         in_specs=[whole(HBM)] * (NZ + 6),
         out_specs=(whole(VMEM),) * NZ + (whole(HBM),) * 2 + (whole(VMEM),),
@@ -553,48 +559,36 @@
 
     forward, backward = forward_step(grads[4]), backward_step(grads[5])
     arrived = lax.ppermute(previous_grad, "seq", ROW_DOWN)
-    own_grad, *sum_grads = pl.pallas_call(
+    own_grad, sum_grad = pl.pallas_call(
         key_grad_kernel,
-        out_shape=(shape((2 * TOK, FEAT), F32),) + (shape((NX * BARS_HERE, 2 * FEAT)),) * NY,
+        out_shape=(shape((2 * TOK, FEAT), F32), shape((bars, 2 * FEAT))),
         in_specs=[whole(HBM)] * (NZ + 2),
-        out_specs=(whole(VMEM),) * (1 + NY),
+        out_specs=(whole(VMEM),) * 2,
         scratch_shapes=[
             VMEM((NZ, ROWS, FEAT), BF16),
             VMEM(coarse_shape, BF16),
             VMEM(window_shape, BF16),
-            VMEM((NXY, BARS_HERE, 2 * FEAT), F32),
-            dma((NZ + 2,)),
+            dma((3, NZ)),
         ],
         compiler_params=params,
     )(*[chunks[o] for o in ORDER], coarse, window)
 
-    move = lambda array, *by: lax.ppermute(array, "seq", route(*by))
+    forward, backward, sum_grad = lax.optimization_barrier((forward, backward, sum_grad))
     forward, backward = forward_step(add_low(forward, grads[3])), backward_step(add_low(backward, grads[6]))
-    moved = [move(sum_grads[i], -i, 0, 0) for i in range(1, NY)]
-    forward, backward, *moved = lax.optimization_barrier((forward, backward, *moved))
+    parts = lax.all_to_all(
+        sum_grad.reshape(NXY, BARS_HERE, 2 * FEAT), "seq", 0, 0, axis_index_groups=XY_GROUPS
+    )
+    forward, backward, parts = lax.optimization_barrier((forward, backward, parts))
     forward, backward = forward_step(add_low(forward, grads[2])), backward_step(add_low(backward, grads[7]))
-    row_grad = add_low(sum_grads[0], *moved)
-    parts = [
-        move(row_grad[k * BARS_HERE : (k + 1) * BARS_HERE], 0, -k, 0) for k in range(1, NX)
-    ]
-    forward, backward, *parts = lax.optimization_barrier((forward, backward, *parts))
     forward = forward_step(add_low(forward, grads[1]))
 
-    grad_queries, grad_keys, grad_values = pl.pallas_call(
+    grad_keys, grad_values = pl.pallas_call(
         finish_kernel,
-        out_shape=(shape((TOK, FEAT)),) * 3,
-        in_specs=[whole(SMEM)] * 2 + [whole(VMEM)] * 9,
-        out_specs=(whole(VMEM),) * 3,
-    )(
-        *pinned(bar_start, bar_summary_token),
-        own_grad,
-        arrived,
-        row_grad,
-        *parts,
-        grads[0],
-        forward,
-        backward,
-    )
+        out_shape=(shape((TOK, FEAT)),) * 2,
+        in_specs=[whole(SMEM)] * 2 + [whole(VMEM)] * 3,
+        out_specs=(whole(VMEM),) * 2,
+    )(*pinned(bar_start, bar_summary_token), own_grad, arrived, parts)
+    grad_queries = add_low(grads[0], forward, backward)
     return grad_queries, grad_keys, grad_values
 
 

time: 116 us -> 106 us (0.914)
  waiting for transfers between devices: 39.3 us -> 32.5 us
  starting transfers between devices: 35.8 us -> 33.8 us
  Pallas kernels: 23.8 us -> 22.6 us
    ppermute x6 -> x0, waiting for transfers between devices: 8.48 us -> none  [shards(): move = lambda array, *by: lax.ppermute(array, 'seq', route(*by))]
    ppermute x6 -> x0, starting transfers between devices: 6.05 us -> none  [shards(): move = lambda array, *by: lax.ppermute(array, 'seq', route(*by))]
    all_to_all x0 -> x1, starting transfers between devices: none -> 4.81 us  [shards(): lax.all_to_all(sum_grad.reshape(NXY, BARS_HERE, 2 * FEAT), 'seq', 0, 0, a...]
    ppermute x3, waiting for transfers between devices: 0.01 us -> 2.84 us  [backward_step(): return lax.ppermute(array, 'seq', TO_PREVIOUS)]
    pallas_call x3, Pallas kernels: 12.3 us -> 11.1 us  [the longest x1 5.19 us: shards(): pl.pallas_call(query_grad_kernel, out_shape=(shape((TOK, FEAT)),) * NZ +...]
  transfers between devices with their start and end apart: 24 -> 19, of which waited for: 13 -> 9; matrix products, arithmetic and copies ran while one was open for 0% -> 0% of each run, Pallas kernels for 10% -> 14%
where the time goes in v4:
time: 106 us
  starting transfers between devices  33.8 us (32%)
  waiting for transfers between devices  32.5 us (31%)
  Pallas kernels  22.6 us (21%)
  blocking collectives  14.4 us (14%)
    all_to_all x1, blocking collectives, shards(): stats = lax.all_to_all(stats, 'seq', 0, 0, axis_index_groups=Z_GROUPS)  14.4 us
    ppermute x3, waiting for transfers between devices, ring_step(): after.append(lax.ppermute(after[-1], 'seq', TO_PREVIOUS))  11 us
    ppermute x3, starting transfers between devices, backward_step(): return lax.ppermute(array, 'seq', TO_PREVIOUS)  8.83 us
    ppermute x4, waiting for transfers between devices, forward_step(): return lax.ppermute(array, 'seq', TO_NEXT)  8.77 us
    all_to_all x1, starting transfers between devices, shards(): all_sums = lax.all_to_all(sums, 'seq', 0, 0, axis_index_groups=XY_GROUPS)  7.48 us
    all_to_all x1, waiting for transfers between devices, shards(): all_sums = lax.all_to_all(sums, 'seq', 0, 0, axis_index_groups=XY_GROUPS)  7.01 us
    pallas_call x2, Pallas kernels, stats_of(): pl.pallas_call(lambda *refs: stats_kernel(order, *refs), out_shape=out +...  6.62 us
    ppermute x3, starting transfers between devices, ring_step(): after.append(lax.ppermute(after[-1], 'seq', TO_PREVIOUS))  6.05 us
  transfers between devices with their start and end apart: 19, of which 9 were waited for; matrix products, arithmetic and copies ran while one was open for 0% of the time, Pallas kernels for 14%

profile of v4, /device:TPU:2, one launch (start us, length us, event | category | flops | bytes accessed | tf_op | source)
XLA Modules:
  0.0 105.7 jit_solution(10897486035360161218)
XLA Ops:
  0.6 0.1 collective-permute-start
  0.7 3.0 %shard_map.103 = (f32[512,128]{1,0:T(8,128)S(1)}, bf16[272,512]{1,0:T(8,128)(2,1)S(1)}, bf16[272,512]{1,0:T(8,128)(2,1)S(1)}, bf16[16,8,1024]{2,1,0:T(8,128)(2,1)}) custom-call(s32[1]{0:T(128)} %bitcast.core, s32[8]{0:T(128)} %starts.3, s32[8,8]{1,0:T(8,128)} %related.1, s32[8]{0:T(128)} %slots.3, bf16[128,512]{1,0:T(8,128)(2,1)} %queries.1, ...), custom_call_target="tpu_custom_call" | custom-call | tf_op jit(solution)/shard_map/pallas_call | solution.py:457
  3.8 0.0 copy-start.2
  3.8 0.0 collective-permute-done.grad_other
  3.8 1.8 %shard_map.104.refs_0_ = bf16[272,512]{1,0:T(8,128)(2,1)S(1)} custom-call(s32[1]{0:T(128)} %bitcast.core, bf16[272,512]{1,0:T(8,128)(2,1)S(1)} %get-tuple-element.38.pack, f32[512,128]{1,0:T(8,128)S(1)} %get-tuple-element.39.partial, bf16[128,1024]{1,0:T(8,128)(2,1)S(1)} %collective-permute-done.grad_other, bf16[512,2048]{1,0:T(8,128)(2,1)} %out_weight.3), custom_call_target="tpu_custom_call" | custom-call | tf_op jit(solution)/shard_map/pallas_call | solution.py:474
  5.7 2.0 %collective-permute-start.2 = (bf16[272,512]{1,0:T(8,128)(2,1)S(1)}, bf16[272,512]{1,0:T(8,128)(2,1)S(1)}, u32[]{:S(2)}, u32[]{:S(2)}) collective-permute-start(bf16[272,512]{1,0:T(8,128)(2,1)S(1)} %shard_map.104.refs_0_), channel_id=1, source_target_pairs={{0,2},{2,4},{4,6},{6,8},{8,10},{10,12},{12,14},{14,0},{16,18},{18,... | collective-permute-start | bytes 835592 | tf_op jit(solution)/shard_map/ppermute | solution.py:492
  7.7 4.0 %collective-permute-start.1 = (bf16[272,512]{1,0:T(8,128)(2,1)S(1)}, bf16[272,512]{1,0:T(8,128)(2,1)S(1)}, u32[]{:S(2)}, u32[]{:S(2)}) collective-permute-start(bf16[272,512]{1,0:T(8,128)(2,1)S(1)} %shard_map.104.refs_0_), channel_id=1, source_target_pairs={{0,14},{2,0},{4,2},{6,4},{8,6},{10,8},{12,10},{14,12},{16,30},{18,... | collective-permute-start | bytes 835592 | tf_op jit(solution)/shard_map/ppermute | solution.py:491
  11.7 7.5 %all-to-all-start = ((bf16[16,8,1024]{2,1,0:T(8,128)(2,1)}), bf16[16,8,1024]{2,1,0:T(8,128)(2,1)S(1)}, u32[]{:S(2)}, u32[]{:S(2)}) async-start(bf16[16,8,1024]{2,1,0:T(8,128)(2,1)} %get-tuple-element.40), calls=%async_computation | async-start | bytes 524288 | tf_op jit(solution)/shard_map/all_to_all | solution.py:495
  19.2 0.7 collective-permute-start.5
  19.8 7.0 %all-to-all-done = bf16[16,8,1024]{2,1,0:T(8,128)(2,1)S(1)} async-done(((bf16[16,8,1024]{2,1,0:T(8,128)(2,1)}), bf16[16,8,1024]{2,1,0:T(8,128)(2,1)S(1)}, u32[]{:S(2)}, u32[]{:S(2)}) %all-to-all-start) | async-done | bytes 262176 | tf_op jit(solution)/shard_map/all_to_all | solution.py:495
  26.9 0.0 collective-permute-done.2.refs_2_.refs_7_
  26.9 0.0 copy-start
  26.9 0.0 collective-permute-done.1.refs_1_
  26.9 1.7 %collective-permute-start.3 = (bf16[272,512]{1,0:T(8,128)(2,1)S(1)}, bf16[272,512]{1,0:T(8,128)(2,1)S(1)}, u32[]{:S(2)}, u32[]{:S(2)}) collective-permute-start(bf16[272,512]{1,0:T(8,128)(2,1)S(1)} %collective-permute-done.1.refs_1_), channel_id=1, source_target_pairs={{0,14},{2,0},{4,2},{6,4},{8,6},{10,8},{12,10},{14,12},{16,30},{18,... | collective-permute-start | bytes 835592 | tf_op jit(solution)/shard_map/ppermute | solution.py:491
  28.6 0.4 collective-permute-start.4
  29.0 0.0 collective-permute-done.5.refs_8_.refs_2_.refs_9_
  29.0 0.0 copy-start.3
  29.0 5.5 %collective-permute-done.3.refs_3_.refs_2_ = bf16[272,512]{1,0:T(8,128)(2,1)S(1)} collective-permute-done((bf16[272,512]{1,0:T(8,128)(2,1)S(1)}, bf16[272,512]{1,0:T(8,128)(2,1)S(1)}, u32[]{:S(2)}, u32[]{:S(2)}) %collective-permute-start.3) | collective-permute-done | bytes 278560 | tf_op jit(solution)/shard_map/ppermute | solution.py:491
  34.5 2.3 %collective-permute-done.4.refs_4_.refs_6_ = bf16[272,512]{1,0:T(8,128)(2,1)S(1)} collective-permute-done((bf16[272,512]{1,0:T(8,128)(2,1)S(1)}, bf16[272,512]{1,0:T(8,128)(2,1)S(1)}, u32[]{:S(2)}, u32[]{:S(2)}) %collective-permute-start.4) | collective-permute-done | bytes 278560 | tf_op jit(solution)/shard_map/ppermute | solution.py:492
  36.9 0.3 collective-permute-start.6
  37.1 1.7 %collective-permute-start.8 = (bf16[272,512]{1,0:T(8,128)(2,1)S(1)}, bf16[272,512]{1,0:T(8,128)(2,1)S(1)}, u32[]{:S(2)}, u32[]{:S(2)}) collective-permute-start(bf16[272,512]{1,0:T(8,128)(2,1)S(1)} %collective-permute-done.4.refs_4_.refs_6_), channel_id=1, source_target_pairs={{0,2},{2,4},{4,6},{6,8},{8,10},{10,12},{12,14},{14,0},{16,18},{18,... | collective-permute-start | bytes 835592 | tf_op jit(solution)/shard_map/ppermute | solution.py:492
  38.9 5.4 %collective-permute-done.6.refs_5_.refs_3_ = bf16[272,512]{1,0:T(8,128)(2,1)S(1)} collective-permute-done((bf16[272,512]{1,0:T(8,128)(2,1)S(1)}, bf16[272,512]{1,0:T(8,128)(2,1)S(1)}, u32[]{:S(2)}, u32[]{:S(2)}) %collective-permute-start.6) | collective-permute-done | bytes 278560 | tf_op jit(solution)/shard_map/ppermute | solution.py:491
  44.3 0.6 collective-permute-start.7
  44.9 0.0 collective-permute-done.8.refs_6_.refs_5_
  44.9 5.4 %shard_map.105 = (f32[8,8,128]{2,1,0:T(8,128)S(1)}, f32[11,128,128]{2,1,0:T(8,128)S(1)}) custom-call(bf16[272,512]{1,0:T(8,128)(2,1)S(1)} %shard_map.104.refs_0_, bf16[272,512]{1,0:T(8,128)(2,1)S(1)} %collective-permute-done.1.refs_1_, bf16[272,512]{1,0:T(8,128)(2,1)S(1)} %collective-permute-done.2.refs_2_.refs_7_, ...), custom_call_target="tpu_custom_call" | custom-call | tf_op jit(solution)/shard_map/pallas_call | solution.py:517
  50.3 0.0 copy-start.4
  50.3 0.6 collective-permute-done.7.refs_0_.refs_4_.refs_7_
  50.9 0.0 copy-done.2
  50.9 1.2 %shard_map.106 = (f32[8,8,8,128]{3,2,1,0:T(8,128)S(1)}, f32[2,128,128]{2,1,0:T(8,128)S(1)}) custom-call(bf16[272,512]{1,0:T(8,128)(2,1)S(1)} %collective-permute-done.7.refs_0_.refs_4_.refs_7_, bf16[272,512]{1,0:T(8,128)(2,1)S(1)} %get-tuple-element.43.refs_7_.refs_1_.refs_8_, bf16[272,512]{1,0:T(8,128)(2,1)S(1)} %collective-permute-done.5.refs_8_.refs_2_.refs_9_, ...), custom_call_target="tpu_custom_call" | custom-call | tf_op jit(solution)/shard_map/pallas_call | solution.py:517
  52.1 14.4 %all_to_all.15.refs_13_ = f32[8,8,8,128]{3,2,1,0:T(8,128)S(1)} all-to-all(f32[8,8,8,128]{3,2,1,0:T(8,128)S(1)} %get-tuple-element.51), channel_id=1, replica_groups={{0,2,4,6,8,10,12,14},{16,18,20,22,24,26,28,30},{32,34,36,38,40,42,44,46..., dimensions={0} | all-to-all | bytes 524288 | tf_op jit(solution)/shard_map/all_to_all | solution.py:529
  66.5 0.0 copy-done
  66.5 0.0 copy-done.3
  66.5 0.0 copy-done.4
  66.5 0.0 copy-start.1
  66.5 5.2 %shard_map.107 = (bf16[128,512]{1,0:T(8,128)(2,1)S(1)}, bf16[128,512]{1,0:T(8,128)(2,1)S(1)}, bf16[128,512]{1,0:T(8,128)(2,1)S(1)}, bf16[128,512]{1,0:T(8,128)(2...) custom-call(bf16[272,512]{1,0:T(8,128)(2,1)S(1)} %shard_map.104.refs, ...), custom_call_target="tpu_custom_call" | custom-call | tf_op jit(solution)/shard_map/pallas_call | solution.py:533
  71.7 0.2 collective-permute-start.9
  72.0 3.1 %collective-permute-start.10 = (bf16[128,512]{1,0:T(8,128)(2,1)S(1)}, bf16[128,512]{1,0:T(8,128)(2,1)S(1)}, u32[]{:S(2)}, u32[]{:S(2)}) collective-permute-start(bf16[128,512]{1,0:T(8,128)(2,1)S(1)} %get-tuple-element.54), channel_id=1, source_target_pairs={{0,14},{2,0},{4,2},{6,4},{8,6},{10,8},{12,10},{14,12},{16,30},{18,... | collective-permute-start | bytes 393224 | tf_op jit(solution)/shard_map/ppermute | solution.py:558
  75.0 0.0 copy-done.1
  75.0 3.7 %shard_map.108 = (f32[256,512]{1,0:T(8,128)S(1)}, bf16[128,1024]{1,0:T(8,128)(2,1)}) custom-call(bf16[272,512]{1,0:T(8,128)(2,1)S(1)} %shard_map.104.refs_0_, bf16[272,512]{1,0:T(8,128)(2,1)S(1)} %collective-permute-done.1.refs_1_, bf16[272,512]{1,0:T(8,128)(2,1)S(1)} %copy-done.1, bf16[272,512]{1,0:T(8,128)(2,1)S(1)} %collective-permute-done.3.refs_3_.refs_2_, ...), custom_call_target="tpu_custom_call" | custom-call | tf_op jit(solution)/shard_map/pallas_call | solution.py:562
  78.8 0.0 copy-start.5
  78.8 0.0 collective-permute-done.9
  78.8 0.0 collective-permute-done.10
  78.8 4.8 %all-to-all-start.2 = ((bf16[16,8,1024]{2,1,0:T(8,128)(2,1)}), bf16[16,8,1024]{2,1,0:T(8,128)(2,1)S(1)}, u32[]{:S(2)}, u32[]{:S(2)}) async-start(bf16[16,8,1024]{2,1,0:T(8,128)(2,1)} %bitcast.2), calls=%async_computation.2 | async-start | bytes 524288 | tf_op jit(solution)/shard_map/all_to_all | solution.py:578
  83.7 2.5 %collective-permute-start.12 = (bf16[128,512]{1,0:T(8,128)(2,1)S(1)}, bf16[128,512]{1,0:T(8,128)(2,1)S(1)}, u32[]{:S(2)}, u32[]{:S(2)}) collective-permute-start(bf16[128,512]{1,0:T(8,128)(2,1)S(1)} %add_convert_fusion.4), channel_id=1, source_target_pairs={{0,14},{2,0},{4,2},{6,4},{8,6},{10,8},{12,10},{14,12},{16,30},{18,... | collective-permute-start | bytes 393224 | tf_op jit(solution)/shard_map/ppermute | solution.py:558
  86.2 0.1 collective-permute-start.11
  86.3 0.7 collective-permute-start.16
  86.9 2.8 %collective-permute-done.12 = bf16[128,512]{1,0:T(8,128)(2,1)S(1)} collective-permute-done((bf16[128,512]{1,0:T(8,128)(2,1)S(1)}, bf16[128,512]{1,0:T(8,128)(2,1)S(1)}, u32[]{:S(2)}, u32[]{:S(2)}) %collective-permute-start.12) | collective-permute-done | bytes 131104 | tf_op jit(solution)/shard_map/ppermute | solution.py:558
  89.8 2.6 %collective-permute-done.11 = bf16[128,512]{1,0:T(8,128)(2,1)S(1)} collective-permute-done((bf16[128,512]{1,0:T(8,128)(2,1)S(1)}, bf16[128,512]{1,0:T(8,128)(2,1)S(1)}, u32[]{:S(2)}, u32[]{:S(2)}) %collective-permute-start.11) | collective-permute-done | bytes 131104 | tf_op jit(solution)/shard_map/ppermute | solution.py:555
  92.4 0.0 all-to-all-done.2.parts
  92.4 0.0 copy-start.6
  92.5 0.1 collective-permute-start.13
  92.6 3.3 %collective-permute-start.15 = (bf16[128,512]{1,0:T(8,128)(2,1)S(1)}, bf16[128,512]{1,0:T(8,128)(2,1)S(1)}, u32[]{:S(2)}, u32[]{:S(2)}) collective-permute-start(bf16[128,512]{1,0:T(8,128)(2,1)S(1)} %add_convert_fusion.1), channel_id=1, source_target_pairs={{0,14},{2,0},{4,2},{6,4},{8,6},{10,8},{12,10},{14,12},{16,30},{18,... | collective-permute-start | bytes 393224 | tf_op jit(solution)/shard_map/ppermute | solution.py:558
  95.9 2.8 %collective-permute-done.13 = bf16[128,512]{1,0:T(8,128)(2,1)S(1)} collective-permute-done((bf16[128,512]{1,0:T(8,128)(2,1)S(1)}, bf16[128,512]{1,0:T(8,128)(2,1)S(1)}, u32[]{:S(2)}, u32[]{:S(2)}) %collective-permute-start.13) | collective-permute-done | bytes 131104 | tf_op jit(solution)/shard_map/ppermute | solution.py:555
  98.8 0.1 collective-permute-start.14
  98.8 0.0 collective-permute-done.16.arrived
  98.9 0.0 copy-start.7
  98.9 0.0 copy-done.5
  98.9 0.0 copy-done.6
  98.9 0.7 copy-done.7
  99.6 2.2 %shard_map.109 = (bf16[128,512]{1,0:T(8,128)(2,1)}, bf16[128,512]{1,0:T(8,128)(2,1)}) custom-call(s32[8]{0:T(128)} %starts.3, s32[8]{0:T(128)} %slots.3, f32[256,512]{1,0:T(8,128)} %copy-done.5, bf16[256,512]{1,0:T(8,128)(2,1)} %copy-done.7, bf16[16,8,1024]{2,1,0:T(8,128)(2,1)} %copy-done.6), custom_call_target="tpu_custom_call" | custom-call | tf_op jit(solution)/shard_map/pallas_call | solution.py:585
  101.7 0.0 collective-permute-done.15
  101.7 3.3 %collective-permute-done.14 = bf16[128,512]{1,0:T(8,128)(2,1)S(1)} collective-permute-done((bf16[128,512]{1,0:T(8,128)(2,1)S(1)}, bf16[128,512]{1,0:T(8,128)(2,1)S(1)}, u32[]{:S(2)}, u32[]{:S(2)}) %collective-permute-start.14) | collective-permute-done | bytes 131104 | tf_op jit(solution)/shard_map/ppermute | solution.py:555
  105.0 0.7 add_convert_fusion
  (5 shorter events, 0.2 us)
Async XLA Ops:
  0.6 3.2 %collective-permute-start = (bf16[128,1024]{1,0:T(8,128)(2,1)}, bf16[128,1024]{1,0:T(8,128)(2,1)S(1)}, u32[]{:S(2)}, u32[]{:S(2)}) collective-permute-start(bf16[128,1024]{1,0:T(8,128)(2,1)} %grad_own.1), channel_id=1, source_target_pairs={{0,1},{1,0},{2,3},{3,2},{4,5},{5,4},{6,7},{7,6},{8,9},{9,8},{10,11... | collective-permute-start | bytes 786440 | tf_op jit(solution)/shard_map/ppermute | solution.py:454
  3.8 47.1 %copy-start.2 = (bf16[272,512]{1,0:T(8,128)(2,1)}, bf16[272,512]{1,0:T(8,128)(2,1)S(1)}, u32[]{:S(2)}) copy-start(bf16[272,512]{1,0:T(8,128)(2,1)S(1)} %get-tuple-element.43.refs_7_.refs_1_.refs_8_) | copy-start | bytes 835588
  5.7 21.2 %collective-permute-start.2 = (bf16[272,512]{1,0:T(8,128)(2,1)S(1)}, bf16[272,512]{1,0:T(8,128)(2,1)S(1)}, u32[]{:S(2)}, u32[]{:S(2)}) collective-permute-start(bf16[272,512]{1,0:T(8,128)(2,1)S(1)} %shard_map.104.refs_0_), channel_id=1, source_target_pairs={{0,2},{2,4},{4,6},{6,8},{8,10},{10,12},{12,14},{14,0},{16,18},{18,... | collective-permute-start | bytes 835592 | tf_op jit(solution)/shard_map/ppermute | solution.py:492
  7.7 19.2 %collective-permute-start.1 = (bf16[272,512]{1,0:T(8,128)(2,1)S(1)}, bf16[272,512]{1,0:T(8,128)(2,1)S(1)}, u32[]{:S(2)}, u32[]{:S(2)}) collective-permute-start(bf16[272,512]{1,0:T(8,128)(2,1)S(1)} %shard_map.104.refs_0_), channel_id=1, source_target_pairs={{0,14},{2,0},{4,2},{6,4},{8,6},{10,8},{12,10},{14,12},{16,30},{18,... | collective-permute-start | bytes 835592 | tf_op jit(solution)/shard_map/ppermute | solution.py:491
  11.7 15.2 %all-to-all-start = ((bf16[16,8,1024]{2,1,0:T(8,128)(2,1)}), bf16[16,8,1024]{2,1,0:T(8,128)(2,1)S(1)}, u32[]{:S(2)}, u32[]{:S(2)}) async-start(bf16[16,8,1024]{2,1,0:T(8,128)(2,1)} %get-tuple-element.40), calls=%async_computation | async-start | bytes 524288 | tf_op jit(solution)/shard_map/all_to_all | solution.py:495
  19.2 9.8 %collective-permute-start.5 = (bf16[272,512]{1,0:T(8,128)(2,1)S(1)}, bf16[272,512]{1,0:T(8,128)(2,1)S(1)}, u32[]{:S(2)}, u32[]{:S(2)}) collective-permute-start(bf16[272,512]{1,0:T(8,128)(2,1)S(1)} %get-tuple-element.43.refs_7_.refs_1_.refs_8_), channel_id=1, source_target_pairs={{8,24},{10,26},{12,28},{14,30},{24,40},{26,42},{28,44},{30,46},{40... | collective-permute-start | bytes 835592 | tf_op jit(solution)/shard_map/ppermute | solution.py:499
  26.9 39.7 %copy-start = (bf16[272,512]{1,0:T(8,128)(2,1)}, bf16[272,512]{1,0:T(8,128)(2,1)S(1)}, u32[]{:S(2)}) copy-start(bf16[272,512]{1,0:T(8,128)(2,1)S(1)} %collective-permute-done.2.refs_2_.refs_7_) | copy-start | bytes 835588
  26.9 7.6 %collective-permute-start.3 = (bf16[272,512]{1,0:T(8,128)(2,1)S(1)}, bf16[272,512]{1,0:T(8,128)(2,1)S(1)}, u32[]{:S(2)}, u32[]{:S(2)}) collective-permute-start(bf16[272,512]{1,0:T(8,128)(2,1)S(1)} %collective-permute-done.1.refs_1_), channel_id=1, source_target_pairs={{0,14},{2,0},{4,2},{6,4},{8,6},{10,8},{12,10},{14,12},{16,30},{18,... | collective-permute-start | bytes 835592 | tf_op jit(solution)/shard_map/ppermute | solution.py:491
  28.6 8.3 %collective-permute-start.4 = (bf16[272,512]{1,0:T(8,128)(2,1)S(1)}, bf16[272,512]{1,0:T(8,128)(2,1)S(1)}, u32[]{:S(2)}, u32[]{:S(2)}) collective-permute-start(bf16[272,512]{1,0:T(8,128)(2,1)S(1)} %collective-permute-done.2.refs_2_.refs_7_), channel_id=1, source_target_pairs={{0,2},{2,4},{4,6},{6,8},{8,10},{10,12},{12,14},{14,0},{16,18},{18,... | collective-permute-start | bytes 835592 | tf_op jit(solution)/shard_map/ppermute | solution.py:492
  29.0 37.5 %copy-start.3 = (bf16[272,512]{1,0:T(8,128)(2,1)}, bf16[272,512]{1,0:T(8,128)(2,1)S(1)}, u32[]{:S(2)}) copy-start(bf16[272,512]{1,0:T(8,128)(2,1)S(1)} %collective-permute-done.5.refs_8_.refs_2_.refs_9_) | copy-start | bytes 835588
  36.9 7.5 %collective-permute-start.6 = (bf16[272,512]{1,0:T(8,128)(2,1)S(1)}, bf16[272,512]{1,0:T(8,128)(2,1)S(1)}, u32[]{:S(2)}, u32[]{:S(2)}) collective-permute-start(bf16[272,512]{1,0:T(8,128)(2,1)S(1)} %collective-permute-done.3.refs_3_.refs_2_), channel_id=1, source_target_pairs={{0,14},{2,0},{4,2},{6,4},{8,6},{10,8},{12,10},{14,12},{16,30},{18,... | collective-permute-start | bytes 835592 | tf_op jit(solution)/shard_map/ppermute | solution.py:491
  37.1 7.8 %collective-permute-start.8 = (bf16[272,512]{1,0:T(8,128)(2,1)S(1)}, bf16[272,512]{1,0:T(8,128)(2,1)S(1)}, u32[]{:S(2)}, u32[]{:S(2)}) collective-permute-start(bf16[272,512]{1,0:T(8,128)(2,1)S(1)} %collective-permute-done.4.refs_4_.refs_6_), channel_id=1, source_target_pairs={{0,2},{2,4},{4,6},{6,8},{8,10},{10,12},{12,14},{14,0},{16,18},{18,... | collective-permute-start | bytes 835592 | tf_op jit(solution)/shard_map/ppermute | solution.py:492
  44.3 6.5 %collective-permute-start.7 = (bf16[272,512]{1,0:T(8,128)(2,1)S(1)}, bf16[272,512]{1,0:T(8,128)(2,1)S(1)}, u32[]{:S(2)}, u32[]{:S(2)}) collective-permute-start(bf16[272,512]{1,0:T(8,128)(2,1)S(1)} %collective-permute-done.6.refs_5_.refs_3_), channel_id=1, source_target_pairs={{0,14},{2,0},{4,2},{6,4},{8,6},{10,8},{12,10},{14,12},{16,30},{18,... | collective-permute-start | bytes 835592 | tf_op jit(solution)/shard_map/ppermute | solution.py:502
  50.3 16.2 %copy-start.4 = (f32[11,128,128]{2,1,0:T(8,128)}, f32[11,128,128]{2,1,0:T(8,128)S(1)}, u32[]{:S(2)}) copy-start(f32[11,128,128]{2,1,0:T(8,128)S(1)} %get-tuple-element.48.refs_11_) | copy-start | bytes 2162692
  66.5 8.5 %copy-start.1 = (bf16[272,512]{1,0:T(8,128)(2,1)S(1)}, bf16[272,512]{1,0:T(8,128)(2,1)}, u32[]{:S(2)}) copy-start(bf16[272,512]{1,0:T(8,128)(2,1)} %copy-done) | copy-start | bytes 835588
  71.7 7.1 %collective-permute-start.9 = (bf16[128,512]{1,0:T(8,128)(2,1)S(1)}, bf16[128,512]{1,0:T(8,128)(2,1)S(1)}, u32[]{:S(2)}, u32[]{:S(2)}) collective-permute-start(bf16[128,512]{1,0:T(8,128)(2,1)S(1)} %get-tuple-element.53), channel_id=1, source_target_pairs={{0,2},{2,4},{4,6},{6,8},{8,10},{10,12},{12,14},{14,0},{16,18},{18,... | collective-permute-start | bytes 393224 | tf_op jit(solution)/shard_map/ppermute | solution.py:555
  72.0 6.8 %collective-permute-start.10 = (bf16[128,512]{1,0:T(8,128)(2,1)S(1)}, bf16[128,512]{1,0:T(8,128)(2,1)S(1)}, u32[]{:S(2)}, u32[]{:S(2)}) collective-permute-start(bf16[128,512]{1,0:T(8,128)(2,1)S(1)} %get-tuple-element.54), channel_id=1, source_target_pairs={{0,14},{2,0},{4,2},{6,4},{8,6},{10,8},{12,10},{14,12},{16,30},{18,... | collective-permute-start | bytes 393224 | tf_op jit(solution)/shard_map/ppermute | solution.py:558
  78.8 20.1 %copy-start.5 = (f32[256,512]{1,0:T(8,128)}, f32[256,512]{1,0:T(8,128)S(1)}, u32[]{:S(2)}) copy-start(f32[256,512]{1,0:T(8,128)S(1)} %get-tuple-element.68.own_grad) | copy-start | bytes 1572868
  78.8 13.6 %all-to-all-start.2 = ((bf16[16,8,1024]{2,1,0:T(8,128)(2,1)}), bf16[16,8,1024]{2,1,0:T(8,128)(2,1)S(1)}, u32[]{:S(2)}, u32[]{:S(2)}) async-start(bf16[16,8,1024]{2,1,0:T(8,128)(2,1)} %bitcast.2), calls=%async_computation.2 | async-start | bytes 524288 | tf_op jit(solution)/shard_map/all_to_all | solution.py:578
  83.7 6.1 %collective-permute-start.12 = (bf16[128,512]{1,0:T(8,128)(2,1)S(1)}, bf16[128,512]{1,0:T(8,128)(2,1)S(1)}, u32[]{:S(2)}, u32[]{:S(2)}) collective-permute-start(bf16[128,512]{1,0:T(8,128)(2,1)S(1)} %add_convert_fusion.4), channel_id=1, source_target_pairs={{0,14},{2,0},{4,2},{6,4},{8,6},{10,8},{12,10},{14,12},{16,30},{18,... | collective-permute-start | bytes 393224 | tf_op jit(solution)/shard_map/ppermute | solution.py:558
  86.2 6.3 %collective-permute-start.11 = (bf16[128,512]{1,0:T(8,128)(2,1)S(1)}, bf16[128,512]{1,0:T(8,128)(2,1)S(1)}, u32[]{:S(2)}, u32[]{:S(2)}) collective-permute-start(bf16[128,512]{1,0:T(8,128)(2,1)S(1)} %add_convert_fusion.5), channel_id=1, source_target_pairs={{0,2},{2,4},{4,6},{6,8},{8,10},{10,12},{12,14},{14,0},{16,18},{18,... | collective-permute-start | bytes 393224 | tf_op jit(solution)/shard_map/ppermute | solution.py:555
  86.3 12.6 %collective-permute-start.16 = (bf16[256,512]{1,0:T(8,128)(2,1)S(1)}, bf16[256,512]{1,0:T(8,128)(2,1)S(1)}, u32[]{:S(2)}, u32[]{:S(2)}) collective-permute-start(bf16[256,512]{1,0:T(8,128)(2,1)S(1)} %get-tuple-element.69), channel_id=1, source_target_pairs={{24,8},{26,10},{28,12},{30,14},{40,24},{42,26},{44,28},{46,30},{56... | collective-permute-start | bytes 786440 | tf_op jit(solution)/shard_map/ppermute | solution.py:561
  92.4 6.5 %copy-start.6 = (bf16[16,8,1024]{2,1,0:T(8,128)(2,1)}, bf16[16,8,1024]{2,1,0:T(8,128)(2,1)S(1)}, u32[]{:S(2)}) copy-start(bf16[16,8,1024]{2,1,0:T(8,128)(2,1)S(1)} %all-to-all-done.2.parts) | copy-start | bytes 786436
  92.5 6.3 %collective-permute-start.13 = (bf16[128,512]{1,0:T(8,128)(2,1)S(1)}, bf16[128,512]{1,0:T(8,128)(2,1)S(1)}, u32[]{:S(2)}, u32[]{:S(2)}) collective-permute-start(bf16[128,512]{1,0:T(8,128)(2,1)S(1)} %add_convert_fusion.3), channel_id=1, source_target_pairs={{0,2},{2,4},{4,6},{6,8},{8,10},{10,12},{12,14},{14,0},{16,18},{18,... | collective-permute-start | bytes 393224 | tf_op jit(solution)/shard_map/ppermute | solution.py:555
  92.6 9.1 %collective-permute-start.15 = (bf16[128,512]{1,0:T(8,128)(2,1)S(1)}, bf16[128,512]{1,0:T(8,128)(2,1)S(1)}, u32[]{:S(2)}, u32[]{:S(2)}) collective-permute-start(bf16[128,512]{1,0:T(8,128)(2,1)S(1)} %add_convert_fusion.1), channel_id=1, source_target_pairs={{0,14},{2,0},{4,2},{6,4},{8,6},{10,8},{12,10},{14,12},{16,30},{18,... | collective-permute-start | bytes 393224 | tf_op jit(solution)/shard_map/ppermute | solution.py:558
  98.8 6.3 %collective-permute-start.14 = (bf16[128,512]{1,0:T(8,128)(2,1)S(1)}, bf16[128,512]{1,0:T(8,128)(2,1)S(1)}, u32[]{:S(2)}, u32[]{:S(2)}) collective-permute-start(bf16[128,512]{1,0:T(8,128)(2,1)S(1)} %add_convert_fusion.2), channel_id=1, source_target_pairs={{0,2},{2,4},{4,6},{6,8},{8,10},{10,12},{12,14},{14,0},{16,18},{18,... | collective-permute-start | bytes 393224 | tf_op jit(solution)/shard_map/ppermute | solution.py:555
  98.9 0.7 copy-start.7

commit v5 on v4

--- a/solution.py
+++ b/solution.py
@@ -45,7 +45,9 @@
 ROW_DOWN = [(dst, src) for src, dst in ROW_UP]
 EARLY = (0, 1, 7, 2, 6, 3, 5)
 LATE = (4,)
-ORDER = EARLY + LATE
+LEADING = (4, 5)
+TRAILING = (3, 6, 2, 7, 1, 0)
+ORDER = LEADING + TRAILING
 TOGETHER = 2
 
 VMEM_LIMIT = 50 * 2**20
@@ -279,12 +281,13 @@
     merged[:, HEADS_HERE:, :] = mean / total
 
 
-def query_grad_kernel(*refs):
-    order = ORDER
+def query_grad_kernel(order, *refs):
+    count = len(order)
+    merging = order is LEADING
     near = [o for o in order if o <= REACH]
-    chunks, refs = refs[:NZ], refs[NZ:]
-    own, previous, sums, bias_most, bias_last, stats_in, *refs = refs
-    query_grads, (coarse_out, window_out, previous_grad), refs = refs[:NZ], refs[NZ : NZ + 3], refs[NZ + 3 :]
+    chunks, (own, previous, sums, bias_most, bias_last, stats_in), refs = refs[:count], refs[count : count + 6], refs[count + 6 :]
+    query_grads, (coarse_out, window_out), refs = refs[:count], refs[count : count + 2], refs[count + 2 :]
+    merged_out, refs = (refs[0], refs[1:]) if merging else (None, refs)
     packed, pairs, keys, bias, stats, merged, coarse, window, *refs = refs
     key_sems, chunk_sems, bias_sems, stats_sem, out_sems = refs
     stats_copy = pltpu.make_async_copy(stats_in, stats, stats_sem)
@@ -292,7 +295,7 @@
     key_copies = load_keys(own, previous, sums, pairs, keys, key_sems)
     copies = []
     for i, o in enumerate(order):
-        mine = [pltpu.make_async_copy(chunks[o], packed.at[o], chunk_sems.at[o])]
+        mine = [pltpu.make_async_copy(chunks[i], packed.at[o], chunk_sems.at[o])]
         for block in bias_blocks((o,)):
             source, among = (bias_most, EARLY) if o in EARLY else (bias_last, LATE)
             source = source.at[bias_blocks(among).index(block)]
@@ -301,7 +304,11 @@
             copy.start()
         copies.append(mine)
     stats_copy.wait()
-    merge_stats(stats, merged)
+    if merging:
+        merge_stats(stats, merged)
+        merged_out[...] = merged[...]
+    else:
+        merged = stats
     for copy in key_copies:
         copy.wait()
     _, z = place()
@@ -313,8 +320,7 @@
         for h in range(HEADS_HERE)
     ]
     writes = []
-    others = [[None, None] for _ in range(HEADS_HERE)]
-    for first in range(0, NZ, TOGETHER):
+    for first in range(0, count, TOGETHER):
         group = range(first, first + TOGETHER)
         for i in group:
             for copy in copies[i]:
@@ -337,19 +343,11 @@
                 turned = jnp.concatenate([side, turned], axis=1)
             dquery = jnp.dot(turned, dscores, preferred_element_type=F32)
             turned = jnp.transpose(SCALE * dquery)
-            query_grads[o][:, h * HD : (h + 1) * HD] = turned.astype(BF16)
+            query_grads[i][:, h * HD : (h + 1) * HD] = turned.astype(BF16)
         for (i, o, h), (dscores, probs_low) in zip(units, low_parts):
             if o <= REACH:
                 window[near.index(o), 0, h] = dscores[0:TOK]
                 window[near.index(o), 1, h] = probs_low[0:TOK]
-            if 0 < o <= REACH:
-                wraps = (z + o >= NZ).astype(F32)
-                cols = slice(h * HD, (h + 1) * HD)
-                for kind, left in enumerate((dscores, probs_low)):
-                    right = packed[o, kind * TOK : (kind + 1) * TOK, cols]
-                    part = wraps * jnp.dot(left[0:TOK], right, preferred_element_type=F32)
-                    old = others[h][kind]
-                    others[h][kind] = part if old is None else old + part
             coarse[i, 0, h] = dscores[-TOK:]
             coarse[i, 1, h] = probs_low[-TOK:]
         for i in group:
@@ -362,10 +360,6 @@
                     pltpu.make_async_copy(window.at[at], window_out.at[at], out_sems.at[1, o])
                 )
                 writes[-1].start()
-    for h in range(HEADS_HERE):
-        cols = slice(h * HD, (h + 1) * HD)
-        previous_grad[0:TOK, cols] = (others[h][0] * SCALE).astype(BF16)
-        previous_grad[TOK : 2 * TOK, cols] = others[h][1].astype(BF16)
     for copy in writes:
         copy.wait()
 
@@ -373,21 +367,25 @@
 def key_grad_kernel(*refs):
     order = ORDER
     near = [o for o in order if o <= REACH]
-    chunks, (coarse_in, window_in), refs = refs[:NZ], refs[NZ : NZ + 2], refs[NZ + 2 :]
-    own_grad, sum_grad, packed, coarse, window, sems = refs
+    chunks, coarse_in, window_in, refs = refs[:NZ], refs[NZ : NZ + 2], refs[NZ + 2 : NZ + 4], refs[NZ + 4 :]
+    previous_grad, own_grad, sum_grad, packed, coarse, window, sems = refs
     copies = []
     for i, o in enumerate(order):
+        part, group = (0, LEADING) if o in LEADING else (1, TRAILING)
         mine = [pltpu.make_async_copy(chunks[i], packed.at[i], sems.at[0, i])]
-        mine.append(pltpu.make_async_copy(coarse_in.at[i], coarse.at[i], sems.at[1, i]))
+        source = coarse_in[part].at[group.index(o)]
+        mine.append(pltpu.make_async_copy(source, coarse.at[i], sems.at[1, i]))
         if o in near:
-            at = near.index(o)
-            mine.append(pltpu.make_async_copy(window_in.at[at], window.at[at], sems.at[2, i]))
+            source = window_in[part].at[[n for n in group if n <= REACH].index(o)]
+            target = window.at[near.index(o)]
+            mine.append(pltpu.make_async_copy(source, target, sems.at[2, i]))
         for copy in mine:
             copy.start()
         copies.append(mine)
     _, z = place()
     units = [(h, kind) for h in range(HEADS_HERE) for kind in range(2)]
-    totals, mine = [None] * len(units), [None] * len(units)
+    zero = jnp.zeros((TOK, HD), F32)
+    totals, mine, others = [None] * len(units), [zero] * len(units), [zero] * len(units)
     half = NZ // 2
     for first in range(0, NZ, half):
         group = range(first, first + half)
@@ -410,12 +408,16 @@
                         tokens[i - first],
                         preferred_element_type=F32,
                     )
-                    part = part * (z + order[i] < NZ).astype(F32)
-                    mine[unit] = part if mine[unit] is None else mine[unit] + part
+                    wraps = (z + order[i] >= NZ).astype(F32)
+                    mine[unit] = mine[unit] + part * (1.0 - wraps)
+                    if order[i] > 0:
+                        others[unit] = others[unit] + part * wraps
     for unit, (h, kind) in enumerate(units):
         scale = SCALE if kind == 0 else 1.0
         at = (2 * h + kind) * HD
-        own_grad[kind * TOK : (kind + 1) * TOK, h * HD : (h + 1) * HD] = mine[unit] * scale
+        here = (slice(kind * TOK, (kind + 1) * TOK), slice(h * HD, (h + 1) * HD))
+        own_grad[here] = mine[unit] * scale
+        previous_grad[here] = (others[unit] * scale).astype(BF16)
         sum_grad[:, at : at + HD] = (totals[unit] * scale).astype(BF16)
 
 
@@ -528,28 +530,34 @@
 
     stats = lax.all_to_all(stats, "seq", 0, 0, axis_index_groups=Z_GROUPS)
 
-    coarse_shape = (NZ, 2, HEADS_HERE, bars, TOK)
-    window_shape = (REACH + 1, 2, HEADS_HERE, TOK, TOK)
-    *grads, coarse, window, previous_grad = pl.pallas_call(
-        query_grad_kernel,
-        out_shape=(shape((TOK, FEAT)),) * NZ
-        + (shape(coarse_shape), shape(window_shape), shape((2 * TOK, FEAT))),
-        in_specs=[whole(HBM)] * (NZ + 6),
-        out_specs=(whole(VMEM),) * NZ + (whole(HBM),) * 2 + (whole(VMEM),),
-        scratch_shapes=held
-        + [
-            VMEM(stats_shape, F32),
-            VMEM(stats_shape[1:], F32),
-            VMEM(coarse_shape, BF16),
-            VMEM(window_shape, BF16),
-            dma((3,)),
-            dma((NZ,)),
-            dma(bias_shape[:1]),
-            dma,
-            dma((2, NZ)),
-        ],
-        compiler_params=params,
-    )(*chunks, own, previous, all_sums, bias_most, bias_last, stats)
+    def query_grads(order, stats):
+        merging = order is LEADING
+        near = sum(o <= REACH for o in order)
+        coarse_shape = (len(order), 2, HEADS_HERE, bars, TOK)
+        window_shape = (near, 2, HEADS_HERE, TOK, TOK)
+        made = pl.pallas_call(
+            lambda *refs: query_grad_kernel(order, *refs),
+            out_shape=(shape((TOK, FEAT)),) * len(order)
+            + (shape(coarse_shape), shape(window_shape))
+            + (shape(stats_shape[1:], F32),) * merging,
+            in_specs=[whole(HBM)] * (len(order) + 6),
+            out_specs=(whole(VMEM),) * len(order) + (whole(HBM),) * 2 + (whole(VMEM),) * merging,
+            scratch_shapes=held
+            + [
+                VMEM(stats.shape, F32),
+                VMEM(stats_shape[1:], F32),
+                VMEM(coarse_shape, BF16),
+                VMEM(window_shape, BF16),
+                dma((3,)),
+                dma((NZ,)),
+                dma(bias_shape[:1]),
+                dma,
+                dma((2, NZ)),
+            ],
+            compiler_params=params,
+        )(*[chunks[o] for o in order], own, previous, all_sums, bias_most, bias_last, stats)
+        *grads, coarse, window, merged = made if merging else (*made, None)
+        return dict(zip(order, grads)), coarse, window, merged
 
     def forward_step(array):
         return lax.ppermute(array, "seq", TO_NEXT)
@@ -557,29 +565,36 @@
     def backward_step(array):
         return lax.ppermute(array, "seq", TO_PREVIOUS)
 
+    grads, coarse_a, window_a, merged = query_grads(LEADING, stats)
     forward, backward = forward_step(grads[4]), backward_step(grads[5])
-    arrived = lax.ppermute(previous_grad, "seq", ROW_DOWN)
-    own_grad, sum_grad = pl.pallas_call(
+    more, coarse_b, window_b, _ = query_grads(TRAILING, merged)
+    grads.update(more)
+    forward, backward, coarse_b = lax.optimization_barrier((forward, backward, coarse_b))
+    forward, backward = forward_step(add_low(forward, grads[3])), backward_step(add_low(backward, grads[6]))
+    previous_grad, own_grad, sum_grad = pl.pallas_call(
         key_grad_kernel,
-        out_shape=(shape((2 * TOK, FEAT), F32), shape((bars, 2 * FEAT))),
-        in_specs=[whole(HBM)] * (NZ + 2),
-        out_specs=(whole(VMEM),) * 2,
+        out_shape=(
+            shape((2 * TOK, FEAT)),
+            shape((2 * TOK, FEAT), F32),
+            shape((bars, 2 * FEAT)),
+        ),
+        in_specs=[whole(HBM)] * (NZ + 4),
+        out_specs=(whole(VMEM),) * 3,
         scratch_shapes=[
             VMEM((NZ, ROWS, FEAT), BF16),
-            VMEM(coarse_shape, BF16),
-            VMEM(window_shape, BF16),
+            VMEM((NZ, 2, HEADS_HERE, bars, TOK), BF16),
+            VMEM((REACH + 1, 2, HEADS_HERE, TOK, TOK), BF16),
             dma((3, NZ)),
         ],
         compiler_params=params,
-    )(*[chunks[o] for o in ORDER], coarse, window)
-
+    )(*[chunks[o] for o in ORDER], coarse_a, coarse_b, window_a, window_b)
     forward, backward, sum_grad = lax.optimization_barrier((forward, backward, sum_grad))
-    forward, backward = forward_step(add_low(forward, grads[3])), backward_step(add_low(backward, grads[6]))
+    forward = forward_step(forward.astype(F32) + grads[2].astype(F32))
+    backward = backward_step(backward.astype(F32) + grads[7].astype(F32))
+    arrived = lax.ppermute(previous_grad, "seq", ROW_DOWN)
     parts = lax.all_to_all(
         sum_grad.reshape(NXY, BARS_HERE, 2 * FEAT), "seq", 0, 0, axis_index_groups=XY_GROUPS
     )
-    forward, backward, parts = lax.optimization_barrier((forward, backward, parts))
-    forward, backward = forward_step(add_low(forward, grads[2])), backward_step(add_low(backward, grads[7]))
     forward = forward_step(add_low(forward, grads[1]))
 
     grad_keys, grad_values = pl.pallas_call(

time: 106 us -> 104 us (0.981)
  waiting for transfers between devices: 32.5 us -> 26.2 us
  starting transfers between devices: 33.8 us -> 35.7 us
    ppermute x4, waiting for transfers between devices: 8.77 us -> 3.34 us  [forward_step(): return lax.ppermute(array, 'seq', TO_NEXT)]
    ppermute x3, waiting for transfers between devices: 2.84 us -> 0.01 us  [backward_step(): return lax.ppermute(array, 'seq', TO_PREVIOUS)]
    all_to_all x1, waiting for transfers between devices: 0.01 us -> 1.83 us  [shards(): lax.all_to_all(sum_grad.reshape(NXY, BARS_HERE, 2 * FEAT), 'seq', 0, 0, a...]
    ppermute x3, starting transfers between devices: 8.83 us -> 10.6 us  [backward_step(): return lax.ppermute(array, 'seq', TO_PREVIOUS)]
    pallas_call x2 -> x3, Pallas kernels: 8.92 us -> 9.85 us  [the longest x2 6.15 us: query_grads(): pl.pallas_call(lambda *refs: query_grad_kernel(order, *refs), out_shape=(...]
  transfers between devices with their start and end apart: 19 -> 19, of which waited for: 9 -> 8; matrix products, arithmetic and copies ran while one was open for 0% -> 0% of each run, Pallas kernels for 14% -> 18%
where the time goes in v5:
time: 104 us; the launch traced here: 103 us
  starting transfers between devices  35.7 us (34%)
  waiting for transfers between devices  26.2 us (25%)
  Pallas kernels  23.4 us (22%)
  blocking collectives  14.7 us (14%)
  local copies, waits for them, and re-layouts  1.53 us (1%)
    all_to_all x1, blocking collectives, shards(): stats = lax.all_to_all(stats, 'seq', 0, 0, axis_index_groups=Z_GROUPS)  14.7 us
    ppermute x3, waiting for transfers between devices, ring_step(): after.append(lax.ppermute(after[-1], 'seq', TO_PREVIOUS))  11 us
    ppermute x3, starting transfers between devices, backward_step(): return lax.ppermute(array, 'seq', TO_PREVIOUS)  10.6 us
    all_to_all x1, starting transfers between devices, shards(): all_sums = lax.all_to_all(sums, 'seq', 0, 0, axis_index_groups=XY_GROUPS)  7.48 us
    all_to_all x1, waiting for transfers between devices, shards(): all_sums = lax.all_to_all(sums, 'seq', 0, 0, axis_index_groups=XY_GROUPS)  7.02 us
    pallas_call x2, Pallas kernels, stats_of(): pl.pallas_call(lambda *refs: stats_kernel(order, *refs), out_shape=out +...  6.58 us
    pallas_call x2, Pallas kernels, query_grads(): pl.pallas_call(lambda *refs: query_grad_kernel(order, *refs), out_shape=(...  6.15 us
    ppermute x3, starting transfers between devices, ring_step(): after.append(lax.ppermute(after[-1], 'seq', TO_PREVIOUS))  5.96 us
  transfers between devices with their start and end apart: 19, of which 8 were waited for; matrix products, arithmetic and copies ran while one was open for 0% of the time, Pallas kernels for 18%

profile of v5, /device:TPU:2, one launch (start us, length us, event | category | flops | bytes accessed | tf_op | source)
XLA Modules:
  0.0 103.1 jit_solution(4057286658051945078)
XLA Ops:
  0.6 0.1 collective-permute-start
  0.7 3.1 %shard_map.103 = (f32[512,128]{1,0:T(8,128)S(1)}, bf16[272,512]{1,0:T(8,128)(2,1)S(1)}, bf16[272,512]{1,0:T(8,128)(2,1)S(1)}, bf16[16,8,1024]{2,1,0:T(8,128)(2,1)}) custom-call(s32[1]{0:T(128)} %bitcast.core, s32[8]{0:T(128)} %starts.3, s32[8,8]{1,0:T(8,128)} %related.1, s32[8]{0:T(128)} %slots.3, bf16[128,512]{1,0:T(8,128)(2,1)} %queries.1, ...), custom_call_target="tpu_custom_call" | custom-call | tf_op jit(solution)/shard_map/pallas_call | solution.py:459
  3.8 0.0 collective-permute-done.grad_other
  3.8 1.7 %shard_map.104.refs_0_.refs_5_.refs_7_ = bf16[272,512]{1,0:T(8,128)(2,1)S(1)} custom-call(s32[1]{0:T(128)} %bitcast.core, bf16[272,512]{1,0:T(8,128)(2,1)S(1)} %get-tuple-element.41.pack, f32[512,128]{1,0:T(8,128)S(1)} %get-tuple-element.42.partial, bf16[128,1024]{1,0:T(8,128)(2,1)S(1)} %collective-permute-done.grad_other, bf16[512,2048]{1,0:T(8,128)(2,1)} %out_weight.3), custom_call_target="tpu_custom_call" | custom-call | tf_op jit(solution)/shard_map/pallas_call | solution.py:476
  5.6 2.0 %collective-permute-start.2 = (bf16[272,512]{1,0:T(8,128)(2,1)S(1)}, bf16[272,512]{1,0:T(8,128)(2,1)S(1)}, u32[]{:S(2)}, u32[]{:S(2)}) collective-permute-start(bf16[272,512]{1,0:T(8,128)(2,1)S(1)} %shard_map.104.refs_0_.refs_5_.refs_7_), channel_id=1, source_target_pairs={{0,2},{2,4},{4,6},{6,8},{8,10},{10,12},{12,14},{14,0},{16,18},{18,... | collective-permute-start | bytes 835592 | tf_op jit(solution)/shard_map/ppermute | solution.py:494
  7.6 4.0 %collective-permute-start.1 = (bf16[272,512]{1,0:T(8,128)(2,1)S(1)}, bf16[272,512]{1,0:T(8,128)(2,1)S(1)}, u32[]{:S(2)}, u32[]{:S(2)}) collective-permute-start(bf16[272,512]{1,0:T(8,128)(2,1)S(1)} %shard_map.104.refs_0_.refs_5_.refs_7_), channel_id=1, source_target_pairs={{0,14},{2,0},{4,2},{6,4},{8,6},{10,8},{12,10},{14,12},{16,30},{18,... | collective-permute-start | bytes 835592 | tf_op jit(solution)/shard_map/ppermute | solution.py:493
  11.6 7.5 %all-to-all-start = ((bf16[16,8,1024]{2,1,0:T(8,128)(2,1)}), bf16[16,8,1024]{2,1,0:T(8,128)(2,1)S(1)}, u32[]{:S(2)}, u32[]{:S(2)}) async-start(bf16[16,8,1024]{2,1,0:T(8,128)(2,1)} %get-tuple-element.43), calls=%async_computation | async-start | bytes 524288 | tf_op jit(solution)/shard_map/all_to_all | solution.py:497
  19.1 0.7 collective-permute-start.5
  19.7 7.0 %all-to-all-done = bf16[16,8,1024]{2,1,0:T(8,128)(2,1)S(1)} async-done(((bf16[16,8,1024]{2,1,0:T(8,128)(2,1)}), bf16[16,8,1024]{2,1,0:T(8,128)(2,1)S(1)}, u32[]{:S(2)}, u32[]{:S(2)}) %all-to-all-start) | async-done | bytes 262176 | tf_op jit(solution)/shard_map/all_to_all | solution.py:497
  26.8 0.0 collective-permute-done.2.refs_2_.refs_3_.refs_5_
  26.8 0.0 collective-permute-done.1.refs_1_.refs_4_.refs_6_
  26.8 1.7 %collective-permute-start.3 = (bf16[272,512]{1,0:T(8,128)(2,1)S(1)}, bf16[272,512]{1,0:T(8,128)(2,1)S(1)}, u32[]{:S(2)}, u32[]{:S(2)}) collective-permute-start(bf16[272,512]{1,0:T(8,128)(2,1)S(1)} %collective-permute-done.1.refs_1_.refs_4_.refs_6_), channel_id=1, source_target_pairs={{0,14},{2,0},{4,2},{6,4},{8,6},{10,8},{12,10},{14,12},{16,30},{18,... | collective-permute-start | bytes 835592 | tf_op jit(solution)/shard_map/ppermute | solution.py:493
  28.4 0.4 collective-permute-start.4
  28.8 0.0 collective-permute-done.5.refs_8_.refs_2_.refs_3_.refs_7_
  28.8 5.5 %collective-permute-done.3.refs_3_.refs_2_.refs_4_ = bf16[272,512]{1,0:T(8,128)(2,1)S(1)} collective-permute-done((bf16[272,512]{1,0:T(8,128)(2,1)S(1)}, bf16[272,512]{1,0:T(8,128)(2,1)S(1)}, u32[]{:S(2)}, u32[]{:S(2)}) %collective-permute-start.3) | collective-permute-done | bytes 278560 | tf_op jit(solution)/shard_map/ppermute | solution.py:493
  34.3 2.4 %collective-permute-done.4.refs_4_.refs_1_.refs_3_ = bf16[272,512]{1,0:T(8,128)(2,1)S(1)} collective-permute-done((bf16[272,512]{1,0:T(8,128)(2,1)S(1)}, bf16[272,512]{1,0:T(8,128)(2,1)S(1)}, u32[]{:S(2)}, u32[]{:S(2)}) %collective-permute-start.4) | collective-permute-done | bytes 278560 | tf_op jit(solution)/shard_map/ppermute | solution.py:494
  36.7 0.3 collective-permute-start.6
  37.0 1.7 %collective-permute-start.7 = (bf16[272,512]{1,0:T(8,128)(2,1)S(1)}, bf16[272,512]{1,0:T(8,128)(2,1)S(1)}, u32[]{:S(2)}, u32[]{:S(2)}) collective-permute-start(bf16[272,512]{1,0:T(8,128)(2,1)S(1)} %collective-permute-done.4.refs_4_.refs_1_.refs_3_), channel_id=1, source_target_pairs={{0,2},{2,4},{4,6},{6,8},{8,10},{10,12},{12,14},{14,0},{16,18},{18,... | collective-permute-start | bytes 835592 | tf_op jit(solution)/shard_map/ppermute | solution.py:494
  38.7 5.4 %collective-permute-done.6.refs_5_.refs_0_.refs_2_ = bf16[272,512]{1,0:T(8,128)(2,1)S(1)} collective-permute-done((bf16[272,512]{1,0:T(8,128)(2,1)S(1)}, bf16[272,512]{1,0:T(8,128)(2,1)S(1)}, u32[]{:S(2)}, u32[]{:S(2)}) %collective-permute-start.6) | collective-permute-done | bytes 278560 | tf_op jit(solution)/shard_map/ppermute | solution.py:493
  44.2 0.6 collective-permute-start.8
  44.7 0.0 collective-permute-done.7.refs_6_.refs_1_
  44.7 5.4 %shard_map.105 = (f32[8,8,128]{2,1,0:T(8,128)S(1)}, f32[11,128,128]{2,1,0:T(8,128)S(1)}) custom-call(bf16[272,512]{1,0:T(8,128)(2,1)S(1)} %shard_map.104.refs_0_.refs_5_.refs_7_, bf16[272,512]{1,0:T(8,128)(2,1)S(1)} %collective-permute-done.1.refs_1_.refs_4_.refs_6_, bf16[272,512]{1,0:T(8,128)(2,1)S(1)} %collective-permute-done.2.refs_2_.refs_3_.refs_5_, ...), custom_call_target="tpu_custom_call" | custom-call | tf_op jit(solution)/shard_map/pallas_call | solution.py:519
  50.1 0.0 copy-start
  50.1 0.6 collective-permute-done.8.refs_0_
  50.7 1.2 %shard_map.106 = (f32[8,8,8,128]{3,2,1,0:T(8,128)S(1)}, f32[2,128,128]{2,1,0:T(8,128)S(1)}) custom-call(bf16[272,512]{1,0:T(8,128)(2,1)S(1)} %collective-permute-done.8.refs_0_, bf16[272,512]{1,0:T(8,128)(2,1)S(1)} %get-tuple-element.46.refs_7_.refs_1_.refs_2_.refs_6_, bf16[272,512]{1,0:T(8,128)(2,1)S(1)} %collective-permute-done.5.refs_8_.refs_2_.refs_3_.refs_7_, ...), custom_call_target="tpu_custom_call" | custom-call | tf_op jit(solution)/shard_map/pallas_call | solution.py:519
  51.9 14.7 %all_to_all.15.refs_7_ = f32[8,8,8,128]{3,2,1,0:T(8,128)S(1)} all-to-all(f32[8,8,8,128]{3,2,1,0:T(8,128)S(1)} %get-tuple-element.54), channel_id=1, replica_groups={{0,2,4,6,8,10,12,14},{16,18,20,22,24,26,28,30},{32,34,36,38,40,42,44,46..., dimensions={0} | all-to-all | bytes 524288 | tf_op jit(solution)/shard_map/all_to_all | solution.py:531
  66.6 1.8 %shard_map.107 = (bf16[128,512]{1,0:T(8,128)(2,1)S(1)}, bf16[128,512]{1,0:T(8,128)(2,1)S(1)}, bf16[2,2,4,128,128]{4,3,2,1,0:T(8,128)(2,1)S(1)}, bf16[1,2,4,128,128]{4,3,2,1,0:T(8,128)(2,1)S(1)}, f32[8,8,128]{2,1,0:T(8,128)S(1)}) custom-call(bf16[272,512]{1,0:T(8,128)(2,1)S(1)} %collective-permute-done.8.refs_0_, ...), custom_call_target="tpu_custom_call" | custom-call | tf_op jit(solution)/shard_map/pallas_call | solution.py:538
  68.4 0.1 collective-permute-start.9
  68.5 3.2 %collective-permute-start.10 = (bf16[128,512]{1,0:T(8,128)(2,1)S(1)}, bf16[128,512]{1,0:T(8,128)(2,1)S(1)}, u32[]{:S(2)}, u32[]{:S(2)}) collective-permute-start(bf16[128,512]{1,0:T(8,128)(2,1)S(1)} %get-tuple-element.58), channel_id=1, source_target_pairs={{0,14},{2,0},{4,2},{6,4},{8,6},{10,8},{12,10},{14,12},{16,30},{18,... | collective-permute-start | bytes 393224 | tf_op jit(solution)/shard_map/ppermute | solution.py:566
  71.7 0.0 copy-done
  71.7 4.4 %shard_map.108 = (bf16[128,512]{1,0:T(8,128)(2,1)S(1)}, bf16[128,512]{1,0:T(8,128)(2,1)S(1)}, bf16[128,512]{1,0:T(8,128)(2,1)S(1)}, bf16[128,512]{1,0:T(8,128)(2...) custom-call(bf16[272,512]{1,0:T(8,128)(2,1)S(1)} %collective-permute, ...), custom_call_target="tpu_custom_call" | custom-call | tf_op jit(solution)/shard_map/pallas_call | solution.py:538
  76.1 0.0 collective-permute-done.9
  76.1 0.0 collective-permute-done.10
  76.2 2.1 %collective-permute-start.12 = (bf16[128,512]{1,0:T(8,128)(2,1)S(1)}, bf16[128,512]{1,0:T(8,128)(2,1)S(1)}, u32[]{:S(2)}, u32[]{:S(2)}) collective-permute-start(bf16[128,512]{1,0:T(8,128)(2,1)S(1)} %add_convert_fusion.2), channel_id=1, source_target_pairs={{0,14},{2,0},{4,2},{6,4},{8,6},{10,8},{12,10},{14,12},{16,30},{18,... | collective-permute-start | bytes 393224 | tf_op jit(solution)/shard_map/ppermute | solution.py:566
  78.3 0.1 collective-permute-start.11
  78.4 3.7 %shard_map.109 = (bf16[256,512]{1,0:T(8,128)(2,1)S(1)}, f32[256,512]{1,0:T(8,128)S(1)}, bf16[128,1024]{1,0:T(8,128)(2,1)}) custom-call(bf16[272,512]{1,0:T(8,128)(2,1)S(1)} %collective-permute-done.8.refs_0_, bf16[272,512]{1,0:T(8,128)(2,1)S(1)} %collective-permute-done.7.refs_6_.refs_1_, ...), custom_call_target="tpu_custom_call" | custom-call | tf_op jit(solution)/shard_map/pallas_call | solution.py:574
  82.1 0.0 copy-start.1
  82.1 0.8 copy-done.1
  82.9 0.0 collective-permute-done.12
  82.9 1.9 %collective-permute-done.11 = bf16[128,512]{1,0:T(8,128)(2,1)S(1)} collective-permute-done((bf16[128,512]{1,0:T(8,128)(2,1)S(1)}, bf16[128,512]{1,0:T(8,128)(2,1)S(1)}, u32[]{:S(2)}, u32[]{:S(2)}) %collective-permute-start.11) | collective-permute-done | bytes 131104 | tf_op jit(solution)/shard_map/ppermute | solution.py:563
  84.8 0.1 collective-permute-start.13
  84.9 0.7 collective-permute-start.16
  85.6 5.1 %all-to-all-start.2 = ((bf16[16,8,1024]{2,1,0:T(8,128)(2,1)}), bf16[16,8,1024]{2,1,0:T(8,128)(2,1)S(1)}, u32[]{:S(2)}, u32[]{:S(2)}) async-start(bf16[16,8,1024]{2,1,0:T(8,128)(2,1)} %bitcast.2), calls=%async_computation.2 | async-start | bytes 524288 | tf_op jit(solution)/shard_map/all_to_all | solution.py:595
  90.7 5.3 %collective-permute-start.15 = (f32[128,512]{1,0:T(8,128)S(1)}, f32[128,512]{1,0:T(8,128)S(1)}, u32[]{:S(2)}, u32[]{:S(2)}) collective-permute-start(f32[128,512]{1,0:T(8,128)S(1)} %convert_add_fusion), channel_id=1, source_target_pairs={{0,14},{2,0},{4,2},{6,4},{8,6},{10,8},{12,10},{14,12},{16,30},{18,... | collective-permute-start | bytes 786440 | tf_op jit(solution)/shard_map/ppermute | solution.py:566
  96.1 0.0 collective-permute-done.13
  96.1 0.1 collective-permute-start.14
  96.2 0.0 collective-permute-done.16.arrived
  96.2 0.0 copy-start.3
  96.2 1.8 %all-to-all-done.2.parts = bf16[16,8,1024]{2,1,0:T(8,128)(2,1)S(1)} async-done(((bf16[16,8,1024]{2,1,0:T(8,128)(2,1)}), bf16[16,8,1024]{2,1,0:T(8,128)(2,1)S(1)}, u32[]{:S(2)}, u32[]{:S(2)}) %all-to-all-start.2) | async-done | bytes 262176 | tf_op jit(solution)/shard_map/all_to_all | solution.py:595
  98.1 0.0 copy-start.2
  98.1 0.0 copy-done.3
  98.1 0.7 copy-done.2
  98.8 2.2 %shard_map.110 = (bf16[128,512]{1,0:T(8,128)(2,1)}, bf16[128,512]{1,0:T(8,128)(2,1)}) custom-call(s32[8]{0:T(128)} %starts.3, s32[8]{0:T(128)} %slots.3, f32[256,512]{1,0:T(8,128)} %copy-done.1, bf16[256,512]{1,0:T(8,128)(2,1)} %copy-done.3, bf16[16,8,1024]{2,1,0:T(8,128)(2,1)} %copy-done.2), custom_call_target="tpu_custom_call" | custom-call | tf_op jit(solution)/shard_map/pallas_call | solution.py:600
  100.9 0.0 collective-permute-done.15
  100.9 1.4 %collective-permute-done.14 = bf16[128,512]{1,0:T(8,128)(2,1)S(1)} collective-permute-done((bf16[128,512]{1,0:T(8,128)(2,1)S(1)}, bf16[128,512]{1,0:T(8,128)(2,1)S(1)}, u32[]{:S(2)}, u32[]{:S(2)}) %collective-permute-start.14) | collective-permute-done | bytes 131104 | tf_op jit(solution)/shard_map/ppermute | solution.py:563
  102.4 0.7 add_convert_fusion
  (5 shorter events, 0.2 us)
Async XLA Ops:
  0.6 3.2 %collective-permute-start = (bf16[128,1024]{1,0:T(8,128)(2,1)}, bf16[128,1024]{1,0:T(8,128)(2,1)S(1)}, u32[]{:S(2)}, u32[]{:S(2)}) collective-permute-start(bf16[128,1024]{1,0:T(8,128)(2,1)} %grad_own.1), channel_id=1, source_target_pairs={{0,1},{1,0},{2,3},{3,2},{4,5},{5,4},{6,7},{7,6},{8,9},{9,8},{10,11... | collective-permute-start | bytes 786440 | tf_op jit(solution)/shard_map/ppermute | solution.py:456
  5.6 21.2 %collective-permute-start.2 = (bf16[272,512]{1,0:T(8,128)(2,1)S(1)}, bf16[272,512]{1,0:T(8,128)(2,1)S(1)}, u32[]{:S(2)}, u32[]{:S(2)}) collective-permute-start(bf16[272,512]{1,0:T(8,128)(2,1)S(1)} %shard_map.104.refs_0_.refs_5_.refs_7_), channel_id=1, source_target_pairs={{0,2},{2,4},{4,6},{6,8},{8,10},{10,12},{12,14},{14,0},{16,18},{18,... | collective-permute-start | bytes 835592 | tf_op jit(solution)/shard_map/ppermute | solution.py:494
  7.6 19.2 %collective-permute-start.1 = (bf16[272,512]{1,0:T(8,128)(2,1)S(1)}, bf16[272,512]{1,0:T(8,128)(2,1)S(1)}, u32[]{:S(2)}, u32[]{:S(2)}) collective-permute-start(bf16[272,512]{1,0:T(8,128)(2,1)S(1)} %shard_map.104.refs_0_.refs_5_.refs_7_), channel_id=1, source_target_pairs={{0,14},{2,0},{4,2},{6,4},{8,6},{10,8},{12,10},{14,12},{16,30},{18,... | collective-permute-start | bytes 835592 | tf_op jit(solution)/shard_map/ppermute | solution.py:493
  11.6 15.2 %all-to-all-start = ((bf16[16,8,1024]{2,1,0:T(8,128)(2,1)}), bf16[16,8,1024]{2,1,0:T(8,128)(2,1)S(1)}, u32[]{:S(2)}, u32[]{:S(2)}) async-start(bf16[16,8,1024]{2,1,0:T(8,128)(2,1)} %get-tuple-element.43), calls=%async_computation | async-start | bytes 524288 | tf_op jit(solution)/shard_map/all_to_all | solution.py:497
  19.1 9.7 %collective-permute-start.5 = (bf16[272,512]{1,0:T(8,128)(2,1)S(1)}, bf16[272,512]{1,0:T(8,128)(2,1)S(1)}, u32[]{:S(2)}, u32[]{:S(2)}) collective-permute-start(bf16[272,512]{1,0:T(8,128)(2,1)S(1)} %get-tuple-element.46.refs_7_.refs_1_.refs_2_.refs_6_), channel_id=1, source_target_pairs={{8,24},{10,26},{12,28},{14,30},{24,40},{26,42},{28,44},{30,46},{40... | collective-permute-start | bytes 835592 | tf_op jit(solution)/shard_map/ppermute | solution.py:501
  26.8 7.6 %collective-permute-start.3 = (bf16[272,512]{1,0:T(8,128)(2,1)S(1)}, bf16[272,512]{1,0:T(8,128)(2,1)S(1)}, u32[]{:S(2)}, u32[]{:S(2)}) collective-permute-start(bf16[272,512]{1,0:T(8,128)(2,1)S(1)} %collective-permute-done.1.refs_1_.refs_4_.refs_6_), channel_id=1, source_target_pairs={{0,14},{2,0},{4,2},{6,4},{8,6},{10,8},{12,10},{14,12},{16,30},{18,... | collective-permute-start | bytes 835592 | tf_op jit(solution)/shard_map/ppermute | solution.py:493
  28.4 8.3 %collective-permute-start.4 = (bf16[272,512]{1,0:T(8,128)(2,1)S(1)}, bf16[272,512]{1,0:T(8,128)(2,1)S(1)}, u32[]{:S(2)}, u32[]{:S(2)}) collective-permute-start(bf16[272,512]{1,0:T(8,128)(2,1)S(1)} %collective-permute-done.2.refs_2_.refs_3_.refs_5_), channel_id=1, source_target_pairs={{0,2},{2,4},{4,6},{6,8},{8,10},{10,12},{12,14},{14,0},{16,18},{18,... | collective-permute-start | bytes 835592 | tf_op jit(solution)/shard_map/ppermute | solution.py:494
  36.7 7.5 %collective-permute-start.6 = (bf16[272,512]{1,0:T(8,128)(2,1)S(1)}, bf16[272,512]{1,0:T(8,128)(2,1)S(1)}, u32[]{:S(2)}, u32[]{:S(2)}) collective-permute-start(bf16[272,512]{1,0:T(8,128)(2,1)S(1)} %collective-permute-done.3.refs_3_.refs_2_.refs_4_), channel_id=1, source_target_pairs={{0,14},{2,0},{4,2},{6,4},{8,6},{10,8},{12,10},{14,12},{16,30},{18,... | collective-permute-start | bytes 835592 | tf_op jit(solution)/shard_map/ppermute | solution.py:493
  37.0 7.8 %collective-permute-start.7 = (bf16[272,512]{1,0:T(8,128)(2,1)S(1)}, bf16[272,512]{1,0:T(8,128)(2,1)S(1)}, u32[]{:S(2)}, u32[]{:S(2)}) collective-permute-start(bf16[272,512]{1,0:T(8,128)(2,1)S(1)} %collective-permute-done.4.refs_4_.refs_1_.refs_3_), channel_id=1, source_target_pairs={{0,2},{2,4},{4,6},{6,8},{8,10},{10,12},{12,14},{14,0},{16,18},{18,... | collective-permute-start | bytes 835592 | tf_op jit(solution)/shard_map/ppermute | solution.py:494
  44.2 6.5 %collective-permute-start.8 = (bf16[272,512]{1,0:T(8,128)(2,1)S(1)}, bf16[272,512]{1,0:T(8,128)(2,1)S(1)}, u32[]{:S(2)}, u32[]{:S(2)}) collective-permute-start(bf16[272,512]{1,0:T(8,128)(2,1)S(1)} %collective-permute-done.6.refs_5_.refs_0_.refs_2_), channel_id=1, source_target_pairs={{0,14},{2,0},{4,2},{6,4},{8,6},{10,8},{12,10},{14,12},{16,30},{18,... | collective-permute-start | bytes 835592 | tf_op jit(solution)/shard_map/ppermute | solution.py:504
  50.1 21.6 %copy-start = (f32[11,128,128]{2,1,0:T(8,128)}, f32[11,128,128]{2,1,0:T(8,128)S(1)}, u32[]{:S(2)}) copy-start(f32[11,128,128]{2,1,0:T(8,128)S(1)} %get-tuple-element.51.refs_5_.refs_9_) | copy-start | bytes 2162692
  68.4 7.7 %collective-permute-start.9 = (bf16[128,512]{1,0:T(8,128)(2,1)S(1)}, bf16[128,512]{1,0:T(8,128)(2,1)S(1)}, u32[]{:S(2)}, u32[]{:S(2)}) collective-permute-start(bf16[128,512]{1,0:T(8,128)(2,1)S(1)} %get-tuple-element.57), channel_id=1, source_target_pairs={{0,2},{2,4},{4,6},{6,8},{8,10},{10,12},{12,14},{14,0},{16,18},{18,... | collective-permute-start | bytes 393224 | tf_op jit(solution)/shard_map/ppermute | solution.py:563
  68.5 7.6 %collective-permute-start.10 = (bf16[128,512]{1,0:T(8,128)(2,1)S(1)}, bf16[128,512]{1,0:T(8,128)(2,1)S(1)}, u32[]{:S(2)}, u32[]{:S(2)}) collective-permute-start(bf16[128,512]{1,0:T(8,128)(2,1)S(1)} %get-tuple-element.58), channel_id=1, source_target_pairs={{0,14},{2,0},{4,2},{6,4},{8,6},{10,8},{12,10},{14,12},{16,30},{18,... | collective-permute-start | bytes 393224 | tf_op jit(solution)/shard_map/ppermute | solution.py:566
  76.2 6.7 %collective-permute-start.12 = (bf16[128,512]{1,0:T(8,128)(2,1)S(1)}, bf16[128,512]{1,0:T(8,128)(2,1)S(1)}, u32[]{:S(2)}, u32[]{:S(2)}) collective-permute-start(bf16[128,512]{1,0:T(8,128)(2,1)S(1)} %add_convert_fusion.2), channel_id=1, source_target_pairs={{0,14},{2,0},{4,2},{6,4},{8,6},{10,8},{12,10},{14,12},{16,30},{18,... | collective-permute-start | bytes 393224 | tf_op jit(solution)/shard_map/ppermute | solution.py:566
  78.3 6.5 %collective-permute-start.11 = (bf16[128,512]{1,0:T(8,128)(2,1)S(1)}, bf16[128,512]{1,0:T(8,128)(2,1)S(1)}, u32[]{:S(2)}, u32[]{:S(2)}) collective-permute-start(bf16[128,512]{1,0:T(8,128)(2,1)S(1)} %add_convert_fusion.3), channel_id=1, source_target_pairs={{0,2},{2,4},{4,6},{6,8},{8,10},{10,12},{12,14},{14,0},{16,18},{18,... | collective-permute-start | bytes 393224 | tf_op jit(solution)/shard_map/ppermute | solution.py:563
  82.1 0.8 copy-start.1
  84.8 11.3 %collective-permute-start.13 = (f32[128,512]{1,0:T(8,128)S(1)}, f32[128,512]{1,0:T(8,128)S(1)}, u32[]{:S(2)}, u32[]{:S(2)}) collective-permute-start(f32[128,512]{1,0:T(8,128)S(1)} %convert_add_fusion.1), channel_id=1, source_target_pairs={{0,2},{2,4},{4,6},{6,8},{8,10},{10,12},{12,14},{14,0},{16,18},{18,... | collective-permute-start | bytes 786440 | tf_op jit(solution)/shard_map/ppermute | solution.py:563
  84.9 11.3 %collective-permute-start.16 = (bf16[256,512]{1,0:T(8,128)(2,1)S(1)}, bf16[256,512]{1,0:T(8,128)(2,1)S(1)}, u32[]{:S(2)}, u32[]{:S(2)}) collective-permute-start(bf16[256,512]{1,0:T(8,128)(2,1)S(1)} %get-tuple-element.75), channel_id=1, source_target_pairs={{24,8},{26,10},{28,12},{30,14},{40,24},{42,26},{44,28},{46,30},{56... | collective-permute-start | bytes 786440 | tf_op jit(solution)/shard_map/ppermute | solution.py:594
  85.6 12.5 %all-to-all-start.2 = ((bf16[16,8,1024]{2,1,0:T(8,128)(2,1)}), bf16[16,8,1024]{2,1,0:T(8,128)(2,1)S(1)}, u32[]{:S(2)}, u32[]{:S(2)}) async-start(bf16[16,8,1024]{2,1,0:T(8,128)(2,1)} %bitcast.2), calls=%async_computation.2 | async-start | bytes 524288 | tf_op jit(solution)/shard_map/all_to_all | solution.py:595
  90.7 10.2 %collective-permute-start.15 = (f32[128,512]{1,0:T(8,128)S(1)}, f32[128,512]{1,0:T(8,128)S(1)}, u32[]{:S(2)}, u32[]{:S(2)}) collective-permute-start(f32[128,512]{1,0:T(8,128)S(1)} %convert_add_fusion), channel_id=1, source_target_pairs={{0,14},{2,0},{4,2},{6,4},{8,6},{10,8},{12,10},{14,12},{16,30},{18,... | collective-permute-start | bytes 786440 | tf_op jit(solution)/shard_map/ppermute | solution.py:566
  96.1 6.3 %collective-permute-start.14 = (bf16[128,512]{1,0:T(8,128)(2,1)S(1)}, bf16[128,512]{1,0:T(8,128)(2,1)S(1)}, u32[]{:S(2)}, u32[]{:S(2)}) collective-permute-start(bf16[128,512]{1,0:T(8,128)(2,1)S(1)} %add_convert_fusion.1), channel_id=1, source_target_pairs={{0,2},{2,4},{4,6},{6,8},{8,10},{10,12},{12,14},{14,0},{16,18},{18,... | collective-permute-start | bytes 393224 | tf_op jit(solution)/shard_map/ppermute | solution.py:563
  96.2 1.8 %copy-start.3 = (bf16[256,512]{1,0:T(8,128)(2,1)}, bf16[256,512]{1,0:T(8,128)(2,1)S(1)}, u32[]{:S(2)}) copy-start(bf16[256,512]{1,0:T(8,128)(2,1)S(1)} %collective-permute-done.16.arrived) | copy-start | bytes 786436
  98.1 0.7 copy-start.2

commit v6 on v5

--- a/solution.py
+++ b/solution.py
@@ -286,10 +286,9 @@
     merging = order is LEADING
     near = [o for o in order if o <= REACH]
     chunks, (own, previous, sums, bias_most, bias_last, stats_in), refs = refs[:count], refs[count : count + 6], refs[count + 6 :]
-    query_grads, (coarse_out, window_out), refs = refs[:count], refs[count : count + 2], refs[count + 2 :]
+    query_grads, (coarse, window), refs = refs[:count], refs[count : count + 2], refs[count + 2 :]
     merged_out, refs = (refs[0], refs[1:]) if merging else (None, refs)
-    packed, pairs, keys, bias, stats, merged, coarse, window, *refs = refs
-    key_sems, chunk_sems, bias_sems, stats_sem, out_sems = refs
+    packed, pairs, keys, bias, stats, merged, key_sems, chunk_sems, bias_sems, stats_sem = refs
     stats_copy = pltpu.make_async_copy(stats_in, stats, stats_sem)
     stats_copy.start()
     key_copies = load_keys(own, previous, sums, pairs, keys, key_sems)
@@ -319,7 +318,6 @@
         [jnp.transpose(pairs[i, 0:TOK, h * HD : (h + 1) * HD]) for i in range(2)]
         for h in range(HEADS_HERE)
     ]
-    writes = []
     for first in range(0, count, TOGETHER):
         group = range(first, first + TOGETHER)
         for i in group:
@@ -350,38 +348,21 @@
                 window[near.index(o), 1, h] = probs_low[0:TOK]
             coarse[i, 0, h] = dscores[-TOK:]
             coarse[i, 1, h] = probs_low[-TOK:]
-        for i in group:
-            o = order[i]
-            writes.append(pltpu.make_async_copy(coarse.at[i], coarse_out.at[i], out_sems.at[0, o]))
-            writes[-1].start()
-            if o <= REACH:
-                at = near.index(o)
-                writes.append(
-                    pltpu.make_async_copy(window.at[at], window_out.at[at], out_sems.at[1, o])
-                )
-                writes[-1].start()
-    for copy in writes:
-        copy.wait()
 
 
 def key_grad_kernel(*refs):
     order = ORDER
     near = [o for o in order if o <= REACH]
     chunks, coarse_in, window_in, refs = refs[:NZ], refs[NZ : NZ + 2], refs[NZ + 2 : NZ + 4], refs[NZ + 4 :]
-    previous_grad, own_grad, sum_grad, packed, coarse, window, sems = refs
-    copies = []
+    previous_grad, own_grad, sum_grad, packed, sems = refs
+    copies, coarse, window = [], [], {}
     for i, o in enumerate(order):
         part, group = (0, LEADING) if o in LEADING else (1, TRAILING)
-        mine = [pltpu.make_async_copy(chunks[i], packed.at[i], sems.at[0, i])]
-        source = coarse_in[part].at[group.index(o)]
-        mine.append(pltpu.make_async_copy(source, coarse.at[i], sems.at[1, i]))
+        coarse.append(coarse_in[part].at[group.index(o)])
         if o in near:
-            source = window_in[part].at[[n for n in group if n <= REACH].index(o)]
-            target = window.at[near.index(o)]
-            mine.append(pltpu.make_async_copy(source, target, sems.at[2, i]))
-        for copy in mine:
-            copy.start()
-        copies.append(mine)
+            window[o] = window_in[part].at[[n for n in group if n <= REACH].index(o)]
+        copies.append(pltpu.make_async_copy(chunks[i], packed.at[i], sems.at[i]))
+        copies[-1].start()
     _, z = place()
     units = [(h, kind) for h in range(HEADS_HERE) for kind in range(2)]
     zero = jnp.zeros((TOK, HD), F32)
@@ -390,13 +371,12 @@
     for first in range(0, NZ, half):
         group = range(first, first + half)
         for i in group:
-            for copy in copies[i]:
-                copy.wait()
+            copies[i].wait()
         for unit, (h, kind) in enumerate(units):
             cols = slice(h * HD, (h + 1) * HD)
             tokens = [packed[i, kind * TOK : (kind + 1) * TOK, cols] for i in group]
             part = jnp.dot(
-                jnp.concatenate([coarse[i, kind, h] for i in group], axis=1),
+                jnp.concatenate([coarse[i][kind, h] for i in group], axis=1),
                 jnp.concatenate(tokens, axis=0),
                 preferred_element_type=F32,
             )
@@ -404,7 +384,7 @@
             for i in group:
                 if order[i] in near:
                     part = jnp.dot(
-                        window[near.index(order[i]), kind, h],
+                        window[order[i]][kind, h],
                         tokens[i - first],
                         preferred_element_type=F32,
                     )
@@ -538,21 +518,18 @@
         made = pl.pallas_call(
             lambda *refs: query_grad_kernel(order, *refs),
             out_shape=(shape((TOK, FEAT)),) * len(order)
-            + (shape(coarse_shape), shape(window_shape))
+            + (VMEM(coarse_shape, BF16), VMEM(window_shape, BF16))
             + (shape(stats_shape[1:], F32),) * merging,
             in_specs=[whole(HBM)] * (len(order) + 6),
-            out_specs=(whole(VMEM),) * len(order) + (whole(HBM),) * 2 + (whole(VMEM),) * merging,
+            out_specs=(whole(VMEM),) * (len(order) + 2 + merging),
             scratch_shapes=held
             + [
                 VMEM(stats.shape, F32),
                 VMEM(stats_shape[1:], F32),
-                VMEM(coarse_shape, BF16),
-                VMEM(window_shape, BF16),
                 dma((3,)),
                 dma((NZ,)),
                 dma(bias_shape[:1]),
                 dma,
-                dma((2, NZ)),
             ],
             compiler_params=params,
         )(*[chunks[o] for o in order], own, previous, all_sums, bias_most, bias_last, stats)
@@ -578,16 +555,17 @@
             shape((2 * TOK, FEAT), F32),
             shape((bars, 2 * FEAT)),
         ),
-        in_specs=[whole(HBM)] * (NZ + 4),
+        in_specs=[whole(HBM)] * NZ + [whole(VMEM)] * 4,
         out_specs=(whole(VMEM),) * 3,
-        scratch_shapes=[
-            VMEM((NZ, ROWS, FEAT), BF16),
-            VMEM((NZ, 2, HEADS_HERE, bars, TOK), BF16),
-            VMEM((REACH + 1, 2, HEADS_HERE, TOK, TOK), BF16),
-            dma((3, NZ)),
+        scratch_shapes=[VMEM((NZ, ROWS, FEAT), BF16), dma((NZ,))],
+        compiler_params=params,
+    )(
+        *[chunks[o] for o in ORDER],
+        *[
+            pltpu.with_memory_space_constraint(x, VMEM)
+            for x in (coarse_a, coarse_b, window_a, window_b)
         ],
-        compiler_params=params,
-    )(*[chunks[o] for o in ORDER], coarse_a, coarse_b, window_a, window_b)
+    )
     forward, backward, sum_grad = lax.optimization_barrier((forward, backward, sum_grad))
     forward = forward_step(forward.astype(F32) + grads[2].astype(F32))
     backward = backward_step(backward.astype(F32) + grads[7].astype(F32))

time: 104 us -> 104 us (level)
  Pallas kernels: 23.4 us -> 22.3 us
  transfers between devices with their start and end apart: 19 -> 19, of which waited for: 8 -> 8; matrix products, arithmetic and copies ran while one was open for 0% -> 0% of each run, Pallas kernels for 18% -> 17%
where the time goes in v6:
time: 104 us; the launch traced here: 103 us
  starting transfers between devices  36.7 us (35%)
  waiting for transfers between devices  26.9 us (26%)
  Pallas kernels  22.3 us (21%)
  blocking collectives  14.7 us (14%)
    all_to_all x1, blocking collectives, shards(): stats = lax.all_to_all(stats, 'seq', 0, 0, axis_index_groups=Z_GROUPS)  14.7 us
    ppermute x3, starting transfers between devices, backward_step(): return lax.ppermute(array, 'seq', TO_PREVIOUS)  11.6 us
    ppermute x3, waiting for transfers between devices, ring_step(): after.append(lax.ppermute(after[-1], 'seq', TO_PREVIOUS))  11 us
    all_to_all x1, starting transfers between devices, shards(): all_sums = lax.all_to_all(sums, 'seq', 0, 0, axis_index_groups=XY_GROUPS)  7.48 us
    all_to_all x1, waiting for transfers between devices, shards(): all_sums = lax.all_to_all(sums, 'seq', 0, 0, axis_index_groups=XY_GROUPS)  7.01 us
    pallas_call x2, Pallas kernels, stats_of(): pl.pallas_call(lambda *refs: stats_kernel(order, *refs), out_shape=out +...  6.58 us
    ppermute x3, starting transfers between devices, ring_step(): after.append(lax.ppermute(after[-1], 'seq', TO_PREVIOUS))  6.12 us
    pallas_call x2, Pallas kernels, query_grads(): pl.pallas_call(lambda *refs: query_grad_kernel(order, *refs), out_shape=(...  5.2 us
  transfers between devices with their start and end apart: 19, of which 8 were waited for; matrix products, arithmetic and copies ran while one was open for 0% of the time, Pallas kernels for 17%

profile of v6, /device:TPU:2, one launch (start us, length us, event | category | flops | bytes accessed | tf_op | source)
XLA Modules:
  0.0 103.1 jit_solution(12641940497038584363)
XLA Ops:
  0.6 0.1 collective-permute-start
  0.7 3.1 %shard_map.103 = (f32[512,128]{1,0:T(8,128)S(1)}, bf16[272,512]{1,0:T(8,128)(2,1)S(1)}, bf16[272,512]{1,0:T(8,128)(2,1)S(1)}, bf16[16,8,1024]{2,1,0:T(8,128)(2,1)}) custom-call(s32[1]{0:T(128)} %bitcast.core, s32[8]{0:T(128)} %starts.3, s32[8,8]{1,0:T(8,128)} %related.1, s32[8]{0:T(128)} %slots.3, bf16[128,512]{1,0:T(8,128)(2,1)} %queries.1, ...), custom_call_target="tpu_custom_call" | custom-call | tf_op jit(solution)/shard_map/pallas_call | solution.py:439
  3.8 0.0 copy-start
  3.8 0.0 collective-permute-done.grad_other
  3.8 1.8 %shard_map.104.refs_0_.refs_5_.refs_7_ = bf16[272,512]{1,0:T(8,128)(2,1)S(1)} custom-call(s32[1]{0:T(128)} %bitcast.core, bf16[272,512]{1,0:T(8,128)(2,1)S(1)} %get-tuple-element.41.pack, f32[512,128]{1,0:T(8,128)S(1)} %get-tuple-element.42.partial, bf16[128,1024]{1,0:T(8,128)(2,1)S(1)} %collective-permute-done.grad_other, bf16[512,2048]{1,0:T(8,128)(2,1)} %out_weight.3), custom_call_target="tpu_custom_call" | custom-call | tf_op jit(solution)/shard_map/pallas_call | solution.py:456
  5.7 0.0 copy-start.2
  5.7 2.0 %collective-permute-start.2 = (bf16[272,512]{1,0:T(8,128)(2,1)S(1)}, bf16[272,512]{1,0:T(8,128)(2,1)S(1)}, u32[]{:S(2)}, u32[]{:S(2)}) collective-permute-start(bf16[272,512]{1,0:T(8,128)(2,1)S(1)} %shard_map.104.refs_0_.refs_5_.refs_7_), channel_id=1, source_target_pairs={{0,2},{2,4},{4,6},{6,8},{8,10},{10,12},{12,14},{14,0},{16,18},{18,... | collective-permute-start | bytes 835592 | tf_op jit(solution)/shard_map/ppermute | solution.py:474
  7.7 4.0 %collective-permute-start.1 = (bf16[272,512]{1,0:T(8,128)(2,1)S(1)}, bf16[272,512]{1,0:T(8,128)(2,1)S(1)}, u32[]{:S(2)}, u32[]{:S(2)}) collective-permute-start(bf16[272,512]{1,0:T(8,128)(2,1)S(1)} %shard_map.104.refs_0_.refs_5_.refs_7_), channel_id=1, source_target_pairs={{0,14},{2,0},{4,2},{6,4},{8,6},{10,8},{12,10},{14,12},{16,30},{18,... | collective-permute-start | bytes 835592 | tf_op jit(solution)/shard_map/ppermute | solution.py:473
  11.7 7.5 %all-to-all-start = ((bf16[16,8,1024]{2,1,0:T(8,128)(2,1)}), bf16[16,8,1024]{2,1,0:T(8,128)(2,1)S(1)}, u32[]{:S(2)}, u32[]{:S(2)}) async-start(bf16[16,8,1024]{2,1,0:T(8,128)(2,1)} %get-tuple-element.43), calls=%async_computation | async-start | bytes 524288 | tf_op jit(solution)/shard_map/all_to_all | solution.py:477
  19.2 0.7 collective-permute-start.5
  19.9 7.0 %all-to-all-done = bf16[16,8,1024]{2,1,0:T(8,128)(2,1)S(1)} async-done(((bf16[16,8,1024]{2,1,0:T(8,128)(2,1)}), bf16[16,8,1024]{2,1,0:T(8,128)(2,1)S(1)}, u32[]{:S(2)}, u32[]{:S(2)}) %all-to-all-start) | async-done | bytes 262176 | tf_op jit(solution)/shard_map/all_to_all | solution.py:477
  26.9 0.0 collective-permute-done.2.refs_2_.refs_3_.refs_5_
  26.9 0.0 collective-permute-done.1.refs_1_.refs_4_.refs_6_
  26.9 0.0 copy-start.6
  26.9 1.7 %collective-permute-start.3 = (bf16[272,512]{1,0:T(8,128)(2,1)S(1)}, bf16[272,512]{1,0:T(8,128)(2,1)S(1)}, u32[]{:S(2)}, u32[]{:S(2)}) collective-permute-start(bf16[272,512]{1,0:T(8,128)(2,1)S(1)} %collective-permute-done.1.refs_1_.refs_4_.refs_6_), channel_id=1, source_target_pairs={{0,14},{2,0},{4,2},{6,4},{8,6},{10,8},{12,10},{14,12},{16,30},{18,... | collective-permute-start | bytes 835592 | tf_op jit(solution)/shard_map/ppermute | solution.py:473
  28.6 0.4 collective-permute-start.4
  29.0 0.0 collective-permute-done.5.refs_8_.refs_2_.refs_3_.refs_7_
  29.0 5.5 %collective-permute-done.3.refs_3_.refs_2_.refs_4_ = bf16[272,512]{1,0:T(8,128)(2,1)S(1)} collective-permute-done((bf16[272,512]{1,0:T(8,128)(2,1)S(1)}, bf16[272,512]{1,0:T(8,128)(2,1)S(1)}, u32[]{:S(2)}, u32[]{:S(2)}) %collective-permute-start.3) | collective-permute-done | bytes 278560 | tf_op jit(solution)/shard_map/ppermute | solution.py:473
  34.5 2.3 %collective-permute-done.4.refs_4_.refs_1_.refs_3_ = bf16[272,512]{1,0:T(8,128)(2,1)S(1)} collective-permute-done((bf16[272,512]{1,0:T(8,128)(2,1)S(1)}, bf16[272,512]{1,0:T(8,128)(2,1)S(1)}, u32[]{:S(2)}, u32[]{:S(2)}) %collective-permute-start.4) | collective-permute-done | bytes 278560 | tf_op jit(solution)/shard_map/ppermute | solution.py:474
  36.9 0.4 collective-permute-start.6
  37.2 1.7 %collective-permute-start.7 = (bf16[272,512]{1,0:T(8,128)(2,1)S(1)}, bf16[272,512]{1,0:T(8,128)(2,1)S(1)}, u32[]{:S(2)}, u32[]{:S(2)}) collective-permute-start(bf16[272,512]{1,0:T(8,128)(2,1)S(1)} %collective-permute-done.4.refs_4_.refs_1_.refs_3_), channel_id=1, source_target_pairs={{0,2},{2,4},{4,6},{6,8},{8,10},{10,12},{12,14},{14,0},{16,18},{18,... | collective-permute-start | bytes 835592 | tf_op jit(solution)/shard_map/ppermute | solution.py:474
  38.9 5.5 %collective-permute-done.6.refs_5_.refs_0_.refs_2_ = bf16[272,512]{1,0:T(8,128)(2,1)S(1)} collective-permute-done((bf16[272,512]{1,0:T(8,128)(2,1)S(1)}, bf16[272,512]{1,0:T(8,128)(2,1)S(1)}, u32[]{:S(2)}, u32[]{:S(2)}) %collective-permute-start.6) | collective-permute-done | bytes 278560 | tf_op jit(solution)/shard_map/ppermute | solution.py:473
  44.4 0.6 collective-permute-start.8
  45.0 0.0 collective-permute-done.7.refs_6_.refs_1_
  45.0 5.3 %shard_map.105 = (f32[8,8,128]{2,1,0:T(8,128)S(1)}, f32[11,128,128]{2,1,0:T(8,128)S(1)}) custom-call(bf16[272,512]{1,0:T(8,128)(2,1)S(1)} %shard_map.104.refs_0_.refs_5_.refs_7_, bf16[272,512]{1,0:T(8,128)(2,1)S(1)} %collective-permute-done.1.refs_1_.refs_4_.refs_6_, bf16[272,512]{1,0:T(8,128)(2,1)S(1)} %collective-permute-done.2.refs_2_.refs_3_.refs_5_, ...), custom_call_target="tpu_custom_call" | custom-call | tf_op jit(solution)/shard_map/pallas_call | solution.py:499
  50.4 0.0 copy-start.3
  50.4 0.5 collective-permute-done.8.refs_0_
  50.9 1.2 %shard_map.106 = (f32[8,8,8,128]{3,2,1,0:T(8,128)S(1)}, f32[2,128,128]{2,1,0:T(8,128)S(1)}) custom-call(bf16[272,512]{1,0:T(8,128)(2,1)S(1)} %collective-permute-done.8.refs_0_, bf16[272,512]{1,0:T(8,128)(2,1)S(1)} %get-tuple-element.46.refs_7_.refs_1_.refs_2_.refs_6_, bf16[272,512]{1,0:T(8,128)(2,1)S(1)} %collective-permute-done.5.refs_8_.refs_2_.refs_3_.refs_7_, ...), custom_call_target="tpu_custom_call" | custom-call | tf_op jit(solution)/shard_map/pallas_call | solution.py:499
  52.2 0.0 copy-done.2
  52.2 14.7 %all_to_all.15.refs_7_ = f32[8,8,8,128]{3,2,1,0:T(8,128)S(1)} all-to-all(f32[8,8,8,128]{3,2,1,0:T(8,128)S(1)} %get-tuple-element.54), channel_id=1, replica_groups={{0,2,4,6,8,10,12,14},{16,18,20,22,24,26,28,30},{32,34,36,38,40,42,44,46..., dimensions={0} | all-to-all | bytes 524288 | tf_op jit(solution)/shard_map/all_to_all | solution.py:511
  66.9 0.0 copy-done.5
  66.9 0.0 copy-done.6
  66.9 0.0 copy-done.7
  66.9 0.0 copy-done.8
  66.9 0.0 copy-done
  66.9 0.0 copy-done.1
  66.9 0.0 copy-done.10
  66.9 1.6 %shard_map.107 = (bf16[128,512]{1,0:T(8,128)(2,1)S(1)}, bf16[128,512]{1,0:T(8,128)(2,1)S(1)}, bf16[2,2,4,128,128]{4,3,2,1,0:T(8,128)(2,1)S(1)}, bf16[1,2,4,128,128]{4,3,2,1,0:T(8,128)(2,1)S(1)}, f32[8,8,128]{2,1,0:T(8,128)S(1)}) custom-call(bf16[272,512]{1,0:T(8,128)(2,1)S(1)} %collective-permute-done.8.refs_0_, ...), custom_call_target="tpu_custom_call" | custom-call | tf_op jit(solution)/shard_map/pallas_call | solution.py:518
  68.5 0.1 collective-permute-start.9
  68.6 3.2 %collective-permute-start.10 = (bf16[128,512]{1,0:T(8,128)(2,1)S(1)}, bf16[128,512]{1,0:T(8,128)(2,1)S(1)}, u32[]{:S(2)}, u32[]{:S(2)}) collective-permute-start(bf16[128,512]{1,0:T(8,128)(2,1)S(1)} %get-tuple-element.58), channel_id=1, source_target_pairs={{0,14},{2,0},{4,2},{6,4},{8,6},{10,8},{12,10},{14,12},{16,30},{18,... | collective-permute-start | bytes 393224 | tf_op jit(solution)/shard_map/ppermute | solution.py:543
  71.9 0.0 copy-done.9
  71.9 0.0 copy-done.3
  71.9 3.6 %shard_map.108 = (bf16[128,512]{1,0:T(8,128)(2,1)S(1)}, bf16[128,512]{1,0:T(8,128)(2,1)S(1)}, bf16[128,512]{1,0:T(8,128)(2,1)S(1)}, bf16[128,512]{1,0:T(8,128)(2...) custom-call(bf16[272,512]{1,0:T(8,128)(2,1)S(1)} %collective-permute, ...), custom_call_target="tpu_custom_call" | custom-call | tf_op jit(solution)/shard_map/pallas_call | solution.py:518
  75.5 0.0 copy-done.4
  75.5 0.0 collective-permute-done.9
  75.5 0.0 collective-permute-done.10
  75.5 2.9 %collective-permute-start.12 = (bf16[128,512]{1,0:T(8,128)(2,1)S(1)}, bf16[128,512]{1,0:T(8,128)(2,1)S(1)}, u32[]{:S(2)}, u32[]{:S(2)}) collective-permute-start(bf16[128,512]{1,0:T(8,128)(2,1)S(1)} %add_convert_fusion.2), channel_id=1, source_target_pairs={{0,14},{2,0},{4,2},{6,4},{8,6},{10,8},{12,10},{14,12},{16,30},{18,... | collective-permute-start | bytes 393224 | tf_op jit(solution)/shard_map/ppermute | solution.py:543
  78.4 0.1 collective-permute-start.11
  78.5 3.5 %shard_map.109 = (bf16[256,512]{1,0:T(8,128)(2,1)S(1)}, f32[256,512]{1,0:T(8,128)}, bf16[128,1024]{1,0:T(8,128)(2,1)}) custom-call(bf16[272,512]{1,0:T(8,128)(2,1)} %copy-done.4, bf16[272,512]{1,0:T(8,128)(2,1)} %copy-done.10, bf16[272,512]{1,0:T(8,128)(2,1)} %copy-done.9, bf16[272,512]{1,0:T(8,128)(2,1)} %copy-done.8, bf16[272,512]{1,0:T(8,128)(2,1)} %copy-done.7, ...), custom_call_target="tpu_custom_call" | custom-call | tf_op jit(solution)/shard_map/pallas_call | solution.py:551
  82.0 0.0 collective-permute-done.12
  82.0 2.7 %collective-permute-done.11 = bf16[128,512]{1,0:T(8,128)(2,1)S(1)} collective-permute-done((bf16[128,512]{1,0:T(8,128)(2,1)S(1)}, bf16[128,512]{1,0:T(8,128)(2,1)S(1)}, u32[]{:S(2)}, u32[]{:S(2)}) %collective-permute-start.11) | collective-permute-done | bytes 131104 | tf_op jit(solution)/shard_map/ppermute | solution.py:540
  84.7 0.1 collective-permute-start.13
  84.8 0.7 collective-permute-start.16
  85.5 5.1 %all-to-all-start.2 = ((bf16[16,8,1024]{2,1,0:T(8,128)(2,1)}), bf16[16,8,1024]{2,1,0:T(8,128)(2,1)S(1)}, u32[]{:S(2)}, u32[]{:S(2)}) async-start(bf16[16,8,1024]{2,1,0:T(8,128)(2,1)} %bitcast.2), calls=%async_computation.2 | async-start | bytes 524288 | tf_op jit(solution)/shard_map/all_to_all | solution.py:573
  90.6 5.5 %collective-permute-start.15 = (f32[128,512]{1,0:T(8,128)S(1)}, f32[128,512]{1,0:T(8,128)S(1)}, u32[]{:S(2)}, u32[]{:S(2)}) collective-permute-start(f32[128,512]{1,0:T(8,128)S(1)} %convert_add_fusion), channel_id=1, source_target_pairs={{0,14},{2,0},{4,2},{6,4},{8,6},{10,8},{12,10},{14,12},{16,30},{18,... | collective-permute-start | bytes 786440 | tf_op jit(solution)/shard_map/ppermute | solution.py:543
  96.1 0.0 collective-permute-done.13
  96.2 0.1 collective-permute-start.14
  96.3 0.0 collective-permute-done.16.arrived
  96.3 1.8 %all-to-all-done.2.parts = bf16[16,8,1024]{2,1,0:T(8,128)(2,1)S(1)} async-done(((bf16[16,8,1024]{2,1,0:T(8,128)(2,1)}), bf16[16,8,1024]{2,1,0:T(8,128)(2,1)S(1)}, u32[]{:S(2)}, u32[]{:S(2)}) %all-to-all-start.2) | async-done | bytes 262176 | tf_op jit(solution)/shard_map/all_to_all | solution.py:573
  98.0 0.7 copy-done.11
  98.7 2.2 %shard_map.110 = (bf16[128,512]{1,0:T(8,128)(2,1)}, bf16[128,512]{1,0:T(8,128)(2,1)}) custom-call(s32[8]{0:T(128)} %starts.3, s32[8]{0:T(128)} %slots.3, f32[256,512]{1,0:T(8,128)} %get-tuple-element.74.own_grad, bf16[256,512]{1,0:T(8,128)(2,1)} %copy-done.12, bf16[16,8,1024]{2,1,0:T(8,128)(2,1)} %copy-done.11), custom_call_target="tpu_custom_call" | custom-call | tf_op jit(solution)/shard_map/pallas_call | solution.py:578
  100.9 0.0 collective-permute-done.15
  100.9 1.5 %collective-permute-done.14 = bf16[128,512]{1,0:T(8,128)(2,1)S(1)} collective-permute-done((bf16[128,512]{1,0:T(8,128)(2,1)S(1)}, bf16[128,512]{1,0:T(8,128)(2,1)S(1)}, u32[]{:S(2)}, u32[]{:S(2)}) %collective-permute-start.14) | collective-permute-done | bytes 131104 | tf_op jit(solution)/shard_map/ppermute | solution.py:540
  102.4 0.7 add_convert_fusion
  (15 shorter events, 0.2 us)
Async XLA Ops:
  0.6 3.2 %collective-permute-start = (bf16[128,1024]{1,0:T(8,128)(2,1)}, bf16[128,1024]{1,0:T(8,128)(2,1)S(1)}, u32[]{:S(2)}, u32[]{:S(2)}) collective-permute-start(bf16[128,1024]{1,0:T(8,128)(2,1)} %grad_own.1), channel_id=1, source_target_pairs={{0,1},{1,0},{2,3},{3,2},{4,5},{5,4},{6,7},{7,6},{8,9},{9,8},{10,11... | collective-permute-start | bytes 786440 | tf_op jit(solution)/shard_map/ppermute | solution.py:436
  3.8 63.1 %copy-start = (bf16[272,512]{1,0:T(8,128)(2,1)}, bf16[272,512]{1,0:T(8,128)(2,1)S(1)}, u32[]{:S(2)}) copy-start(bf16[272,512]{1,0:T(8,128)(2,1)S(1)} %get-tuple-element.46.refs_7_.refs_1_.refs_2_.refs_6_) | copy-start | bytes 835588
  5.7 46.5 %copy-start.2 = (bf16[272,512]{1,0:T(8,128)(2,1)}, bf16[272,512]{1,0:T(8,128)(2,1)S(1)}, u32[]{:S(2)}) copy-start(bf16[272,512]{1,0:T(8,128)(2,1)S(1)} %shard_map.104.refs_0_.refs_5_.refs_7_) | copy-start | bytes 835588
  5.7 21.2 %collective-permute-start.2 = (bf16[272,512]{1,0:T(8,128)(2,1)S(1)}, bf16[272,512]{1,0:T(8,128)(2,1)S(1)}, u32[]{:S(2)}, u32[]{:S(2)}) collective-permute-start(bf16[272,512]{1,0:T(8,128)(2,1)S(1)} %shard_map.104.refs_0_.refs_5_.refs_7_), channel_id=1, source_target_pairs={{0,2},{2,4},{4,6},{6,8},{8,10},{10,12},{12,14},{14,0},{16,18},{18,... | collective-permute-start | bytes 835592 | tf_op jit(solution)/shard_map/ppermute | solution.py:474
  7.7 19.2 %collective-permute-start.1 = (bf16[272,512]{1,0:T(8,128)(2,1)S(1)}, bf16[272,512]{1,0:T(8,128)(2,1)S(1)}, u32[]{:S(2)}, u32[]{:S(2)}) collective-permute-start(bf16[272,512]{1,0:T(8,128)(2,1)S(1)} %shard_map.104.refs_0_.refs_5_.refs_7_), channel_id=1, source_target_pairs={{0,14},{2,0},{4,2},{6,4},{8,6},{10,8},{12,10},{14,12},{16,30},{18,... | collective-permute-start | bytes 835592 | tf_op jit(solution)/shard_map/ppermute | solution.py:473
  11.7 15.2 %all-to-all-start = ((bf16[16,8,1024]{2,1,0:T(8,128)(2,1)}), bf16[16,8,1024]{2,1,0:T(8,128)(2,1)S(1)}, u32[]{:S(2)}, u32[]{:S(2)}) async-start(bf16[16,8,1024]{2,1,0:T(8,128)(2,1)} %get-tuple-element.43), calls=%async_computation | async-start | bytes 524288 | tf_op jit(solution)/shard_map/all_to_all | solution.py:477
  19.2 9.8 %collective-permute-start.5 = (bf16[272,512]{1,0:T(8,128)(2,1)S(1)}, bf16[272,512]{1,0:T(8,128)(2,1)S(1)}, u32[]{:S(2)}, u32[]{:S(2)}) collective-permute-start(bf16[272,512]{1,0:T(8,128)(2,1)S(1)} %get-tuple-element.46.refs_7_.refs_1_.refs_2_.refs_6_), channel_id=1, source_target_pairs={{8,24},{10,26},{12,28},{14,30},{24,40},{26,42},{28,44},{30,46},{40... | collective-permute-start | bytes 835592 | tf_op jit(solution)/shard_map/ppermute | solution.py:481
  26.9 40.0 %copy-start.5 = (bf16[272,512]{1,0:T(8,128)(2,1)}, bf16[272,512]{1,0:T(8,128)(2,1)S(1)}, u32[]{:S(2)}) copy-start(bf16[272,512]{1,0:T(8,128)(2,1)S(1)} %collective-permute-done.2.refs_2_.refs_3_.refs_5_) | copy-start | bytes 835588
  26.9 40.0 %copy-start.6 = (bf16[272,512]{1,0:T(8,128)(2,1)}, bf16[272,512]{1,0:T(8,128)(2,1)S(1)}, u32[]{:S(2)}) copy-start(bf16[272,512]{1,0:T(8,128)(2,1)S(1)} %collective-permute-done.1.refs_1_.refs_4_.refs_6_) | copy-start | bytes 835588
  26.9 7.6 %collective-permute-start.3 = (bf16[272,512]{1,0:T(8,128)(2,1)S(1)}, bf16[272,512]{1,0:T(8,128)(2,1)S(1)}, u32[]{:S(2)}, u32[]{:S(2)}) collective-permute-start(bf16[272,512]{1,0:T(8,128)(2,1)S(1)} %collective-permute-done.1.refs_1_.refs_4_.refs_6_), channel_id=1, source_target_pairs={{0,14},{2,0},{4,2},{6,4},{8,6},{10,8},{12,10},{14,12},{16,30},{18,... | collective-permute-start | bytes 835592 | tf_op jit(solution)/shard_map/ppermute | solution.py:473
  28.6 8.2 %collective-permute-start.4 = (bf16[272,512]{1,0:T(8,128)(2,1)S(1)}, bf16[272,512]{1,0:T(8,128)(2,1)S(1)}, u32[]{:S(2)}, u32[]{:S(2)}) collective-permute-start(bf16[272,512]{1,0:T(8,128)(2,1)S(1)} %collective-permute-done.2.refs_2_.refs_3_.refs_5_), channel_id=1, source_target_pairs={{0,2},{2,4},{4,6},{6,8},{8,10},{10,12},{12,14},{14,0},{16,18},{18,... | collective-permute-start | bytes 835592 | tf_op jit(solution)/shard_map/ppermute | solution.py:474
  29.0 37.9 %copy-start.1 = (bf16[272,512]{1,0:T(8,128)(2,1)}, bf16[272,512]{1,0:T(8,128)(2,1)S(1)}, u32[]{:S(2)}) copy-start(bf16[272,512]{1,0:T(8,128)(2,1)S(1)} %collective-permute-done.5.refs_8_.refs_2_.refs_3_.refs_7_) | copy-start | bytes 835588
  34.5 32.3 %copy-start.7 = (bf16[272,512]{1,0:T(8,128)(2,1)}, bf16[272,512]{1,0:T(8,128)(2,1)S(1)}, u32[]{:S(2)}) copy-start(bf16[272,512]{1,0:T(8,128)(2,1)S(1)} %collective-permute-done.3.refs_3_.refs_2_.refs_4_) | copy-start | bytes 835588
  36.9 30.0 %copy-start.8 = (bf16[272,512]{1,0:T(8,128)(2,1)}, bf16[272,512]{1,0:T(8,128)(2,1)S(1)}, u32[]{:S(2)}) copy-start(bf16[272,512]{1,0:T(8,128)(2,1)S(1)} %collective-permute-done.4.refs_4_.refs_1_.refs_3_) | copy-start | bytes 835588
  36.9 7.5 %collective-permute-start.6 = (bf16[272,512]{1,0:T(8,128)(2,1)S(1)}, bf16[272,512]{1,0:T(8,128)(2,1)S(1)}, u32[]{:S(2)}, u32[]{:S(2)}) collective-permute-start(bf16[272,512]{1,0:T(8,128)(2,1)S(1)} %collective-permute-done.3.refs_3_.refs_2_.refs_4_), channel_id=1, source_target_pairs={{0,14},{2,0},{4,2},{6,4},{8,6},{10,8},{12,10},{14,12},{16,30},{18,... | collective-permute-start | bytes 835592 | tf_op jit(solution)/shard_map/ppermute | solution.py:473
  37.2 7.8 %collective-permute-start.7 = (bf16[272,512]{1,0:T(8,128)(2,1)S(1)}, bf16[272,512]{1,0:T(8,128)(2,1)S(1)}, u32[]{:S(2)}, u32[]{:S(2)}) collective-permute-start(bf16[272,512]{1,0:T(8,128)(2,1)S(1)} %collective-permute-done.4.refs_4_.refs_1_.refs_3_), channel_id=1, source_target_pairs={{0,2},{2,4},{4,6},{6,8},{8,10},{10,12},{12,14},{14,0},{16,18},{18,... | collective-permute-start | bytes 835592 | tf_op jit(solution)/shard_map/ppermute | solution.py:474
  44.4 27.5 %copy-start.9 = (bf16[272,512]{1,0:T(8,128)(2,1)}, bf16[272,512]{1,0:T(8,128)(2,1)S(1)}, u32[]{:S(2)}) copy-start(bf16[272,512]{1,0:T(8,128)(2,1)S(1)} %collective-permute-done.6.refs_5_.refs_0_.refs_2_) | copy-start | bytes 835588
  44.4 6.5 %collective-permute-start.8 = (bf16[272,512]{1,0:T(8,128)(2,1)S(1)}, bf16[272,512]{1,0:T(8,128)(2,1)S(1)}, u32[]{:S(2)}, u32[]{:S(2)}) collective-permute-start(bf16[272,512]{1,0:T(8,128)(2,1)S(1)} %collective-permute-done.6.refs_5_.refs_0_.refs_2_), channel_id=1, source_target_pairs={{0,14},{2,0},{4,2},{6,4},{8,6},{10,8},{12,10},{14,12},{16,30},{18,... | collective-permute-start | bytes 835592 | tf_op jit(solution)/shard_map/ppermute | solution.py:484
  45.0 21.9 %copy-start.10 = (bf16[272,512]{1,0:T(8,128)(2,1)}, bf16[272,512]{1,0:T(8,128)(2,1)S(1)}, u32[]{:S(2)}) copy-start(bf16[272,512]{1,0:T(8,128)(2,1)S(1)} %collective-permute-done.7.refs_6_.refs_1_) | copy-start | bytes 835588
  50.4 21.5 %copy-start.3 = (f32[11,128,128]{2,1,0:T(8,128)}, f32[11,128,128]{2,1,0:T(8,128)S(1)}, u32[]{:S(2)}) copy-start(f32[11,128,128]{2,1,0:T(8,128)S(1)} %get-tuple-element.51.refs_5_.refs_9_) | copy-start | bytes 2162692
  50.9 24.5 %copy-start.4 = (bf16[272,512]{1,0:T(8,128)(2,1)}, bf16[272,512]{1,0:T(8,128)(2,1)S(1)}, u32[]{:S(2)}) copy-start(bf16[272,512]{1,0:T(8,128)(2,1)S(1)} %collective-permute-done.8.refs_0_) | copy-start | bytes 835588
  68.5 6.9 %collective-permute-start.9 = (bf16[128,512]{1,0:T(8,128)(2,1)S(1)}, bf16[128,512]{1,0:T(8,128)(2,1)S(1)}, u32[]{:S(2)}, u32[]{:S(2)}) collective-permute-start(bf16[128,512]{1,0:T(8,128)(2,1)S(1)} %get-tuple-element.57), channel_id=1, source_target_pairs={{0,2},{2,4},{4,6},{6,8},{8,10},{10,12},{12,14},{14,0},{16,18},{18,... | collective-permute-start | bytes 393224 | tf_op jit(solution)/shard_map/ppermute | solution.py:540
  68.6 6.9 %collective-permute-start.10 = (bf16[128,512]{1,0:T(8,128)(2,1)S(1)}, bf16[128,512]{1,0:T(8,128)(2,1)S(1)}, u32[]{:S(2)}, u32[]{:S(2)}) collective-permute-start(bf16[128,512]{1,0:T(8,128)(2,1)S(1)} %get-tuple-element.58), channel_id=1, source_target_pairs={{0,14},{2,0},{4,2},{6,4},{8,6},{10,8},{12,10},{14,12},{16,30},{18,... | collective-permute-start | bytes 393224 | tf_op jit(solution)/shard_map/ppermute | solution.py:543
  75.5 6.5 %collective-permute-start.12 = (bf16[128,512]{1,0:T(8,128)(2,1)S(1)}, bf16[128,512]{1,0:T(8,128)(2,1)S(1)}, u32[]{:S(2)}, u32[]{:S(2)}) collective-permute-start(bf16[128,512]{1,0:T(8,128)(2,1)S(1)} %add_convert_fusion.2), channel_id=1, source_target_pairs={{0,14},{2,0},{4,2},{6,4},{8,6},{10,8},{12,10},{14,12},{16,30},{18,... | collective-permute-start | bytes 393224 | tf_op jit(solution)/shard_map/ppermute | solution.py:543
  78.4 6.3 %collective-permute-start.11 = (bf16[128,512]{1,0:T(8,128)(2,1)S(1)}, bf16[128,512]{1,0:T(8,128)(2,1)S(1)}, u32[]{:S(2)}, u32[]{:S(2)}) collective-permute-start(bf16[128,512]{1,0:T(8,128)(2,1)S(1)} %add_convert_fusion.3), channel_id=1, source_target_pairs={{0,2},{2,4},{4,6},{6,8},{8,10},{10,12},{12,14},{14,0},{16,18},{18,... | collective-permute-start | bytes 393224 | tf_op jit(solution)/shard_map/ppermute | solution.py:540
  84.7 11.4 %collective-permute-start.13 = (f32[128,512]{1,0:T(8,128)S(1)}, f32[128,512]{1,0:T(8,128)S(1)}, u32[]{:S(2)}, u32[]{:S(2)}) collective-permute-start(f32[128,512]{1,0:T(8,128)S(1)} %convert_add_fusion.1), channel_id=1, source_target_pairs={{0,2},{2,4},{4,6},{6,8},{8,10},{10,12},{12,14},{14,0},{16,18},{18,... | collective-permute-start | bytes 786440 | tf_op jit(solution)/shard_map/ppermute | solution.py:540
  84.8 11.4 %collective-permute-start.16 = (bf16[256,512]{1,0:T(8,128)(2,1)S(1)}, bf16[256,512]{1,0:T(8,128)(2,1)S(1)}, u32[]{:S(2)}, u32[]{:S(2)}) collective-permute-start(bf16[256,512]{1,0:T(8,128)(2,1)S(1)} %get-tuple-element.75), channel_id=1, source_target_pairs={{24,8},{26,10},{28,12},{30,14},{40,24},{42,26},{44,28},{46,30},{56... | collective-permute-start | bytes 786440 | tf_op jit(solution)/shard_map/ppermute | solution.py:572
  85.5 12.5 %all-to-all-start.2 = ((bf16[16,8,1024]{2,1,0:T(8,128)(2,1)}), bf16[16,8,1024]{2,1,0:T(8,128)(2,1)S(1)}, u32[]{:S(2)}, u32[]{:S(2)}) async-start(bf16[16,8,1024]{2,1,0:T(8,128)(2,1)} %bitcast.2), calls=%async_computation.2 | async-start | bytes 524288 | tf_op jit(solution)/shard_map/all_to_all | solution.py:573
  90.6 10.2 %collective-permute-start.15 = (f32[128,512]{1,0:T(8,128)S(1)}, f32[128,512]{1,0:T(8,128)S(1)}, u32[]{:S(2)}, u32[]{:S(2)}) collective-permute-start(f32[128,512]{1,0:T(8,128)S(1)} %convert_add_fusion), channel_id=1, source_target_pairs={{0,14},{2,0},{4,2},{6,4},{8,6},{10,8},{12,10},{14,12},{16,30},{18,... | collective-permute-start | bytes 786440 | tf_op jit(solution)/shard_map/ppermute | solution.py:543
  96.2 6.3 %collective-permute-start.14 = (bf16[128,512]{1,0:T(8,128)(2,1)S(1)}, bf16[128,512]{1,0:T(8,128)(2,1)S(1)}, u32[]{:S(2)}, u32[]{:S(2)}) collective-permute-start(bf16[128,512]{1,0:T(8,128)(2,1)S(1)} %add_convert_fusion.1), channel_id=1, source_target_pairs={{0,2},{2,4},{4,6},{6,8},{8,10},{10,12},{12,14},{14,0},{16,18},{18,... | collective-permute-start | bytes 393224 | tf_op jit(solution)/shard_map/ppermute | solution.py:540
  96.3 1.8 %copy-start.12 = (bf16[256,512]{1,0:T(8,128)(2,1)}, bf16[256,512]{1,0:T(8,128)(2,1)S(1)}, u32[]{:S(2)}) copy-start(bf16[256,512]{1,0:T(8,128)(2,1)S(1)} %collective-permute-done.16.arrived) | copy-start | bytes 786436
  98.0 0.7 copy-start.11

commit v7 on v6

--- a/solution.py
+++ b/solution.py
@@ -205,6 +205,21 @@
     return [o for o in order if o <= REACH] + [REACH + 1 + o for o in order]
 
 
+class BiasBlocks:
+    def __init__(self, *groups):
+        self.where = {
+            block: (ref, i) for order, ref in groups for i, block in enumerate(bias_blocks(order))
+        }
+
+    def __getitem__(self, block):
+        ref, i = self.where[block]
+        return ref[i]
+
+    def __setitem__(self, block, value):
+        ref, i = self.where[block]
+        ref[i] = value
+
+
 def products(packed, pairs, keys, bias, h, o):
     _, z = place()
     cols = slice(h * HD, (h + 1) * HD)
@@ -226,7 +241,8 @@
 def stats_kernel(order, *refs):
     chunks, (own, previous, sums), refs = refs[: len(order)], refs[len(order) : len(order) + 3], refs[len(order) + 3 :]
     earlier, refs = (refs[0], refs[1:]) if len(order) < REACH else (None, refs)
-    stats, bias_out, packed, pairs, keys, bias, key_sems, chunk_sems, bias_sems = refs
+    stats, bias_out, packed, pairs, keys, key_sems, chunk_sems = refs
+    bias = BiasBlocks((order, bias_out))
     key_copies = load_keys(own, previous, sums, pairs, keys, key_sems)
     copies = [
         pltpu.make_async_copy(chunk, packed.at[o], chunk_sems.at[o])
@@ -237,14 +253,9 @@
     for copy in key_copies:
         copy.wait()
     masks = Bias(packed, pairs)
-    writes = []
     for i, o in enumerate(order):
         copies[i].wait()
         masks.build(o, bias)
-        for block in bias_blocks((o,)):
-            place_out = bias_out.at[bias_blocks(order).index(block)]
-            writes.append(pltpu.make_async_copy(bias.at[block], place_out, bias_sems.at[block]))
-            writes[-1].start()
         chunk = jnp.bitwise_and(masks.z + o, NZ - 1)
         log_sums, means = [], []
         made = [products(packed, pairs, keys, bias, h, o) for h in range(HEADS_HERE)]
@@ -263,8 +274,6 @@
         for peer in range(NZ):
             stats[peer] = earlier[...]
             stats[peer, chunk] = merged
-    for copy in writes:
-        copy.wait()
 
 
 def merge_stats(stats, merged):
@@ -288,17 +297,14 @@
     chunks, (own, previous, sums, bias_most, bias_last, stats_in), refs = refs[:count], refs[count : count + 6], refs[count + 6 :]
     query_grads, (coarse, window), refs = refs[:count], refs[count : count + 2], refs[count + 2 :]
     merged_out, refs = (refs[0], refs[1:]) if merging else (None, refs)
-    packed, pairs, keys, bias, stats, merged, key_sems, chunk_sems, bias_sems, stats_sem = refs
+    packed, pairs, keys, stats, merged, key_sems, chunk_sems, stats_sem = refs
+    bias = BiasBlocks((EARLY, bias_most), (LATE, bias_last))
     stats_copy = pltpu.make_async_copy(stats_in, stats, stats_sem)
     stats_copy.start()
     key_copies = load_keys(own, previous, sums, pairs, keys, key_sems)
     copies = []
     for i, o in enumerate(order):
         mine = [pltpu.make_async_copy(chunks[i], packed.at[o], chunk_sems.at[o])]
-        for block in bias_blocks((o,)):
-            source, among = (bias_most, EARLY) if o in EARLY else (bias_last, LATE)
-            source = source.at[bias_blocks(among).index(block)]
-            mine.append(pltpu.make_async_copy(source, bias.at[block], bias_sems.at[block]))
         for copy in mine:
             copy.start()
         copies.append(mine)
@@ -491,22 +497,24 @@
         VMEM((NZ, ROWS, FEAT), BF16),
         VMEM((2, ROWS, FEAT), BF16),
         VMEM((bars, 2 * FEAT), BF16),
-        VMEM(bias_shape, F32),
     ]
     def stats_of(order, *earlier):
         out = (shape(stats_shape, F32),) if earlier else (shape(stats_shape[1:], F32),)
         blocks = (len(bias_blocks(order)),) + bias_shape[1:]
         return pl.pallas_call(
             lambda *refs: stats_kernel(order, *refs),
-            out_shape=out + (shape(blocks, F32),),
+            out_shape=out + (VMEM(blocks, F32),),
             in_specs=[whole(HBM)] * (len(order) + 3) + [whole(VMEM)] * len(earlier),
-            out_specs=(whole(VMEM), whole(HBM)),
-            scratch_shapes=held + [dma((3,)), dma((NZ,)), dma(bias_shape[:1])],
+            out_specs=(whole(VMEM),) * 2,
+            scratch_shapes=held + [dma((3,)), dma((NZ,))],
             compiler_params=params,
         )(*[chunks[o] for o in order], own, previous, all_sums, *earlier)
 
     partial_stats, bias_most = stats_of(EARLY)
     stats, bias_last = stats_of(LATE, partial_stats)
+    bias_most, bias_last = (
+        pltpu.with_memory_space_constraint(array, VMEM) for array in (bias_most, bias_last)
+    )
 
     stats = lax.all_to_all(stats, "seq", 0, 0, axis_index_groups=Z_GROUPS)
 
@@ -520,7 +528,7 @@
             out_shape=(shape((TOK, FEAT)),) * len(order)
             + (VMEM(coarse_shape, BF16), VMEM(window_shape, BF16))
             + (shape(stats_shape[1:], F32),) * merging,
-            in_specs=[whole(HBM)] * (len(order) + 6),
+            in_specs=[whole(HBM)] * (len(order) + 3) + [whole(VMEM)] * 2 + [whole(HBM)],
             out_specs=(whole(VMEM),) * (len(order) + 2 + merging),
             scratch_shapes=held
             + [
@@ -528,7 +536,6 @@
                 VMEM(stats_shape[1:], F32),
                 dma((3,)),
                 dma((NZ,)),
-                dma(bias_shape[:1]),
                 dma,
             ],
             compiler_params=params,

time: 104 us -> 103 us (level)
  Pallas kernels: 22.3 us -> 20.8 us
  waiting for transfers between devices: 26.9 us -> 28.2 us
    pallas_call x2, Pallas kernels: 6.58 us -> 4.42 us  [stats_of(): pl.pallas_call(lambda *refs: stats_kernel(order, *refs), out_shape=out +...]
    ppermute x1, waiting for transfers between devices: 0.55 us -> 2.3 us  [shards(): after.append(lax.ppermute(after[-1], 'seq', TO_PREVIOUS))]
    ppermute x3, starting transfers between devices: 11.6 us -> 10.4 us  [backward_step(): return lax.ppermute(array, 'seq', TO_PREVIOUS)]
  transfers between devices with their start and end apart: 19 -> 19, of which waited for: 8 -> 8; matrix products, arithmetic and copies ran while one was open for 0% -> 0% of each run, Pallas kernels for 17% -> 16%
where the time goes in v7:
time: 103 us
  starting transfers between devices  35.8 us (35%)
  waiting for transfers between devices  28.2 us (27%)
  Pallas kernels  20.8 us (20%)
  blocking collectives  15.7 us (15%)
    all_to_all x1, blocking collectives, shards(): stats = lax.all_to_all(stats, 'seq', 0, 0, axis_index_groups=Z_GROUPS)  15.7 us
    ppermute x3, waiting for transfers between devices, ring_step(): after.append(lax.ppermute(after[-1], 'seq', TO_PREVIOUS))  11 us
    ppermute x3, starting transfers between devices, backward_step(): return lax.ppermute(array, 'seq', TO_PREVIOUS)  10.4 us
    all_to_all x1, starting transfers between devices, shards(): all_sums = lax.all_to_all(sums, 'seq', 0, 0, axis_index_groups=XY_GROUPS)  7.48 us
    all_to_all x1, waiting for transfers between devices, shards(): all_sums = lax.all_to_all(sums, 'seq', 0, 0, axis_index_groups=XY_GROUPS)  7.01 us
    ppermute x3, starting transfers between devices, ring_step(): after.append(lax.ppermute(after[-1], 'seq', TO_PREVIOUS))  6.12 us
    pallas_call x2, Pallas kernels, query_grads(): pl.pallas_call(lambda *refs: query_grad_kernel(order, *refs), out_shape=(...  5.79 us
    all_to_all x1, starting transfers between devices, shards(): lax.all_to_all(sum_grad.reshape(NXY, BARS_HERE, 2 * FEAT), 'seq', 0, 0, a...  4.76 us
  transfers between devices with their start and end apart: 19, of which 8 were waited for; matrix products, arithmetic and copies ran while one was open for 0% of the time, Pallas kernels for 16%

profile of v7, /device:TPU:2, one launch (start us, length us, event | category | flops | bytes accessed | tf_op | source)
XLA Modules:
  0.0 103.0 jit_solution(7437420303789101321)
XLA Ops:
  0.6 0.1 collective-permute-start
  0.7 3.1 %shard_map.103 = (f32[512,128]{1,0:T(8,128)S(1)}, bf16[272,512]{1,0:T(8,128)(2,1)S(1)}, bf16[272,512]{1,0:T(8,128)(2,1)S(1)}, bf16[16,8,1024]{2,1,0:T(8,128)(2,1)}) custom-call(s32[1]{0:T(128)} %bitcast.core, s32[8]{0:T(128)} %starts.3, s32[8,8]{1,0:T(8,128)} %related.1, s32[8]{0:T(128)} %slots.3, bf16[128,512]{1,0:T(8,128)(2,1)} %queries.1, ...), custom_call_target="tpu_custom_call" | custom-call | tf_op jit(solution)/shard_map/pallas_call | solution.py:445
  3.8 0.0 copy-start.1
  3.8 0.0 collective-permute-done.grad_other
  3.8 1.8 %shard_map.104.refs_0_.refs_5_.refs_7_ = bf16[272,512]{1,0:T(8,128)(2,1)S(1)} custom-call(s32[1]{0:T(128)} %bitcast.core, bf16[272,512]{1,0:T(8,128)(2,1)S(1)} %get-tuple-element.41.pack, f32[512,128]{1,0:T(8,128)S(1)} %get-tuple-element.42.partial, bf16[128,1024]{1,0:T(8,128)(2,1)S(1)} %collective-permute-done.grad_other, bf16[512,2048]{1,0:T(8,128)(2,1)} %out_weight.3), custom_call_target="tpu_custom_call" | custom-call | tf_op jit(solution)/shard_map/pallas_call | solution.py:462
  5.7 0.0 copy-start.3
  5.7 2.0 %collective-permute-start.2 = (bf16[272,512]{1,0:T(8,128)(2,1)S(1)}, bf16[272,512]{1,0:T(8,128)(2,1)S(1)}, u32[]{:S(2)}, u32[]{:S(2)}) collective-permute-start(bf16[272,512]{1,0:T(8,128)(2,1)S(1)} %shard_map.104.refs_0_.refs_5_.refs_7_), channel_id=1, source_target_pairs={{0,2},{2,4},{4,6},{6,8},{8,10},{10,12},{12,14},{14,0},{16,18},{18,... | collective-permute-start | bytes 835592 | tf_op jit(solution)/shard_map/ppermute | solution.py:480
  7.7 4.0 %collective-permute-start.1 = (bf16[272,512]{1,0:T(8,128)(2,1)S(1)}, bf16[272,512]{1,0:T(8,128)(2,1)S(1)}, u32[]{:S(2)}, u32[]{:S(2)}) collective-permute-start(bf16[272,512]{1,0:T(8,128)(2,1)S(1)} %shard_map.104.refs_0_.refs_5_.refs_7_), channel_id=1, source_target_pairs={{0,14},{2,0},{4,2},{6,4},{8,6},{10,8},{12,10},{14,12},{16,30},{18,... | collective-permute-start | bytes 835592 | tf_op jit(solution)/shard_map/ppermute | solution.py:479
  11.7 7.5 %all-to-all-start = ((bf16[16,8,1024]{2,1,0:T(8,128)(2,1)}), bf16[16,8,1024]{2,1,0:T(8,128)(2,1)S(1)}, u32[]{:S(2)}, u32[]{:S(2)}) async-start(bf16[16,8,1024]{2,1,0:T(8,128)(2,1)} %get-tuple-element.43), calls=%async_computation | async-start | bytes 524288 | tf_op jit(solution)/shard_map/all_to_all | solution.py:483
  19.2 0.7 collective-permute-start.5
  19.9 7.0 %all-to-all-done = bf16[16,8,1024]{2,1,0:T(8,128)(2,1)S(1)} async-done(((bf16[16,8,1024]{2,1,0:T(8,128)(2,1)}), bf16[16,8,1024]{2,1,0:T(8,128)(2,1)S(1)}, u32[]{:S(2)}, u32[]{:S(2)}) %all-to-all-start) | async-done | bytes 262176 | tf_op jit(solution)/shard_map/all_to_all | solution.py:483
  26.9 0.0 collective-permute-done.2.refs_2_.refs_3_.refs_5_
  26.9 0.0 collective-permute-done.1.refs_1_.refs_4_.refs_6_
  26.9 0.0 copy-start.6
  26.9 1.7 %collective-permute-start.3 = (bf16[272,512]{1,0:T(8,128)(2,1)S(1)}, bf16[272,512]{1,0:T(8,128)(2,1)S(1)}, u32[]{:S(2)}, u32[]{:S(2)}) collective-permute-start(bf16[272,512]{1,0:T(8,128)(2,1)S(1)} %collective-permute-done.1.refs_1_.refs_4_.refs_6_), channel_id=1, source_target_pairs={{0,14},{2,0},{4,2},{6,4},{8,6},{10,8},{12,10},{14,12},{16,30},{18,... | collective-permute-start | bytes 835592 | tf_op jit(solution)/shard_map/ppermute | solution.py:479
  28.6 0.4 collective-permute-start.4
  29.0 0.0 collective-permute-done.5.refs_8_.refs_2_.refs_3_.refs_7_
  29.0 5.5 %collective-permute-done.3.refs_3_.refs_2_.refs_4_ = bf16[272,512]{1,0:T(8,128)(2,1)S(1)} collective-permute-done((bf16[272,512]{1,0:T(8,128)(2,1)S(1)}, bf16[272,512]{1,0:T(8,128)(2,1)S(1)}, u32[]{:S(2)}, u32[]{:S(2)}) %collective-permute-start.3) | collective-permute-done | bytes 278560 | tf_op jit(solution)/shard_map/ppermute | solution.py:479
  34.5 2.3 %collective-permute-done.4.refs_4_.refs_1_.refs_3_ = bf16[272,512]{1,0:T(8,128)(2,1)S(1)} collective-permute-done((bf16[272,512]{1,0:T(8,128)(2,1)S(1)}, bf16[272,512]{1,0:T(8,128)(2,1)S(1)}, u32[]{:S(2)}, u32[]{:S(2)}) %collective-permute-start.4) | collective-permute-done | bytes 278560 | tf_op jit(solution)/shard_map/ppermute | solution.py:480
  36.9 0.4 collective-permute-start.6
  37.2 1.7 %collective-permute-start.7 = (bf16[272,512]{1,0:T(8,128)(2,1)S(1)}, bf16[272,512]{1,0:T(8,128)(2,1)S(1)}, u32[]{:S(2)}, u32[]{:S(2)}) collective-permute-start(bf16[272,512]{1,0:T(8,128)(2,1)S(1)} %collective-permute-done.4.refs_4_.refs_1_.refs_3_), channel_id=1, source_target_pairs={{0,2},{2,4},{4,6},{6,8},{8,10},{10,12},{12,14},{14,0},{16,18},{18,... | collective-permute-start | bytes 835592 | tf_op jit(solution)/shard_map/ppermute | solution.py:480
  38.9 5.5 %collective-permute-done.6.refs_5_.refs_0_.refs_2_ = bf16[272,512]{1,0:T(8,128)(2,1)S(1)} collective-permute-done((bf16[272,512]{1,0:T(8,128)(2,1)S(1)}, bf16[272,512]{1,0:T(8,128)(2,1)S(1)}, u32[]{:S(2)}, u32[]{:S(2)}) %collective-permute-start.6) | collective-permute-done | bytes 278560 | tf_op jit(solution)/shard_map/ppermute | solution.py:479
  44.4 0.6 collective-permute-start.8
  45.0 0.0 collective-permute-done.7.refs_6_.refs_1_
  45.0 3.6 %shard_map.105 = (f32[8,8,128]{2,1,0:T(8,128)S(1)}, f32[11,128,128]{2,1,0:T(8,128)S(1)}) custom-call(bf16[272,512]{1,0:T(8,128)(2,1)S(1)} %shard_map.104.refs_0_.refs_5_.refs_7_, bf16[272,512]{1,0:T(8,128)(2,1)S(1)} %collective-permute-done.1.refs_1_.refs_4_.refs_6_, bf16[272,512]{1,0:T(8,128)(2,1)S(1)} %collective-permute-done.2.refs_2_.refs_3_.refs_5_, ...), custom_call_target="tpu_custom_call" | custom-call | tf_op jit(solution)/shard_map/pallas_call | solution.py:504
  48.6 2.3 %collective-permute-done.8.refs_0_ = bf16[272,512]{1,0:T(8,128)(2,1)S(1)} collective-permute-done((bf16[272,512]{1,0:T(8,128)(2,1)S(1)}, bf16[272,512]{1,0:T(8,128)(2,1)S(1)}, u32[]{:S(2)}, u32[]{:S(2)}) %collective-permute-start.8) | collective-permute-done | bytes 278560 | tf_op jit(solution)/shard_map/ppermute | solution.py:490
  50.9 0.8 shard_map.106
  51.7 0.0 copy-done.3
  51.8 15.7 %all_to_all.15.refs_7_ = f32[8,8,8,128]{3,2,1,0:T(8,128)S(1)} all-to-all(f32[8,8,8,128]{3,2,1,0:T(8,128)S(1)} %get-tuple-element.54), channel_id=1, replica_groups={{0,2,4,6,8,10,12,14},{16,18,20,22,24,26,28,30},{32,34,36,38,40,42,44,46..., dimensions={0} | all-to-all | bytes 524288 | tf_op jit(solution)/shard_map/all_to_all | solution.py:519
  67.4 0.0 copy-done.5
  67.4 0.0 copy-done.6
  67.5 0.0 copy-done.7
  67.5 0.0 copy-done.8
  67.5 0.0 copy-done.9
  67.5 0.0 copy-done.1
  67.5 0.0 copy-done
  67.5 1.2 %shard_map.107 = (bf16[128,512]{1,0:T(8,128)(2,1)S(1)}, bf16[128,512]{1,0:T(8,128)(2,1)S(1)}, bf16[2,2,4,128,128]{4,3,2,1,0:T(8,128)(2,1)S(1)}, bf16[1,2,4,128,128]{4,3,2,1,0:T(8,128)(2,1)S(1)}, f32[8,8,128]{2,1,0:T(8,128)S(1)}) custom-call(bf16[272,512]{1,0:T(8,128)(2,1)S(1)} %collective-permute-done.8.refs_0_, ...), custom_call_target="tpu_custom_call" | custom-call | tf_op jit(solution)/shard_map/pallas_call | solution.py:526
  68.8 0.3 collective-permute-start.9
  69.0 3.2 %collective-permute-start.10 = (bf16[128,512]{1,0:T(8,128)(2,1)S(1)}, bf16[128,512]{1,0:T(8,128)(2,1)S(1)}, u32[]{:S(2)}, u32[]{:S(2)}) collective-permute-start(bf16[128,512]{1,0:T(8,128)(2,1)S(1)} %get-tuple-element.58), channel_id=1, source_target_pairs={{0,14},{2,0},{4,2},{6,4},{8,6},{10,8},{12,10},{14,12},{16,30},{18,... | collective-permute-start | bytes 393224 | tf_op jit(solution)/shard_map/ppermute | solution.py:550
  72.3 4.6 %shard_map.108 = (bf16[128,512]{1,0:T(8,128)(2,1)S(1)}, bf16[128,512]{1,0:T(8,128)(2,1)S(1)}, bf16[128,512]{1,0:T(8,128)(2,1)S(1)}, bf16[128,512]{1,0:T(8,128)(2...) custom-call(bf16[272,512]{1,0:T(8,128)(2,1)} %copy-done.9, ...), custom_call_target="tpu_custom_call" | custom-call | tf_op jit(solution)/shard_map/pallas_call | solution.py:526
  76.8 0.0 copy-done.4
  76.8 0.0 collective-permute-done.9
  76.8 0.0 collective-permute-done.10
  76.9 1.7 %collective-permute-start.12 = (bf16[128,512]{1,0:T(8,128)(2,1)S(1)}, bf16[128,512]{1,0:T(8,128)(2,1)S(1)}, u32[]{:S(2)}, u32[]{:S(2)}) collective-permute-start(bf16[128,512]{1,0:T(8,128)(2,1)S(1)} %add_convert_fusion.2), channel_id=1, source_target_pairs={{0,14},{2,0},{4,2},{6,4},{8,6},{10,8},{12,10},{14,12},{16,30},{18,... | collective-permute-start | bytes 393224 | tf_op jit(solution)/shard_map/ppermute | solution.py:550
  78.6 0.5 collective-permute-start.11
  79.1 3.5 %shard_map.109 = (bf16[256,512]{1,0:T(8,128)(2,1)S(1)}, f32[256,512]{1,0:T(8,128)}, bf16[128,1024]{1,0:T(8,128)(2,1)}) custom-call(bf16[272,512]{1,0:T(8,128)(2,1)} %copy-done.4, bf16[272,512]{1,0:T(8,128)(2,1)} %copy-done.10, bf16[272,512]{1,0:T(8,128)(2,1)} %copy-done.9, bf16[272,512]{1,0:T(8,128)(2,1)} %copy-done.8, bf16[272,512]{1,0:T(8,128)(2,1)} %copy-done.7, ...), custom_call_target="tpu_custom_call" | custom-call | tf_op jit(solution)/shard_map/pallas_call | solution.py:558
  82.6 0.0 copy-start.13
  82.6 0.0 collective-permute-done.12
  82.6 2.2 %collective-permute-done.11 = bf16[128,512]{1,0:T(8,128)(2,1)S(1)} collective-permute-done((bf16[128,512]{1,0:T(8,128)(2,1)S(1)}, bf16[128,512]{1,0:T(8,128)(2,1)S(1)}, u32[]{:S(2)}, u32[]{:S(2)}) %collective-permute-start.11) | collective-permute-done | bytes 131104 | tf_op jit(solution)/shard_map/ppermute | solution.py:547
  84.9 0.1 collective-permute-start.13
  85.0 0.7 collective-permute-start.16
  85.7 4.8 %all-to-all-start.2 = ((bf16[16,8,1024]{2,1,0:T(8,128)(2,1)}), bf16[16,8,1024]{2,1,0:T(8,128)(2,1)S(1)}, u32[]{:S(2)}, u32[]{:S(2)}) async-start(bf16[16,8,1024]{2,1,0:T(8,128)(2,1)} %bitcast.2), calls=%async_computation.2 | async-start | bytes 524288 | tf_op jit(solution)/shard_map/all_to_all | solution.py:580
  90.4 5.5 %collective-permute-start.15 = (f32[128,512]{1,0:T(8,128)S(1)}, f32[128,512]{1,0:T(8,128)S(1)}, u32[]{:S(2)}, u32[]{:S(2)}) collective-permute-start(f32[128,512]{1,0:T(8,128)S(1)} %convert_add_fusion), channel_id=1, source_target_pairs={{0,14},{2,0},{4,2},{6,4},{8,6},{10,8},{12,10},{14,12},{16,30},{18,... | collective-permute-start | bytes 786440 | tf_op jit(solution)/shard_map/ppermute | solution.py:550
  96.0 0.0 collective-permute-done.13
  96.0 0.1 collective-permute-start.14
  96.1 0.0 collective-permute-done.16.arrived
  96.1 0.0 copy-start.12
  96.1 1.7 %all-to-all-done.2.parts = bf16[16,8,1024]{2,1,0:T(8,128)(2,1)S(1)} async-done(((bf16[16,8,1024]{2,1,0:T(8,128)(2,1)}), bf16[16,8,1024]{2,1,0:T(8,128)(2,1)S(1)}, u32[]{:S(2)}, u32[]{:S(2)}) %all-to-all-start.2) | async-done | bytes 262176 | tf_op jit(solution)/shard_map/all_to_all | solution.py:580
  97.8 0.7 copy-done.11
  98.5 2.2 %shard_map.110 = (bf16[128,512]{1,0:T(8,128)(2,1)}, bf16[128,512]{1,0:T(8,128)(2,1)}) custom-call(s32[8]{0:T(128)} %starts.3, s32[8]{0:T(128)} %slots.3, f32[256,512]{1,0:T(8,128)} %get-tuple-element.74.own_grad, bf16[256,512]{1,0:T(8,128)(2,1)} %copy-done.12, bf16[16,8,1024]{2,1,0:T(8,128)(2,1)} %copy-done.11), custom_call_target="tpu_custom_call" | custom-call | tf_op jit(solution)/shard_map/pallas_call | solution.py:585
  100.7 0.0 collective-permute-done.15
  100.7 1.6 %collective-permute-done.14 = bf16[128,512]{1,0:T(8,128)(2,1)S(1)} collective-permute-done((bf16[128,512]{1,0:T(8,128)(2,1)S(1)}, bf16[128,512]{1,0:T(8,128)(2,1)S(1)}, u32[]{:S(2)}, u32[]{:S(2)}) %collective-permute-start.14) | collective-permute-done | bytes 131104 | tf_op jit(solution)/shard_map/ppermute | solution.py:547
  102.3 0.0 copy-done.13
  102.3 0.7 add_convert_fusion
  (19 shorter events, 0.2 us)
Async XLA Ops:
  0.6 3.2 %collective-permute-start = (bf16[128,1024]{1,0:T(8,128)(2,1)}, bf16[128,1024]{1,0:T(8,128)(2,1)S(1)}, u32[]{:S(2)}, u32[]{:S(2)}) collective-permute-start(bf16[128,1024]{1,0:T(8,128)(2,1)} %grad_own.1), channel_id=1, source_target_pairs={{0,1},{1,0},{2,3},{3,2},{4,5},{5,4},{6,7},{7,6},{8,9},{9,8},{10,11... | collective-permute-start | bytes 786440 | tf_op jit(solution)/shard_map/ppermute | solution.py:442
  3.8 63.7 %copy-start.1 = (bf16[272,512]{1,0:T(8,128)(2,1)}, bf16[272,512]{1,0:T(8,128)(2,1)S(1)}, u32[]{:S(2)}) copy-start(bf16[272,512]{1,0:T(8,128)(2,1)S(1)} %get-tuple-element.46.refs_7_.refs_1_.refs_2_.refs_6_) | copy-start | bytes 835588
  5.7 46.1 %copy-start.3 = (bf16[272,512]{1,0:T(8,128)(2,1)}, bf16[272,512]{1,0:T(8,128)(2,1)S(1)}, u32[]{:S(2)}) copy-start(bf16[272,512]{1,0:T(8,128)(2,1)S(1)} %shard_map.104.refs_0_.refs_5_.refs_7_) | copy-start | bytes 835588
  5.7 21.2 %collective-permute-start.2 = (bf16[272,512]{1,0:T(8,128)(2,1)S(1)}, bf16[272,512]{1,0:T(8,128)(2,1)S(1)}, u32[]{:S(2)}, u32[]{:S(2)}) collective-permute-start(bf16[272,512]{1,0:T(8,128)(2,1)S(1)} %shard_map.104.refs_0_.refs_5_.refs_7_), channel_id=1, source_target_pairs={{0,2},{2,4},{4,6},{6,8},{8,10},{10,12},{12,14},{14,0},{16,18},{18,... | collective-permute-start | bytes 835592 | tf_op jit(solution)/shard_map/ppermute | solution.py:480
  7.7 19.2 %collective-permute-start.1 = (bf16[272,512]{1,0:T(8,128)(2,1)S(1)}, bf16[272,512]{1,0:T(8,128)(2,1)S(1)}, u32[]{:S(2)}, u32[]{:S(2)}) collective-permute-start(bf16[272,512]{1,0:T(8,128)(2,1)S(1)} %shard_map.104.refs_0_.refs_5_.refs_7_), channel_id=1, source_target_pairs={{0,14},{2,0},{4,2},{6,4},{8,6},{10,8},{12,10},{14,12},{16,30},{18,... | collective-permute-start | bytes 835592 | tf_op jit(solution)/shard_map/ppermute | solution.py:479
  11.7 15.2 %all-to-all-start = ((bf16[16,8,1024]{2,1,0:T(8,128)(2,1)}), bf16[16,8,1024]{2,1,0:T(8,128)(2,1)S(1)}, u32[]{:S(2)}, u32[]{:S(2)}) async-start(bf16[16,8,1024]{2,1,0:T(8,128)(2,1)} %get-tuple-element.43), calls=%async_computation | async-start | bytes 524288 | tf_op jit(solution)/shard_map/all_to_all | solution.py:483
  19.2 9.8 %collective-permute-start.5 = (bf16[272,512]{1,0:T(8,128)(2,1)S(1)}, bf16[272,512]{1,0:T(8,128)(2,1)S(1)}, u32[]{:S(2)}, u32[]{:S(2)}) collective-permute-start(bf16[272,512]{1,0:T(8,128)(2,1)S(1)} %get-tuple-element.46.refs_7_.refs_1_.refs_2_.refs_6_), channel_id=1, source_target_pairs={{8,24},{10,26},{12,28},{14,30},{24,40},{26,42},{28,44},{30,46},{40... | collective-permute-start | bytes 835592 | tf_op jit(solution)/shard_map/ppermute | solution.py:487
  26.9 40.6 %copy-start = (bf16[16,8,1024]{2,1,0:T(8,128)(2,1)}, bf16[16,8,1024]{2,1,0:T(8,128)(2,1)S(1)}, u32[]{:S(2)}) copy-start(bf16[16,8,1024]{2,1,0:T(8,128)(2,1)S(1)} %all-to-all-done) | copy-start | bytes 786436
  26.9 40.6 %copy-start.5 = (bf16[272,512]{1,0:T(8,128)(2,1)}, bf16[272,512]{1,0:T(8,128)(2,1)S(1)}, u32[]{:S(2)}) copy-start(bf16[272,512]{1,0:T(8,128)(2,1)S(1)} %collective-permute-done.2.refs_2_.refs_3_.refs_5_) | copy-start | bytes 835588
  26.9 40.6 %copy-start.6 = (bf16[272,512]{1,0:T(8,128)(2,1)}, bf16[272,512]{1,0:T(8,128)(2,1)S(1)}, u32[]{:S(2)}) copy-start(bf16[272,512]{1,0:T(8,128)(2,1)S(1)} %collective-permute-done.1.refs_1_.refs_4_.refs_6_) | copy-start | bytes 835588
  26.9 7.6 %collective-permute-start.3 = (bf16[272,512]{1,0:T(8,128)(2,1)S(1)}, bf16[272,512]{1,0:T(8,128)(2,1)S(1)}, u32[]{:S(2)}, u32[]{:S(2)}) collective-permute-start(bf16[272,512]{1,0:T(8,128)(2,1)S(1)} %collective-permute-done.1.refs_1_.refs_4_.refs_6_), channel_id=1, source_target_pairs={{0,14},{2,0},{4,2},{6,4},{8,6},{10,8},{12,10},{14,12},{16,30},{18,... | collective-permute-start | bytes 835592 | tf_op jit(solution)/shard_map/ppermute | solution.py:479
  28.6 8.2 %collective-permute-start.4 = (bf16[272,512]{1,0:T(8,128)(2,1)S(1)}, bf16[272,512]{1,0:T(8,128)(2,1)S(1)}, u32[]{:S(2)}, u32[]{:S(2)}) collective-permute-start(bf16[272,512]{1,0:T(8,128)(2,1)S(1)} %collective-permute-done.2.refs_2_.refs_3_.refs_5_), channel_id=1, source_target_pairs={{0,2},{2,4},{4,6},{6,8},{8,10},{10,12},{12,14},{14,0},{16,18},{18,... | collective-permute-start | bytes 835592 | tf_op jit(solution)/shard_map/ppermute | solution.py:480
  29.0 38.5 %copy-start.2 = (bf16[272,512]{1,0:T(8,128)(2,1)}, bf16[272,512]{1,0:T(8,128)(2,1)S(1)}, u32[]{:S(2)}) copy-start(bf16[272,512]{1,0:T(8,128)(2,1)S(1)} %collective-permute-done.5.refs_8_.refs_2_.refs_3_.refs_7_) | copy-start | bytes 835588
  34.5 32.9 %copy-start.7 = (bf16[272,512]{1,0:T(8,128)(2,1)}, bf16[272,512]{1,0:T(8,128)(2,1)S(1)}, u32[]{:S(2)}) copy-start(bf16[272,512]{1,0:T(8,128)(2,1)S(1)} %collective-permute-done.3.refs_3_.refs_2_.refs_4_) | copy-start | bytes 835588
  36.9 30.6 %copy-start.8 = (bf16[272,512]{1,0:T(8,128)(2,1)}, bf16[272,512]{1,0:T(8,128)(2,1)S(1)}, u32[]{:S(2)}) copy-start(bf16[272,512]{1,0:T(8,128)(2,1)S(1)} %collective-permute-done.4.refs_4_.refs_1_.refs_3_) | copy-start | bytes 835588
  36.9 7.5 %collective-permute-start.6 = (bf16[272,512]{1,0:T(8,128)(2,1)S(1)}, bf16[272,512]{1,0:T(8,128)(2,1)S(1)}, u32[]{:S(2)}, u32[]{:S(2)}) collective-permute-start(bf16[272,512]{1,0:T(8,128)(2,1)S(1)} %collective-permute-done.3.refs_3_.refs_2_.refs_4_), channel_id=1, source_target_pairs={{0,14},{2,0},{4,2},{6,4},{8,6},{10,8},{12,10},{14,12},{16,30},{18,... | collective-permute-start | bytes 835592 | tf_op jit(solution)/shard_map/ppermute | solution.py:479
  37.2 7.8 %collective-permute-start.7 = (bf16[272,512]{1,0:T(8,128)(2,1)S(1)}, bf16[272,512]{1,0:T(8,128)(2,1)S(1)}, u32[]{:S(2)}, u32[]{:S(2)}) collective-permute-start(bf16[272,512]{1,0:T(8,128)(2,1)S(1)} %collective-permute-done.4.refs_4_.refs_1_.refs_3_), channel_id=1, source_target_pairs={{0,2},{2,4},{4,6},{6,8},{8,10},{10,12},{12,14},{14,0},{16,18},{18,... | collective-permute-start | bytes 835592 | tf_op jit(solution)/shard_map/ppermute | solution.py:480
  44.4 23.1 %copy-start.9 = (bf16[272,512]{1,0:T(8,128)(2,1)}, bf16[272,512]{1,0:T(8,128)(2,1)S(1)}, u32[]{:S(2)}) copy-start(bf16[272,512]{1,0:T(8,128)(2,1)S(1)} %collective-permute-done.6.refs_5_.refs_0_.refs_2_) | copy-start | bytes 835588
  44.4 6.5 %collective-permute-start.8 = (bf16[272,512]{1,0:T(8,128)(2,1)S(1)}, bf16[272,512]{1,0:T(8,128)(2,1)S(1)}, u32[]{:S(2)}, u32[]{:S(2)}) collective-permute-start(bf16[272,512]{1,0:T(8,128)(2,1)S(1)} %collective-permute-done.6.refs_5_.refs_0_.refs_2_), channel_id=1, source_target_pairs={{0,14},{2,0},{4,2},{6,4},{8,6},{10,8},{12,10},{14,12},{16,30},{18,... | collective-permute-start | bytes 835592 | tf_op jit(solution)/shard_map/ppermute | solution.py:490
  45.0 22.5 %copy-start.10 = (bf16[272,512]{1,0:T(8,128)(2,1)}, bf16[272,512]{1,0:T(8,128)(2,1)S(1)}, u32[]{:S(2)}) copy-start(bf16[272,512]{1,0:T(8,128)(2,1)S(1)} %collective-permute-done.7.refs_6_.refs_1_) | copy-start | bytes 835588
  50.9 25.9 %copy-start.4 = (bf16[272,512]{1,0:T(8,128)(2,1)}, bf16[272,512]{1,0:T(8,128)(2,1)S(1)}, u32[]{:S(2)}) copy-start(bf16[272,512]{1,0:T(8,128)(2,1)S(1)} %collective-permute-done.8.refs_0_) | copy-start | bytes 835588
  68.8 8.1 %collective-permute-start.9 = (bf16[128,512]{1,0:T(8,128)(2,1)S(1)}, bf16[128,512]{1,0:T(8,128)(2,1)S(1)}, u32[]{:S(2)}, u32[]{:S(2)}) collective-permute-start(bf16[128,512]{1,0:T(8,128)(2,1)S(1)} %get-tuple-element.57), channel_id=1, source_target_pairs={{0,2},{2,4},{4,6},{6,8},{8,10},{10,12},{12,14},{14,0},{16,18},{18,... | collective-permute-start | bytes 393224 | tf_op jit(solution)/shard_map/ppermute | solution.py:547
  69.0 7.8 %collective-permute-start.10 = (bf16[128,512]{1,0:T(8,128)(2,1)S(1)}, bf16[128,512]{1,0:T(8,128)(2,1)S(1)}, u32[]{:S(2)}, u32[]{:S(2)}) collective-permute-start(bf16[128,512]{1,0:T(8,128)(2,1)S(1)} %get-tuple-element.58), channel_id=1, source_target_pairs={{0,14},{2,0},{4,2},{6,4},{8,6},{10,8},{12,10},{14,12},{16,30},{18,... | collective-permute-start | bytes 393224 | tf_op jit(solution)/shard_map/ppermute | solution.py:550
  76.9 5.7 %collective-permute-start.12 = (bf16[128,512]{1,0:T(8,128)(2,1)S(1)}, bf16[128,512]{1,0:T(8,128)(2,1)S(1)}, u32[]{:S(2)}, u32[]{:S(2)}) collective-permute-start(bf16[128,512]{1,0:T(8,128)(2,1)S(1)} %add_convert_fusion.2), channel_id=1, source_target_pairs={{0,14},{2,0},{4,2},{6,4},{8,6},{10,8},{12,10},{14,12},{16,30},{18,... | collective-permute-start | bytes 393224 | tf_op jit(solution)/shard_map/ppermute | solution.py:550
  78.6 6.3 %collective-permute-start.11 = (bf16[128,512]{1,0:T(8,128)(2,1)S(1)}, bf16[128,512]{1,0:T(8,128)(2,1)S(1)}, u32[]{:S(2)}, u32[]{:S(2)}) collective-permute-start(bf16[128,512]{1,0:T(8,128)(2,1)S(1)} %add_convert_fusion.3), channel_id=1, source_target_pairs={{0,2},{2,4},{4,6},{6,8},{8,10},{10,12},{12,14},{14,0},{16,18},{18,... | collective-permute-start | bytes 393224 | tf_op jit(solution)/shard_map/ppermute | solution.py:547
  79.1 16.9 %copy-start.14 = (bf16[128,512]{1,0:T(8,128)(2,1)S(1)}, bf16[128,512]{1,0:T(8,128)(2,1)}, u32[]{:S(2)}) copy-start(bf16[128,512]{1,0:T(8,128)(2,1)} %get-tuple-element.71) | copy-start | bytes 393220
  82.6 19.6 %copy-start.13 = (bf16[128,512]{1,0:T(8,128)(2,1)S(1)}, bf16[128,512]{1,0:T(8,128)(2,1)}, u32[]{:S(2)}) copy-start(bf16[128,512]{1,0:T(8,128)(2,1)} %get-tuple-element.56) | copy-start | bytes 393220
  84.9 11.1 %collective-permute-start.13 = (f32[128,512]{1,0:T(8,128)S(1)}, f32[128,512]{1,0:T(8,128)S(1)}, u32[]{:S(2)}, u32[]{:S(2)}) collective-permute-start(f32[128,512]{1,0:T(8,128)S(1)} %convert_add_fusion.1), channel_id=1, source_target_pairs={{0,2},{2,4},{4,6},{6,8},{8,10},{10,12},{12,14},{14,0},{16,18},{18,... | collective-permute-start | bytes 786440 | tf_op jit(solution)/shard_map/ppermute | solution.py:547
  85.0 11.1 %collective-permute-start.16 = (bf16[256,512]{1,0:T(8,128)(2,1)S(1)}, bf16[256,512]{1,0:T(8,128)(2,1)S(1)}, u32[]{:S(2)}, u32[]{:S(2)}) collective-permute-start(bf16[256,512]{1,0:T(8,128)(2,1)S(1)} %get-tuple-element.75), channel_id=1, source_target_pairs={{24,8},{26,10},{28,12},{30,14},{40,24},{42,26},{44,28},{46,30},{56... | collective-permute-start | bytes 786440 | tf_op jit(solution)/shard_map/ppermute | solution.py:579
  85.7 12.2 %all-to-all-start.2 = ((bf16[16,8,1024]{2,1,0:T(8,128)(2,1)}), bf16[16,8,1024]{2,1,0:T(8,128)(2,1)S(1)}, u32[]{:S(2)}, u32[]{:S(2)}) async-start(bf16[16,8,1024]{2,1,0:T(8,128)(2,1)} %bitcast.2), calls=%async_computation.2 | async-start | bytes 524288 | tf_op jit(solution)/shard_map/all_to_all | solution.py:580
  90.4 10.2 %collective-permute-start.15 = (f32[128,512]{1,0:T(8,128)S(1)}, f32[128,512]{1,0:T(8,128)S(1)}, u32[]{:S(2)}, u32[]{:S(2)}) collective-permute-start(f32[128,512]{1,0:T(8,128)S(1)} %convert_add_fusion), channel_id=1, source_target_pairs={{0,14},{2,0},{4,2},{6,4},{8,6},{10,8},{12,10},{14,12},{16,30},{18,... | collective-permute-start | bytes 786440 | tf_op jit(solution)/shard_map/ppermute | solution.py:550
  96.0 6.3 %collective-permute-start.14 = (bf16[128,512]{1,0:T(8,128)(2,1)S(1)}, bf16[128,512]{1,0:T(8,128)(2,1)S(1)}, u32[]{:S(2)}, u32[]{:S(2)}) collective-permute-start(bf16[128,512]{1,0:T(8,128)(2,1)S(1)} %add_convert_fusion.1), channel_id=1, source_target_pairs={{0,2},{2,4},{4,6},{6,8},{8,10},{10,12},{12,14},{14,0},{16,18},{18,... | collective-permute-start | bytes 393224 | tf_op jit(solution)/shard_map/ppermute | solution.py:547
  96.1 1.7 %copy-start.12 = (bf16[256,512]{1,0:T(8,128)(2,1)}, bf16[256,512]{1,0:T(8,128)(2,1)S(1)}, u32[]{:S(2)}) copy-start(bf16[256,512]{1,0:T(8,128)(2,1)S(1)} %collective-permute-done.16.arrived) | copy-start | bytes 786436
  97.8 0.7 copy-start.11

commit v8 on v6

--- a/solution.py
+++ b/solution.py
@@ -48,7 +48,7 @@
 LEADING = (4, 5)
 TRAILING = (3, 6, 2, 7, 1, 0)
 ORDER = LEADING + TRAILING
-TOGETHER = 2
+TOGETHER = 3
 
 VMEM_LIMIT = 50 * 2**20
 SMEM = pltpu.SMEM
@@ -319,7 +319,7 @@
         for h in range(HEADS_HERE)
     ]
     for first in range(0, count, TOGETHER):
-        group = range(first, first + TOGETHER)
+        group = range(first, min(first + TOGETHER, count))
         for i in group:
             for copy in copies[i]:
                 copy.wait()

time: 104 us -> 104 us (level)
  no operation moved by 1% of the time
where the time goes in v8:
time: 104 us; the launch traced here: 103 us
  starting transfers between devices  36.9 us (35%)
  waiting for transfers between devices  26.9 us (26%)
  Pallas kernels  22.1 us (21%)
  blocking collectives  14.7 us (14%)
    all_to_all x1, blocking collectives, shards(): stats = lax.all_to_all(stats, 'seq', 0, 0, axis_index_groups=Z_GROUPS)  14.7 us
    ppermute x3, starting transfers between devices, backward_step(): return lax.ppermute(array, 'seq', TO_PREVIOUS)  11.8 us
    ppermute x3, waiting for transfers between devices, ring_step(): after.append(lax.ppermute(after[-1], 'seq', TO_PREVIOUS))  11 us
    all_to_all x1, starting transfers between devices, shards(): all_sums = lax.all_to_all(sums, 'seq', 0, 0, axis_index_groups=XY_GROUPS)  7.48 us
    all_to_all x1, waiting for transfers between devices, shards(): all_sums = lax.all_to_all(sums, 'seq', 0, 0, axis_index_groups=XY_GROUPS)  7.01 us
    pallas_call x2, Pallas kernels, stats_of(): pl.pallas_call(lambda *refs: stats_kernel(order, *refs), out_shape=out +...  6.58 us
    ppermute x3, starting transfers between devices, ring_step(): after.append(lax.ppermute(after[-1], 'seq', TO_PREVIOUS))  6.12 us
    all_to_all x1, starting transfers between devices, shards(): lax.all_to_all(sum_grad.reshape(NXY, BARS_HERE, 2 * FEAT), 'seq', 0, 0, a...  5.11 us
  transfers between devices with their start and end apart: 19, of which 8 were waited for; matrix products, arithmetic and copies ran while one was open for 0% of the time, Pallas kernels for 17%

profile of v8, /device:TPU:2, one launch (start us, length us, event | category | flops | bytes accessed | tf_op | source)
XLA Modules:
  0.0 103.1 jit_solution(13692259090501956059)
XLA Ops:
  0.6 0.1 collective-permute-start
  0.7 3.1 %shard_map.103 = (f32[512,128]{1,0:T(8,128)S(1)}, bf16[272,512]{1,0:T(8,128)(2,1)S(1)}, bf16[272,512]{1,0:T(8,128)(2,1)S(1)}, bf16[16,8,1024]{2,1,0:T(8,128)(2,1)}) custom-call(s32[1]{0:T(128)} %bitcast.core, s32[8]{0:T(128)} %starts.3, s32[8,8]{1,0:T(8,128)} %related.1, s32[8]{0:T(128)} %slots.3, bf16[128,512]{1,0:T(8,128)(2,1)} %queries.1, ...), custom_call_target="tpu_custom_call" | custom-call | tf_op jit(solution)/shard_map/pallas_call | solution.py:439
  3.8 0.0 copy-start
  3.8 0.0 collective-permute-done.grad_other
  3.8 1.8 %shard_map.104.refs_0_.refs_5_.refs_7_ = bf16[272,512]{1,0:T(8,128)(2,1)S(1)} custom-call(s32[1]{0:T(128)} %bitcast.core, bf16[272,512]{1,0:T(8,128)(2,1)S(1)} %get-tuple-element.41.pack, f32[512,128]{1,0:T(8,128)S(1)} %get-tuple-element.42.partial, bf16[128,1024]{1,0:T(8,128)(2,1)S(1)} %collective-permute-done.grad_other, bf16[512,2048]{1,0:T(8,128)(2,1)} %out_weight.3), custom_call_target="tpu_custom_call" | custom-call | tf_op jit(solution)/shard_map/pallas_call | solution.py:456
  5.7 0.0 copy-start.2
  5.7 2.0 %collective-permute-start.2 = (bf16[272,512]{1,0:T(8,128)(2,1)S(1)}, bf16[272,512]{1,0:T(8,128)(2,1)S(1)}, u32[]{:S(2)}, u32[]{:S(2)}) collective-permute-start(bf16[272,512]{1,0:T(8,128)(2,1)S(1)} %shard_map.104.refs_0_.refs_5_.refs_7_), channel_id=1, source_target_pairs={{0,2},{2,4},{4,6},{6,8},{8,10},{10,12},{12,14},{14,0},{16,18},{18,... | collective-permute-start | bytes 835592 | tf_op jit(solution)/shard_map/ppermute | solution.py:474
  7.7 4.0 %collective-permute-start.1 = (bf16[272,512]{1,0:T(8,128)(2,1)S(1)}, bf16[272,512]{1,0:T(8,128)(2,1)S(1)}, u32[]{:S(2)}, u32[]{:S(2)}) collective-permute-start(bf16[272,512]{1,0:T(8,128)(2,1)S(1)} %shard_map.104.refs_0_.refs_5_.refs_7_), channel_id=1, source_target_pairs={{0,14},{2,0},{4,2},{6,4},{8,6},{10,8},{12,10},{14,12},{16,30},{18,... | collective-permute-start | bytes 835592 | tf_op jit(solution)/shard_map/ppermute | solution.py:473
  11.7 7.5 %all-to-all-start = ((bf16[16,8,1024]{2,1,0:T(8,128)(2,1)}), bf16[16,8,1024]{2,1,0:T(8,128)(2,1)S(1)}, u32[]{:S(2)}, u32[]{:S(2)}) async-start(bf16[16,8,1024]{2,1,0:T(8,128)(2,1)} %get-tuple-element.43), calls=%async_computation | async-start | bytes 524288 | tf_op jit(solution)/shard_map/all_to_all | solution.py:477
  19.2 0.7 collective-permute-start.5
  19.9 7.0 %all-to-all-done = bf16[16,8,1024]{2,1,0:T(8,128)(2,1)S(1)} async-done(((bf16[16,8,1024]{2,1,0:T(8,128)(2,1)}), bf16[16,8,1024]{2,1,0:T(8,128)(2,1)S(1)}, u32[]{:S(2)}, u32[]{:S(2)}) %all-to-all-start) | async-done | bytes 262176 | tf_op jit(solution)/shard_map/all_to_all | solution.py:477
  26.9 0.0 collective-permute-done.2.refs_2_.refs_3_.refs_5_
  26.9 0.0 collective-permute-done.1.refs_1_.refs_4_.refs_6_
  26.9 0.0 copy-start.6
  26.9 1.7 %collective-permute-start.3 = (bf16[272,512]{1,0:T(8,128)(2,1)S(1)}, bf16[272,512]{1,0:T(8,128)(2,1)S(1)}, u32[]{:S(2)}, u32[]{:S(2)}) collective-permute-start(bf16[272,512]{1,0:T(8,128)(2,1)S(1)} %collective-permute-done.1.refs_1_.refs_4_.refs_6_), channel_id=1, source_target_pairs={{0,14},{2,0},{4,2},{6,4},{8,6},{10,8},{12,10},{14,12},{16,30},{18,... | collective-permute-start | bytes 835592 | tf_op jit(solution)/shard_map/ppermute | solution.py:473
  28.6 0.4 collective-permute-start.4
  29.0 0.0 collective-permute-done.5.refs_8_.refs_2_.refs_3_.refs_7_
  29.0 5.5 %collective-permute-done.3.refs_3_.refs_2_.refs_4_ = bf16[272,512]{1,0:T(8,128)(2,1)S(1)} collective-permute-done((bf16[272,512]{1,0:T(8,128)(2,1)S(1)}, bf16[272,512]{1,0:T(8,128)(2,1)S(1)}, u32[]{:S(2)}, u32[]{:S(2)}) %collective-permute-start.3) | collective-permute-done | bytes 278560 | tf_op jit(solution)/shard_map/ppermute | solution.py:473
  34.5 2.3 %collective-permute-done.4.refs_4_.refs_1_.refs_3_ = bf16[272,512]{1,0:T(8,128)(2,1)S(1)} collective-permute-done((bf16[272,512]{1,0:T(8,128)(2,1)S(1)}, bf16[272,512]{1,0:T(8,128)(2,1)S(1)}, u32[]{:S(2)}, u32[]{:S(2)}) %collective-permute-start.4) | collective-permute-done | bytes 278560 | tf_op jit(solution)/shard_map/ppermute | solution.py:474
  36.9 0.4 collective-permute-start.6
  37.2 1.7 %collective-permute-start.7 = (bf16[272,512]{1,0:T(8,128)(2,1)S(1)}, bf16[272,512]{1,0:T(8,128)(2,1)S(1)}, u32[]{:S(2)}, u32[]{:S(2)}) collective-permute-start(bf16[272,512]{1,0:T(8,128)(2,1)S(1)} %collective-permute-done.4.refs_4_.refs_1_.refs_3_), channel_id=1, source_target_pairs={{0,2},{2,4},{4,6},{6,8},{8,10},{10,12},{12,14},{14,0},{16,18},{18,... | collective-permute-start | bytes 835592 | tf_op jit(solution)/shard_map/ppermute | solution.py:474
  38.9 5.5 %collective-permute-done.6.refs_5_.refs_0_.refs_2_ = bf16[272,512]{1,0:T(8,128)(2,1)S(1)} collective-permute-done((bf16[272,512]{1,0:T(8,128)(2,1)S(1)}, bf16[272,512]{1,0:T(8,128)(2,1)S(1)}, u32[]{:S(2)}, u32[]{:S(2)}) %collective-permute-start.6) | collective-permute-done | bytes 278560 | tf_op jit(solution)/shard_map/ppermute | solution.py:473
  44.4 0.6 collective-permute-start.8
  45.0 0.0 collective-permute-done.7.refs_6_.refs_1_
  45.0 5.3 %shard_map.105 = (f32[8,8,128]{2,1,0:T(8,128)S(1)}, f32[11,128,128]{2,1,0:T(8,128)S(1)}) custom-call(bf16[272,512]{1,0:T(8,128)(2,1)S(1)} %shard_map.104.refs_0_.refs_5_.refs_7_, bf16[272,512]{1,0:T(8,128)(2,1)S(1)} %collective-permute-done.1.refs_1_.refs_4_.refs_6_, bf16[272,512]{1,0:T(8,128)(2,1)S(1)} %collective-permute-done.2.refs_2_.refs_3_.refs_5_, ...), custom_call_target="tpu_custom_call" | custom-call | tf_op jit(solution)/shard_map/pallas_call | solution.py:499
  50.4 0.0 copy-start.3
  50.4 0.5 collective-permute-done.8.refs_0_
  50.9 1.2 %shard_map.106 = (f32[8,8,8,128]{3,2,1,0:T(8,128)S(1)}, f32[2,128,128]{2,1,0:T(8,128)S(1)}) custom-call(bf16[272,512]{1,0:T(8,128)(2,1)S(1)} %collective-permute-done.8.refs_0_, bf16[272,512]{1,0:T(8,128)(2,1)S(1)} %get-tuple-element.46.refs_7_.refs_1_.refs_2_.refs_6_, bf16[272,512]{1,0:T(8,128)(2,1)S(1)} %collective-permute-done.5.refs_8_.refs_2_.refs_3_.refs_7_, ...), custom_call_target="tpu_custom_call" | custom-call | tf_op jit(solution)/shard_map/pallas_call | solution.py:499
  52.2 0.0 copy-done.2
  52.2 14.7 %all_to_all.15.refs_7_ = f32[8,8,8,128]{3,2,1,0:T(8,128)S(1)} all-to-all(f32[8,8,8,128]{3,2,1,0:T(8,128)S(1)} %get-tuple-element.54), channel_id=1, replica_groups={{0,2,4,6,8,10,12,14},{16,18,20,22,24,26,28,30},{32,34,36,38,40,42,44,46..., dimensions={0} | all-to-all | bytes 524288 | tf_op jit(solution)/shard_map/all_to_all | solution.py:511
  66.9 0.0 copy-done.5
  66.9 0.0 copy-done.6
  66.9 0.0 copy-done.7
  66.9 0.0 copy-done.8
  66.9 0.0 copy-done
  66.9 0.0 copy-done.1
  66.9 0.0 copy-done.10
  66.9 1.6 %shard_map.107 = (bf16[128,512]{1,0:T(8,128)(2,1)S(1)}, bf16[128,512]{1,0:T(8,128)(2,1)S(1)}, bf16[2,2,4,128,128]{4,3,2,1,0:T(8,128)(2,1)S(1)}, bf16[1,2,4,128,128]{4,3,2,1,0:T(8,128)(2,1)S(1)}, f32[8,8,128]{2,1,0:T(8,128)S(1)}) custom-call(bf16[272,512]{1,0:T(8,128)(2,1)S(1)} %collective-permute-done.8.refs_0_, ...), custom_call_target="tpu_custom_call" | custom-call | tf_op jit(solution)/shard_map/pallas_call | solution.py:518
  68.5 0.1 collective-permute-start.9
  68.6 3.2 %collective-permute-start.10 = (bf16[128,512]{1,0:T(8,128)(2,1)S(1)}, bf16[128,512]{1,0:T(8,128)(2,1)S(1)}, u32[]{:S(2)}, u32[]{:S(2)}) collective-permute-start(bf16[128,512]{1,0:T(8,128)(2,1)S(1)} %get-tuple-element.58), channel_id=1, source_target_pairs={{0,14},{2,0},{4,2},{6,4},{8,6},{10,8},{12,10},{14,12},{16,30},{18,... | collective-permute-start | bytes 393224 | tf_op jit(solution)/shard_map/ppermute | solution.py:543
  71.9 0.0 copy-done.9
  71.9 0.0 copy-done.3
  71.9 3.4 %shard_map.108 = (bf16[128,512]{1,0:T(8,128)(2,1)S(1)}, bf16[128,512]{1,0:T(8,128)(2,1)S(1)}, bf16[128,512]{1,0:T(8,128)(2,1)S(1)}, bf16[128,512]{1,0:T(8,128)(2...) custom-call(bf16[272,512]{1,0:T(8,128)(2,1)S(1)} %collective-permute, ...), custom_call_target="tpu_custom_call" | custom-call | tf_op jit(solution)/shard_map/pallas_call | solution.py:518
  75.3 0.0 copy-done.4
  75.3 0.0 collective-permute-done.9
  75.3 0.0 collective-permute-done.10
  75.3 3.1 %collective-permute-start.12 = (bf16[128,512]{1,0:T(8,128)(2,1)S(1)}, bf16[128,512]{1,0:T(8,128)(2,1)S(1)}, u32[]{:S(2)}, u32[]{:S(2)}) collective-permute-start(bf16[128,512]{1,0:T(8,128)(2,1)S(1)} %add_convert_fusion.2), channel_id=1, source_target_pairs={{0,14},{2,0},{4,2},{6,4},{8,6},{10,8},{12,10},{14,12},{16,30},{18,... | collective-permute-start | bytes 393224 | tf_op jit(solution)/shard_map/ppermute | solution.py:543
  78.4 0.1 collective-permute-start.11
  78.5 3.5 %shard_map.109 = (bf16[256,512]{1,0:T(8,128)(2,1)S(1)}, f32[256,512]{1,0:T(8,128)}, bf16[128,1024]{1,0:T(8,128)(2,1)}) custom-call(bf16[272,512]{1,0:T(8,128)(2,1)} %copy-done.4, bf16[272,512]{1,0:T(8,128)(2,1)} %copy-done.10, bf16[272,512]{1,0:T(8,128)(2,1)} %copy-done.9, bf16[272,512]{1,0:T(8,128)(2,1)} %copy-done.8, bf16[272,512]{1,0:T(8,128)(2,1)} %copy-done.7, ...), custom_call_target="tpu_custom_call" | custom-call | tf_op jit(solution)/shard_map/pallas_call | solution.py:551
  82.0 0.0 collective-permute-done.12
  82.0 2.7 %collective-permute-done.11 = bf16[128,512]{1,0:T(8,128)(2,1)S(1)} collective-permute-done((bf16[128,512]{1,0:T(8,128)(2,1)S(1)}, bf16[128,512]{1,0:T(8,128)(2,1)S(1)}, u32[]{:S(2)}, u32[]{:S(2)}) %collective-permute-start.11) | collective-permute-done | bytes 131104 | tf_op jit(solution)/shard_map/ppermute | solution.py:540
  84.7 0.1 collective-permute-start.13
  84.8 0.7 collective-permute-start.16
  85.5 5.1 %all-to-all-start.2 = ((bf16[16,8,1024]{2,1,0:T(8,128)(2,1)}), bf16[16,8,1024]{2,1,0:T(8,128)(2,1)S(1)}, u32[]{:S(2)}, u32[]{:S(2)}) async-start(bf16[16,8,1024]{2,1,0:T(8,128)(2,1)} %bitcast.2), calls=%async_computation.2 | async-start | bytes 524288 | tf_op jit(solution)/shard_map/all_to_all | solution.py:573
  90.6 5.5 %collective-permute-start.15 = (f32[128,512]{1,0:T(8,128)S(1)}, f32[128,512]{1,0:T(8,128)S(1)}, u32[]{:S(2)}, u32[]{:S(2)}) collective-permute-start(f32[128,512]{1,0:T(8,128)S(1)} %convert_add_fusion), channel_id=1, source_target_pairs={{0,14},{2,0},{4,2},{6,4},{8,6},{10,8},{12,10},{14,12},{16,30},{18,... | collective-permute-start | bytes 786440 | tf_op jit(solution)/shard_map/ppermute | solution.py:543
  96.1 0.0 collective-permute-done.13
  96.2 0.1 collective-permute-start.14
  96.3 0.0 collective-permute-done.16.arrived
  96.3 1.8 %all-to-all-done.2.parts = bf16[16,8,1024]{2,1,0:T(8,128)(2,1)S(1)} async-done(((bf16[16,8,1024]{2,1,0:T(8,128)(2,1)}), bf16[16,8,1024]{2,1,0:T(8,128)(2,1)S(1)}, u32[]{:S(2)}, u32[]{:S(2)}) %all-to-all-start.2) | async-done | bytes 262176 | tf_op jit(solution)/shard_map/all_to_all | solution.py:573
  98.0 0.7 copy-done.11
  98.7 2.2 %shard_map.110 = (bf16[128,512]{1,0:T(8,128)(2,1)}, bf16[128,512]{1,0:T(8,128)(2,1)}) custom-call(s32[8]{0:T(128)} %starts.3, s32[8]{0:T(128)} %slots.3, f32[256,512]{1,0:T(8,128)} %get-tuple-element.74.own_grad, bf16[256,512]{1,0:T(8,128)(2,1)} %copy-done.12, bf16[16,8,1024]{2,1,0:T(8,128)(2,1)} %copy-done.11), custom_call_target="tpu_custom_call" | custom-call | tf_op jit(solution)/shard_map/pallas_call | solution.py:578
  100.9 0.0 collective-permute-done.15
  100.9 1.5 %collective-permute-done.14 = bf16[128,512]{1,0:T(8,128)(2,1)S(1)} collective-permute-done((bf16[128,512]{1,0:T(8,128)(2,1)S(1)}, bf16[128,512]{1,0:T(8,128)(2,1)S(1)}, u32[]{:S(2)}, u32[]{:S(2)}) %collective-permute-start.14) | collective-permute-done | bytes 131104 | tf_op jit(solution)/shard_map/ppermute | solution.py:540
  102.4 0.7 add_convert_fusion
  (15 shorter events, 0.2 us)
Async XLA Ops:
  0.6 3.2 %collective-permute-start = (bf16[128,1024]{1,0:T(8,128)(2,1)}, bf16[128,1024]{1,0:T(8,128)(2,1)S(1)}, u32[]{:S(2)}, u32[]{:S(2)}) collective-permute-start(bf16[128,1024]{1,0:T(8,128)(2,1)} %grad_own.1), channel_id=1, source_target_pairs={{0,1},{1,0},{2,3},{3,2},{4,5},{5,4},{6,7},{7,6},{8,9},{9,8},{10,11... | collective-permute-start | bytes 786440 | tf_op jit(solution)/shard_map/ppermute | solution.py:436
  3.8 63.1 %copy-start = (bf16[272,512]{1,0:T(8,128)(2,1)}, bf16[272,512]{1,0:T(8,128)(2,1)S(1)}, u32[]{:S(2)}) copy-start(bf16[272,512]{1,0:T(8,128)(2,1)S(1)} %get-tuple-element.46.refs_7_.refs_1_.refs_2_.refs_6_) | copy-start | bytes 835588
  5.7 46.5 %copy-start.2 = (bf16[272,512]{1,0:T(8,128)(2,1)}, bf16[272,512]{1,0:T(8,128)(2,1)S(1)}, u32[]{:S(2)}) copy-start(bf16[272,512]{1,0:T(8,128)(2,1)S(1)} %shard_map.104.refs_0_.refs_5_.refs_7_) | copy-start | bytes 835588
  5.7 21.2 %collective-permute-start.2 = (bf16[272,512]{1,0:T(8,128)(2,1)S(1)}, bf16[272,512]{1,0:T(8,128)(2,1)S(1)}, u32[]{:S(2)}, u32[]{:S(2)}) collective-permute-start(bf16[272,512]{1,0:T(8,128)(2,1)S(1)} %shard_map.104.refs_0_.refs_5_.refs_7_), channel_id=1, source_target_pairs={{0,2},{2,4},{4,6},{6,8},{8,10},{10,12},{12,14},{14,0},{16,18},{18,... | collective-permute-start | bytes 835592 | tf_op jit(solution)/shard_map/ppermute | solution.py:474
  7.7 19.2 %collective-permute-start.1 = (bf16[272,512]{1,0:T(8,128)(2,1)S(1)}, bf16[272,512]{1,0:T(8,128)(2,1)S(1)}, u32[]{:S(2)}, u32[]{:S(2)}) collective-permute-start(bf16[272,512]{1,0:T(8,128)(2,1)S(1)} %shard_map.104.refs_0_.refs_5_.refs_7_), channel_id=1, source_target_pairs={{0,14},{2,0},{4,2},{6,4},{8,6},{10,8},{12,10},{14,12},{16,30},{18,... | collective-permute-start | bytes 835592 | tf_op jit(solution)/shard_map/ppermute | solution.py:473
  11.7 15.2 %all-to-all-start = ((bf16[16,8,1024]{2,1,0:T(8,128)(2,1)}), bf16[16,8,1024]{2,1,0:T(8,128)(2,1)S(1)}, u32[]{:S(2)}, u32[]{:S(2)}) async-start(bf16[16,8,1024]{2,1,0:T(8,128)(2,1)} %get-tuple-element.43), calls=%async_computation | async-start | bytes 524288 | tf_op jit(solution)/shard_map/all_to_all | solution.py:477
  19.2 9.8 %collective-permute-start.5 = (bf16[272,512]{1,0:T(8,128)(2,1)S(1)}, bf16[272,512]{1,0:T(8,128)(2,1)S(1)}, u32[]{:S(2)}, u32[]{:S(2)}) collective-permute-start(bf16[272,512]{1,0:T(8,128)(2,1)S(1)} %get-tuple-element.46.refs_7_.refs_1_.refs_2_.refs_6_), channel_id=1, source_target_pairs={{8,24},{10,26},{12,28},{14,30},{24,40},{26,42},{28,44},{30,46},{40... | collective-permute-start | bytes 835592 | tf_op jit(solution)/shard_map/ppermute | solution.py:481
  26.9 40.0 %copy-start.5 = (bf16[272,512]{1,0:T(8,128)(2,1)}, bf16[272,512]{1,0:T(8,128)(2,1)S(1)}, u32[]{:S(2)}) copy-start(bf16[272,512]{1,0:T(8,128)(2,1)S(1)} %collective-permute-done.2.refs_2_.refs_3_.refs_5_) | copy-start | bytes 835588
  26.9 40.0 %copy-start.6 = (bf16[272,512]{1,0:T(8,128)(2,1)}, bf16[272,512]{1,0:T(8,128)(2,1)S(1)}, u32[]{:S(2)}) copy-start(bf16[272,512]{1,0:T(8,128)(2,1)S(1)} %collective-permute-done.1.refs_1_.refs_4_.refs_6_) | copy-start | bytes 835588
  26.9 7.6 %collective-permute-start.3 = (bf16[272,512]{1,0:T(8,128)(2,1)S(1)}, bf16[272,512]{1,0:T(8,128)(2,1)S(1)}, u32[]{:S(2)}, u32[]{:S(2)}) collective-permute-start(bf16[272,512]{1,0:T(8,128)(2,1)S(1)} %collective-permute-done.1.refs_1_.refs_4_.refs_6_), channel_id=1, source_target_pairs={{0,14},{2,0},{4,2},{6,4},{8,6},{10,8},{12,10},{14,12},{16,30},{18,... | collective-permute-start | bytes 835592 | tf_op jit(solution)/shard_map/ppermute | solution.py:473
  28.6 8.2 %collective-permute-start.4 = (bf16[272,512]{1,0:T(8,128)(2,1)S(1)}, bf16[272,512]{1,0:T(8,128)(2,1)S(1)}, u32[]{:S(2)}, u32[]{:S(2)}) collective-permute-start(bf16[272,512]{1,0:T(8,128)(2,1)S(1)} %collective-permute-done.2.refs_2_.refs_3_.refs_5_), channel_id=1, source_target_pairs={{0,2},{2,4},{4,6},{6,8},{8,10},{10,12},{12,14},{14,0},{16,18},{18,... | collective-permute-start | bytes 835592 | tf_op jit(solution)/shard_map/ppermute | solution.py:474
  29.0 37.9 %copy-start.1 = (bf16[272,512]{1,0:T(8,128)(2,1)}, bf16[272,512]{1,0:T(8,128)(2,1)S(1)}, u32[]{:S(2)}) copy-start(bf16[272,512]{1,0:T(8,128)(2,1)S(1)} %collective-permute-done.5.refs_8_.refs_2_.refs_3_.refs_7_) | copy-start | bytes 835588
  34.5 32.3 %copy-start.7 = (bf16[272,512]{1,0:T(8,128)(2,1)}, bf16[272,512]{1,0:T(8,128)(2,1)S(1)}, u32[]{:S(2)}) copy-start(bf16[272,512]{1,0:T(8,128)(2,1)S(1)} %collective-permute-done.3.refs_3_.refs_2_.refs_4_) | copy-start | bytes 835588
  36.9 30.0 %copy-start.8 = (bf16[272,512]{1,0:T(8,128)(2,1)}, bf16[272,512]{1,0:T(8,128)(2,1)S(1)}, u32[]{:S(2)}) copy-start(bf16[272,512]{1,0:T(8,128)(2,1)S(1)} %collective-permute-done.4.refs_4_.refs_1_.refs_3_) | copy-start | bytes 835588
  36.9 7.5 %collective-permute-start.6 = (bf16[272,512]{1,0:T(8,128)(2,1)S(1)}, bf16[272,512]{1,0:T(8,128)(2,1)S(1)}, u32[]{:S(2)}, u32[]{:S(2)}) collective-permute-start(bf16[272,512]{1,0:T(8,128)(2,1)S(1)} %collective-permute-done.3.refs_3_.refs_2_.refs_4_), channel_id=1, source_target_pairs={{0,14},{2,0},{4,2},{6,4},{8,6},{10,8},{12,10},{14,12},{16,30},{18,... | collective-permute-start | bytes 835592 | tf_op jit(solution)/shard_map/ppermute | solution.py:473
  37.2 7.8 %collective-permute-start.7 = (bf16[272,512]{1,0:T(8,128)(2,1)S(1)}, bf16[272,512]{1,0:T(8,128)(2,1)S(1)}, u32[]{:S(2)}, u32[]{:S(2)}) collective-permute-start(bf16[272,512]{1,0:T(8,128)(2,1)S(1)} %collective-permute-done.4.refs_4_.refs_1_.refs_3_), channel_id=1, source_target_pairs={{0,2},{2,4},{4,6},{6,8},{8,10},{10,12},{12,14},{14,0},{16,18},{18,... | collective-permute-start | bytes 835592 | tf_op jit(solution)/shard_map/ppermute | solution.py:474
  44.4 27.5 %copy-start.9 = (bf16[272,512]{1,0:T(8,128)(2,1)}, bf16[272,512]{1,0:T(8,128)(2,1)S(1)}, u32[]{:S(2)}) copy-start(bf16[272,512]{1,0:T(8,128)(2,1)S(1)} %collective-permute-done.6.refs_5_.refs_0_.refs_2_) | copy-start | bytes 835588
  44.4 6.5 %collective-permute-start.8 = (bf16[272,512]{1,0:T(8,128)(2,1)S(1)}, bf16[272,512]{1,0:T(8,128)(2,1)S(1)}, u32[]{:S(2)}, u32[]{:S(2)}) collective-permute-start(bf16[272,512]{1,0:T(8,128)(2,1)S(1)} %collective-permute-done.6.refs_5_.refs_0_.refs_2_), channel_id=1, source_target_pairs={{0,14},{2,0},{4,2},{6,4},{8,6},{10,8},{12,10},{14,12},{16,30},{18,... | collective-permute-start | bytes 835592 | tf_op jit(solution)/shard_map/ppermute | solution.py:484
  45.0 21.9 %copy-start.10 = (bf16[272,512]{1,0:T(8,128)(2,1)}, bf16[272,512]{1,0:T(8,128)(2,1)S(1)}, u32[]{:S(2)}) copy-start(bf16[272,512]{1,0:T(8,128)(2,1)S(1)} %collective-permute-done.7.refs_6_.refs_1_) | copy-start | bytes 835588
  50.4 21.5 %copy-start.3 = (f32[11,128,128]{2,1,0:T(8,128)}, f32[11,128,128]{2,1,0:T(8,128)S(1)}, u32[]{:S(2)}) copy-start(f32[11,128,128]{2,1,0:T(8,128)S(1)} %get-tuple-element.51.refs_5_.refs_9_) | copy-start | bytes 2162692
  50.9 24.3 %copy-start.4 = (bf16[272,512]{1,0:T(8,128)(2,1)}, bf16[272,512]{1,0:T(8,128)(2,1)S(1)}, u32[]{:S(2)}) copy-start(bf16[272,512]{1,0:T(8,128)(2,1)S(1)} %collective-permute-done.8.refs_0_) | copy-start | bytes 835588
  68.5 6.7 %collective-permute-start.9 = (bf16[128,512]{1,0:T(8,128)(2,1)S(1)}, bf16[128,512]{1,0:T(8,128)(2,1)S(1)}, u32[]{:S(2)}, u32[]{:S(2)}) collective-permute-start(bf16[128,512]{1,0:T(8,128)(2,1)S(1)} %get-tuple-element.57), channel_id=1, source_target_pairs={{0,2},{2,4},{4,6},{6,8},{8,10},{10,12},{12,14},{14,0},{16,18},{18,... | collective-permute-start | bytes 393224 | tf_op jit(solution)/shard_map/ppermute | solution.py:540
  68.6 6.6 %collective-permute-start.10 = (bf16[128,512]{1,0:T(8,128)(2,1)S(1)}, bf16[128,512]{1,0:T(8,128)(2,1)S(1)}, u32[]{:S(2)}, u32[]{:S(2)}) collective-permute-start(bf16[128,512]{1,0:T(8,128)(2,1)S(1)} %get-tuple-element.58), channel_id=1, source_target_pairs={{0,14},{2,0},{4,2},{6,4},{8,6},{10,8},{12,10},{14,12},{16,30},{18,... | collective-permute-start | bytes 393224 | tf_op jit(solution)/shard_map/ppermute | solution.py:543
  75.3 6.7 %collective-permute-start.12 = (bf16[128,512]{1,0:T(8,128)(2,1)S(1)}, bf16[128,512]{1,0:T(8,128)(2,1)S(1)}, u32[]{:S(2)}, u32[]{:S(2)}) collective-permute-start(bf16[128,512]{1,0:T(8,128)(2,1)S(1)} %add_convert_fusion.2), channel_id=1, source_target_pairs={{0,14},{2,0},{4,2},{6,4},{8,6},{10,8},{12,10},{14,12},{16,30},{18,... | collective-permute-start | bytes 393224 | tf_op jit(solution)/shard_map/ppermute | solution.py:543
  78.4 6.3 %collective-permute-start.11 = (bf16[128,512]{1,0:T(8,128)(2,1)S(1)}, bf16[128,512]{1,0:T(8,128)(2,1)S(1)}, u32[]{:S(2)}, u32[]{:S(2)}) collective-permute-start(bf16[128,512]{1,0:T(8,128)(2,1)S(1)} %add_convert_fusion.3), channel_id=1, source_target_pairs={{0,2},{2,4},{4,6},{6,8},{8,10},{10,12},{12,14},{14,0},{16,18},{18,... | collective-permute-start | bytes 393224 | tf_op jit(solution)/shard_map/ppermute | solution.py:540
  84.7 11.4 %collective-permute-start.13 = (f32[128,512]{1,0:T(8,128)S(1)}, f32[128,512]{1,0:T(8,128)S(1)}, u32[]{:S(2)}, u32[]{:S(2)}) collective-permute-start(f32[128,512]{1,0:T(8,128)S(1)} %convert_add_fusion.1), channel_id=1, source_target_pairs={{0,2},{2,4},{4,6},{6,8},{8,10},{10,12},{12,14},{14,0},{16,18},{18,... | collective-permute-start | bytes 786440 | tf_op jit(solution)/shard_map/ppermute | solution.py:540
  84.8 11.4 %collective-permute-start.16 = (bf16[256,512]{1,0:T(8,128)(2,1)S(1)}, bf16[256,512]{1,0:T(8,128)(2,1)S(1)}, u32[]{:S(2)}, u32[]{:S(2)}) collective-permute-start(bf16[256,512]{1,0:T(8,128)(2,1)S(1)} %get-tuple-element.75), channel_id=1, source_target_pairs={{24,8},{26,10},{28,12},{30,14},{40,24},{42,26},{44,28},{46,30},{56... | collective-permute-start | bytes 786440 | tf_op jit(solution)/shard_map/ppermute | solution.py:572
  85.5 12.5 %all-to-all-start.2 = ((bf16[16,8,1024]{2,1,0:T(8,128)(2,1)}), bf16[16,8,1024]{2,1,0:T(8,128)(2,1)S(1)}, u32[]{:S(2)}, u32[]{:S(2)}) async-start(bf16[16,8,1024]{2,1,0:T(8,128)(2,1)} %bitcast.2), calls=%async_computation.2 | async-start | bytes 524288 | tf_op jit(solution)/shard_map/all_to_all | solution.py:573
  90.6 10.2 %collective-permute-start.15 = (f32[128,512]{1,0:T(8,128)S(1)}, f32[128,512]{1,0:T(8,128)S(1)}, u32[]{:S(2)}, u32[]{:S(2)}) collective-permute-start(f32[128,512]{1,0:T(8,128)S(1)} %convert_add_fusion), channel_id=1, source_target_pairs={{0,14},{2,0},{4,2},{6,4},{8,6},{10,8},{12,10},{14,12},{16,30},{18,... | collective-permute-start | bytes 786440 | tf_op jit(solution)/shard_map/ppermute | solution.py:543
  96.2 6.3 %collective-permute-start.14 = (bf16[128,512]{1,0:T(8,128)(2,1)S(1)}, bf16[128,512]{1,0:T(8,128)(2,1)S(1)}, u32[]{:S(2)}, u32[]{:S(2)}) collective-permute-start(bf16[128,512]{1,0:T(8,128)(2,1)S(1)} %add_convert_fusion.1), channel_id=1, source_target_pairs={{0,2},{2,4},{4,6},{6,8},{8,10},{10,12},{12,14},{14,0},{16,18},{18,... | collective-permute-start | bytes 393224 | tf_op jit(solution)/shard_map/ppermute | solution.py:540
  96.3 1.8 %copy-start.12 = (bf16[256,512]{1,0:T(8,128)(2,1)}, bf16[256,512]{1,0:T(8,128)(2,1)S(1)}, u32[]{:S(2)}) copy-start(bf16[256,512]{1,0:T(8,128)(2,1)S(1)} %collective-permute-done.16.arrived) | copy-start | bytes 786436
  98.0 0.7 copy-start.11
